TPU v7x, 32 devices: a whole 2x2x4 slice. The times are simulated.
32 devices in a mesh: bucket: 8 (over y, x, core), seq: 4 (over z).
Axes of the slice: x: 2, y: 2, z: 4, core: 2. Of those that a mesh axis runs over, the one named last changes fastest.
Arguments:
- tokens: bfloat16 [16384, 1152], P(('bucket', 'seq')), may hold values from -6 to 6
- segment: int32 [16384], P(('bucket', 'seq')), may hold values from 0 to 7, as said below
- keep_route: int32 [16384], P(('bucket', 'seq')), may hold values 0 or 1
- condition: bfloat16 [64, 1152], P('bucket'), may hold values from -6 to 6
- group_bucket: int32 [8], P('bucket'), may hold values from 0 to 9
- head_mask: int32 [10, 16], replicated, may hold values 0 or 1
- channel_mask: int32 [10, 36], replicated, may hold values 0 or 1
- ada_weight: bfloat16 [1152, 6912], replicated, may hold values from -0.1875 to 0.1875
- ada_bias: float32 [6912], replicated, may hold values from -1.2 to 1.2
- qkv_weight: bfloat16 [1152, 3456], replicated, may hold values from -0.1875 to 0.1875
- query_bias: float32 [1152], replicated, may hold values from -1.8 to 1.8
- value_bias: float32 [1152], replicated, may hold values from -1.8 to 1.8
- proj_weight: bfloat16 [1152, 1152], replicated, may hold values from -1.5 to 1.5
- proj_bias: float32 [1152], replicated, may hold values from -1.8 to 1.8
- inner_weight: bfloat16 [1152, 4608], replicated, may hold values from -0.1875 to 0.1875
- inner_bias: float32 [4608], replicated, may hold values from -1.8 to 1.8
- outer_weight: bfloat16 [4608, 1152], replicated, may hold values from -0.1875 to 0.1875
- outer_bias: float32 [1152], replicated, may hold values from -1.8 to 1.8
- cotangent: bfloat16 [16384, 1152], P(('bucket', 'seq')), may hold values from -6 to 6
Outputs:
- block_out: bfloat16 [16384, 1152], P(('bucket', 'seq'))
- grad_tokens: float32 [16384, 1152], P(('bucket', 'seq'))
- grad_ada_weight: float32 [1152, 6912], P(('bucket', 'seq'))
- grad_ada_bias: float32 [6912], P(('bucket', 'seq'))
- grad_qkv_weight: float32 [1152, 3456], P(('bucket', 'seq'))
- grad_query_bias: float32 [1152], P(('bucket', 'seq'))
- grad_value_bias: float32 [1152], P(('bucket', 'seq'))
- grad_proj_weight: float32 [1152, 1152], P(('bucket', 'seq'))
- grad_proj_bias: float32 [1152], P(('bucket', 'seq'))
- grad_inner_weight: float32 [1152, 4608], P(('bucket', 'seq'))
- grad_inner_bias: float32 [4608], P(('bucket', 'seq'))
- grad_outer_weight: float32 [4608, 1152], P(('bucket', 'seq'))
- grad_outer_bias: float32 [1152], P(('bucket', 'seq'))
Inputs may be any that keep to these rules, and one draw needn't show every extreme that they name: `segment`: A device's rows hold, in order, an equal share of each item of its group, items of 256 or 1024 tokens; every index of seq in a group holds the same ids; ids never fall along a device's rows, id 0 starts them and id 7 (8 - 1) ends them.
All inputs are finite; a program needn't handle non-finite values. No bound on the sum of `keep_route` on one device may be relied on, other than what follows from the above.
Results may differ from a plain program's by a relative error of at most 0.019.
The roundings to bfloat16 on the way count: a program that leaves them out, or rounds other values in their place, can miss the bound.
Values may be sent and summed in bfloat16 or wider, within the bound.
No kernel may reach another device: no remote copies, remote signals or barrier semaphores. Data moves between devices by JAX's collectives and lax.ppermute only.
A program may use at most 384 MiB of HBM per device.

v0:
```python
import jax
import jax.numpy as jnp
from jax import lax
from jax.sharding import PartitionSpec as P

EPSILON = 1e-06
NEGATIVE = -1000000000.0


def norm_modulate(value, shift, scale):
    center = value - jnp.mean(value, -1, keepdims=True)
    spread = jnp.mean(center * center, -1, keepdims=True)
    return center * lax.rsqrt(spread + EPSILON) * (1.0 + scale) + shift


def contract(left, right, left_dim, right_dim):
    return lax.dot_general(
        left, right, (((left_dim,), (right_dim,)), ((), ())), preferred_element_type=jnp.float32
    )


def contract_exact(left, right, left_dim, right_dim):
    return lax.dot_general(
        left, right, (((left_dim,), (right_dim,)), ((), ())), precision=lax.Precision.HIGHEST
    )


def rows_view(grad, groups, members):
    return grad.reshape((groups, members, grad.shape[0] // (groups * members)) + grad.shape[1:])


def rows_back(share):
    return share.reshape(share.shape[2:])


def on_device(
    tokens,
    segment,
    keep_route,
    condition,
    group_bucket,
    head_mask,
    channel_mask,
    ada_weight,
    ada_bias,
    qkv_weight,
    query_bias,
    value_bias,
    proj_weight,
    proj_bias,
    inner_weight,
    inner_bias,
    outer_weight,
    outer_bias,
    cotangent,
):
    row_count, model_width = tokens.shape
    head_count = head_mask.shape[1]
    head_width = model_width // head_count
    slot_count = condition.shape[0]
    hidden_units = inner_weight.shape[1]
    scale_factor = head_width ** (-0.5)
    seq_count = lax.axis_size("seq")
    group_count = lax.axis_size("bucket")
    bucket_pick = (jnp.arange(head_mask.shape[0]) == group_bucket[0]).astype(jnp.float32)
    head_keep = jnp.sum(bucket_pick[:, None] * head_mask.astype(jnp.float32), 0)
    head_cols = jnp.repeat(head_keep, head_width)
    group_keep = jnp.sum(bucket_pick[:, None] * channel_mask.astype(jnp.float32), 0)
    channel_keep = jnp.repeat(group_keep, hidden_units // channel_mask.shape[1])
    cond_act = jax.nn.silu(condition.astype(jnp.float32)).astype(jnp.bfloat16)
    modulation = jnp.dot(cond_act, ada_weight, preferred_element_type=jnp.float32) + ada_bias
    onehot = (segment[:, None] == jnp.arange(slot_count)[None, :]).astype(jnp.float32)
    token_mod = jnp.dot(onehot, modulation, precision=lax.Precision.HIGHEST)
    shift_one, scale_one, gate_one, shift_two, scale_two, gate_two = jnp.split(token_mod, 6, axis=1)
    inputs = tokens.astype(jnp.float32)
    normed_full, pull_one = jax.vjp(norm_modulate, inputs, shift_one, scale_one)
    normed_one = normed_full.astype(jnp.bfloat16)
    projected = jnp.dot(normed_one, qkv_weight, preferred_element_type=jnp.float32)
    queries = (projected[:, :model_width] + query_bias).astype(jnp.bfloat16)
    key_rows = projected[:, model_width : 2 * model_width].astype(jnp.bfloat16)
    value_rows = (projected[:, 2 * model_width :] + value_bias).astype(jnp.bfloat16)
    gathered_keys, gathered_values = (
        lax.all_gather(key_rows, "seq", axis=0, tiled=True),
        lax.all_gather(value_rows, "seq", axis=0, tiled=True),
    )
    same_item = segment[:, None] == jnp.tile(segment, seq_count)[None, :]

    def head_scores(query_head, key_head):
        raw = contract(query_head, key_head, 1, 1) * scale_factor
        return jnp.where(same_item, raw, NEGATIVE)

    def head_forward(head_index):
        start = head_index * head_width
        query_head = lax.dynamic_slice_in_dim(queries, start, head_width, 1)
        key_head = lax.dynamic_slice_in_dim(gathered_keys, start, head_width, 1)
        value_head = lax.dynamic_slice_in_dim(gathered_values, start, head_width, 1)
        scores = head_scores(query_head, key_head)
        row_top = jnp.max(scores, -1, keepdims=True)
        exponent = jnp.exp(scores - row_top)
        row_total = jnp.sum(exponent, -1, keepdims=True)
        attention = (exponent / row_total).astype(jnp.bfloat16)
        mixed = jnp.dot(attention, value_head, preferred_element_type=jnp.float32)
        return (mixed, (row_top + jnp.log(row_total))[:, 0])

    head_out, log_totals = lax.map(head_forward, jnp.arange(head_count))
    attended = (head_out.transpose(1, 0, 2).reshape(row_count, model_width) * head_cols).astype(
        jnp.bfloat16
    )
    branch_one = jnp.dot(attended, proj_weight, preferred_element_type=jnp.float32) + proj_bias
    middle = inputs + gate_one * branch_one
    normed_mid, pull_two = jax.vjp(norm_modulate, middle, shift_two, scale_two)
    normed_two = normed_mid.astype(jnp.bfloat16)
    before = jnp.dot(normed_two, inner_weight, preferred_element_type=jnp.float32) + inner_bias

    def activate(value):
        return jax.nn.gelu(value, approximate=True) * channel_keep

    active_full, pull_gelu = jax.vjp(activate, before)
    activated = active_full.astype(jnp.bfloat16)
    branch_two = jnp.dot(activated, outer_weight, preferred_element_type=jnp.float32) + outer_bias
    route_cols = keep_route.astype(jnp.float32)[:, None]
    block_out = (middle + route_cols * gate_two * branch_two).astype(jnp.bfloat16)
    upstream = cotangent.astype(jnp.float32)
    grad_branch_two = (route_cols * gate_two * upstream).astype(jnp.bfloat16)
    grad_gate_two = route_cols * branch_two * upstream
    grad_outer_weight = contract(activated, grad_branch_two, 0, 0)
    grad_outer_bias = jnp.sum(grad_branch_two.astype(jnp.float32), 0)
    grad_active = contract(grad_branch_two, outer_weight, 1, 1)
    grad_before = pull_gelu(grad_active)[0].astype(jnp.bfloat16)
    grad_inner_weight = contract(normed_two, grad_before, 0, 0)
    grad_inner_bias = jnp.sum(grad_before.astype(jnp.float32), 0)
    grad_normed_two = contract(grad_before, inner_weight, 1, 1)
    grad_mid_part, grad_shift_two, grad_scale_two = pull_two(grad_normed_two)
    grad_middle = upstream + grad_mid_part
    grad_gate_one = grad_middle * branch_one
    grad_branch_one = (gate_one * grad_middle).astype(jnp.bfloat16)
    grad_proj_weight = contract(attended, grad_branch_one, 0, 0)
    grad_proj_bias = jnp.sum(grad_branch_one.astype(jnp.float32), 0)
    grad_attended = contract(grad_branch_one, proj_weight, 1, 1).astype(
        jnp.bfloat16
    ) * head_cols.astype(jnp.bfloat16)

    def head_backward(head_index):
        start = head_index * head_width
        query_head = lax.dynamic_slice_in_dim(queries, start, head_width, 1)
        key_head = lax.dynamic_slice_in_dim(gathered_keys, start, head_width, 1)
        value_head = lax.dynamic_slice_in_dim(gathered_values, start, head_width, 1)
        grad_head = lax.dynamic_slice_in_dim(grad_attended, start, head_width, 1)
        row_lse = lax.dynamic_index_in_dim(log_totals, head_index, 0, keepdims=False)
        scores = head_scores(query_head, key_head)
        probs_full = jnp.exp(scores - row_lse[:, None])
        attention = probs_full.astype(jnp.bfloat16)
        grad_attention = contract(grad_head, value_head, 1, 1)
        inner_sum = jnp.sum(probs_full * grad_attention, -1, keepdims=True)
        grad_scores = (probs_full * (grad_attention - inner_sum)).astype(jnp.bfloat16)
        grad_query = (
            jnp.dot(grad_scores, key_head, preferred_element_type=jnp.float32) * scale_factor
        )
        grad_key = contract(grad_scores, query_head, 0, 0) * scale_factor
        grad_value = contract(attention, grad_head, 0, 0)
        return (grad_query, grad_key, grad_value)

    query_terms, key_terms, value_terms = lax.map(head_backward, jnp.arange(head_count))
    grad_queries = (
        query_terms.transpose(1, 0, 2).reshape(row_count, model_width).astype(jnp.bfloat16)
    )
    key_flat = key_terms.transpose(1, 0, 2).reshape(-1, model_width)
    value_flat = value_terms.transpose(1, 0, 2).reshape(-1, model_width)
    own_keys, own_values = (
        lax.psum_scatter(
            key_flat.astype(jnp.bfloat16), "seq", scatter_dimension=0, tiled=True
        ).astype(jnp.float32),
        lax.psum_scatter(
            value_flat.astype(jnp.bfloat16), "seq", scatter_dimension=0, tiled=True
        ).astype(jnp.float32),
    )
    grad_keys = own_keys.astype(jnp.bfloat16)
    grad_values = own_values.astype(jnp.bfloat16)
    grad_columns = jnp.concatenate([grad_queries, grad_keys, grad_values], 1)
    grad_qkv_weight = contract(normed_one, grad_columns, 0, 0)
    grad_query_bias = jnp.sum(grad_queries.astype(jnp.float32), 0)
    grad_value_bias = jnp.sum(grad_values.astype(jnp.float32), 0)
    grad_normed_one = contract(grad_columns, qkv_weight, 1, 1)
    grad_in_part, grad_shift_one, grad_scale_one = pull_one(grad_normed_one)
    grad_tokens = grad_middle + grad_in_part
    grad_token_mod = jnp.concatenate(
        [
            grad_shift_one,
            grad_scale_one,
            grad_gate_one,
            grad_shift_two,
            grad_scale_two,
            grad_gate_two,
        ],
        1,
    )
    grad_modulation = contract_exact(onehot, grad_token_mod, 0, 0)
    grad_ada_weight = contract_exact(cond_act.astype(jnp.float32), grad_modulation, 0, 0)
    grad_ada_bias = jnp.sum(grad_modulation, 0)
    (
        ada_w_part,
        ada_b_part,
        qkv_w_part,
        query_b_part,
        value_b_part,
        proj_w_part,
        proj_b_part,
        inner_w_part,
        inner_b_part,
        outer_w_part,
        outer_b_part,
    ) = (
        lax.psum_scatter(
            rows_view(grad_ada_weight, group_count, seq_count).astype(jnp.bfloat16),
            "seq",
            scatter_dimension=1,
            tiled=True,
        ).astype(jnp.float32),
        lax.psum_scatter(
            rows_view(grad_ada_bias, group_count, seq_count).astype(jnp.bfloat16),
            "seq",
            scatter_dimension=1,
            tiled=True,
        ).astype(jnp.float32),
        lax.psum_scatter(
            rows_view(grad_qkv_weight, group_count, seq_count).astype(jnp.bfloat16),
            "seq",
            scatter_dimension=1,
            tiled=True,
        ).astype(jnp.float32),
        lax.psum_scatter(
            rows_view(grad_query_bias, group_count, seq_count).astype(jnp.bfloat16),
            "seq",
            scatter_dimension=1,
            tiled=True,
        ).astype(jnp.float32),
        lax.psum_scatter(
            rows_view(grad_value_bias, group_count, seq_count).astype(jnp.bfloat16),
            "seq",
            scatter_dimension=1,
            tiled=True,
        ).astype(jnp.float32),
        lax.psum_scatter(
            rows_view(grad_proj_weight, group_count, seq_count).astype(jnp.bfloat16),
            "seq",
            scatter_dimension=1,
            tiled=True,
        ).astype(jnp.float32),
        lax.psum_scatter(
            rows_view(grad_proj_bias, group_count, seq_count).astype(jnp.bfloat16),
            "seq",
            scatter_dimension=1,
            tiled=True,
        ).astype(jnp.float32),
        lax.psum_scatter(
            rows_view(grad_inner_weight, group_count, seq_count).astype(jnp.bfloat16),
            "seq",
            scatter_dimension=1,
            tiled=True,
        ).astype(jnp.float32),
        lax.psum_scatter(
            rows_view(grad_inner_bias, group_count, seq_count).astype(jnp.bfloat16),
            "seq",
            scatter_dimension=1,
            tiled=True,
        ).astype(jnp.float32),
        lax.psum_scatter(
            rows_view(grad_outer_weight, group_count, seq_count).astype(jnp.bfloat16),
            "seq",
            scatter_dimension=1,
            tiled=True,
        ).astype(jnp.float32),
        lax.psum_scatter(
            rows_view(grad_outer_bias, group_count, seq_count).astype(jnp.bfloat16),
            "seq",
            scatter_dimension=1,
            tiled=True,
        ).astype(jnp.float32),
    )
    shares = (
        lax.psum_scatter(
            ada_w_part.astype(jnp.bfloat16), "bucket", scatter_dimension=0, tiled=True
        ).astype(jnp.float32),
        lax.psum_scatter(
            ada_b_part.astype(jnp.bfloat16), "bucket", scatter_dimension=0, tiled=True
        ).astype(jnp.float32),
        lax.psum_scatter(
            qkv_w_part.astype(jnp.bfloat16), "bucket", scatter_dimension=0, tiled=True
        ).astype(jnp.float32),
        lax.psum_scatter(
            query_b_part.astype(jnp.bfloat16), "bucket", scatter_dimension=0, tiled=True
        ).astype(jnp.float32),
        lax.psum_scatter(
            value_b_part.astype(jnp.bfloat16), "bucket", scatter_dimension=0, tiled=True
        ).astype(jnp.float32),
        lax.psum_scatter(
            proj_w_part.astype(jnp.bfloat16), "bucket", scatter_dimension=0, tiled=True
        ).astype(jnp.float32),
        lax.psum_scatter(
            proj_b_part.astype(jnp.bfloat16), "bucket", scatter_dimension=0, tiled=True
        ).astype(jnp.float32),
        lax.psum_scatter(
            inner_w_part.astype(jnp.bfloat16), "bucket", scatter_dimension=0, tiled=True
        ).astype(jnp.float32),
        lax.psum_scatter(
            inner_b_part.astype(jnp.bfloat16), "bucket", scatter_dimension=0, tiled=True
        ).astype(jnp.float32),
        lax.psum_scatter(
            outer_w_part.astype(jnp.bfloat16), "bucket", scatter_dimension=0, tiled=True
        ).astype(jnp.float32),
        lax.psum_scatter(
            outer_b_part.astype(jnp.bfloat16), "bucket", scatter_dimension=0, tiled=True
        ).astype(jnp.float32),
    )
    shares = tuple((rows_back(share) for share in shares))
    return (
        block_out,
        grad_tokens,
        shares[0],
        shares[1],
        shares[2],
        shares[3],
        shares[4],
        shares[5],
        shares[6],
        shares[7],
        shares[8],
        shares[9],
        shares[10],
    )


def solution(mesh):
    return jax.shard_map(
        on_device,
        mesh=mesh,
        in_specs=(
            P(("bucket", "seq"), None),
            P(("bucket", "seq")),
            P(("bucket", "seq")),
            P("bucket", None),
            P("bucket"),
            P(),
            P(),
            P(),
            P(),
            P(),
            P(),
            P(),
            P(),
            P(),
            P(),
            P(),
            P(),
            P(),
            P(("bucket", "seq"), None),
        ),
        out_specs=(
            P(("bucket", "seq"), None),
            P(("bucket", "seq"), None),
            P(("bucket", "seq"), None),
            P(("bucket", "seq")),
            P(("bucket", "seq"), None),
            P(("bucket", "seq")),
            P(("bucket", "seq")),
            P(("bucket", "seq"), None),
            P(("bucket", "seq")),
            P(("bucket", "seq"), None),
            P(("bucket", "seq")),
            P(("bucket", "seq"), None),
            P(("bucket", "seq")),
        ),
        check_vma=False,
    )
```

profile of v0, /device:TPU:0, one launch (start us, length us, event | category | flops | bytes accessed | tf_op | source)
XLA Modules:
  0.0 2141.9 jit_solution(14081856002778557605)
XLA Ops:
  11.4 7.8 convolution_add_fusion
  19.3 5.7 fusion.62
  25.0 5.0 copy-done.2
  30.7 5.0 fusion.94
  44.6 4.1 fusion.85
  48.7 83.0 %all-gather.5.cloned.1.call-done = bf16[2048,1152]{1,0:T(8,128)(2,1)} async-done(((bf16[512,1152]{1,0:T(8,128)(2,1)}), bf16[2048,1152]{1,0:T(8,128)(2,1)}) %all-gather.5.cloned.1.call-update) | async-done | bytes 4718608 | tf_op jit(solution)/shard_map/all_gather | solution.py:84
  131.7 89.5 %all-gather.3.cloned.1.call-done = bf16[2048,1152]{1,0:T(8,128)(2,1)} async-done(((bf16[512,1152]{1,0:T(8,128)(2,1)}), bf16[2048,1152]{1,0:T(8,128)(2,1)}) %all-gather.3.cloned.1.call-update) | async-done | bytes 4718608 | tf_op jit(solution)/shard_map/all_gather | solution.py:83
  221.2 118.7 %while.30 = (s32[]{:T(128)}, f32[16,512,72]{1,2,0:T(8,128)}, f32[16,512]{1,0:T(8,128)S(1)}, s32[16]{0:T(128)S(1)}, bf16[512,1152]{1,0:T(8,128)(2,1)}, /*index=5*...) while((s32[]{:T(128)}, f32[16,512,72]{1,2,0:T(8,128)}, ...), condition=%wide.region_5.6_spmd.clone.clone, body=%wide.region_2.5_spmd.clone.sunk.clone | while | flops 311426560 | bytes 13941939 | solution.py:105
  225.4 3.1 fusion.156
  232.9 3.1 fusion.156
  240.3 3.1 fusion.156
  247.8 3.1 fusion.156
  255.2 3.1 fusion.156
  262.7 3.1 fusion.156
  270.1 3.1 fusion.156
  277.6 3.1 fusion.156
  285.0 3.1 fusion.156
  292.5 3.1 fusion.156
  299.9 3.1 fusion.156
  307.3 3.1 fusion.156
  314.8 3.1 fusion.156
  322.2 3.1 fusion.156
  329.7 3.1 fusion.156
  342.0 5.8 fusion.90
  348.1 3.4 fusion.53
  351.6 8.8 fusion.95
  360.4 18.0 fusion.93
  378.5 12.0 multiply_reduce_fusion.1
  390.5 17.5 fusion.89
  408.0 3.7 fusion.87
  414.6 256.1 %while.31 = (s32[]{:T(128)}, bf16[16,512,72]{1,2,0:T(8,128)(2,1)}, bf16[16,2048,72]{1,2,0:T(8,128)(2,1)}, bf16[16,2048,72]{1,2,0:T(8,128)(2,1)}, s32[16]{0:T(128...) while((s32[]{:T(128)}, bf16[16,512,72]{1,2,0:T(8,128)(2,1)}, ...), condition=%wide.region_14.15_spmd.clone.clone, body=%wide.region_12.14_spmd.clone.sunk.clone | while | flops 765644288 | bytes 34904308 | solution.py:163
  580.4 3.0 multiply_reduce_fusion.7
  672.2 3.1 convolution_convert_fusion.4
  679.0 13.5 convolution_convert_fusion.1
  693.8 10.3 convolution_convert_fusion.2
  704.1 14.0 convert_element_type.245
  718.0 13.1 copy.76
  731.3 23.3 %reduce-scatter.21.cloned.1.call-done = bf16[512,1152]{0,1:T(8,128)(2,1)} async-done(((bf16[2048,1152]{0,1:T(8,128)(2,1)}), bf16[512,1152]{0,1:T(8,128)(2,1)}) %reduce-scatter.21.cloned.1.call-update) | async-done | bytes 1179664 | tf_op jit(solution)/shard_map/reduce_scatter | solution.py:170
  754.5 88.0 %reduce-scatter.23.cloned.1.call-done = bf16[512,1152]{0,1:T(8,128)(2,1)} async-done(((bf16[2048,1152]{0,1:T(8,128)(2,1)}), bf16[512,1152]{0,1:T(8,128)(2,1)}) %reduce-scatter.23.cloned.1.call-update) | async-done | bytes 1179664 | tf_op jit(solution)/shard_map/reduce_scatter | solution.py:173
  842.5 9.3 convolution_convert_fusion.3
  851.8 12.6 convert_element_type.239
  864.4 9.1 copy.66
  874.8 11.3 constant_dynamic-update-slice_fusion.1
  886.2 4.2 fusion.88
  899.9 8.2 fusion.92
  908.1 15.5 convolution_convert_fusion
  923.6 18.2 convert_element_type.235
  941.8 15.2 copy.62
  962.0 300.6 %all-reduce.17.cloned.1.call-done = bf16[8,4,144,1152]{3,2,1,0:T(8,128)(2,1)} async-done(((bf16[8,4,144,1152]{3,2,1,0:T(8,128)(2,1)}), bf16[8,4,144,1152]{3,2,1,0:T(8,128)(2,1)}) %all-reduce.17.cloned.1.call-update) | async-done | bytes 10616848
  1262.6 4.1 constant_dynamic-slice_fusion.1
  1266.8 177.4 %reduce-scatter.35.cloned.1.call-done = bf16[8,1,36,4608]{3,0,2,1:T(8,128)(2,1)} async-done(((bf16[8,4,36,4608]{3,0,2,1:T(8,128)(2,1)}), bf16[8,1,36,4608]{3,0,2,1:T(8,128)(2,1)}) %reduce-scatter.35.cloned.1.call-update) | async-done | bytes 2654224 | tf_op jit(solution)/shard_map/reduce_scatter | solution.py:255
  1444.2 4.2 copy.77
  1448.5 137.2 %reduce-scatter.31.cloned.1.call-done = bf16[8,1,36,3456]{3,0,2,1:T(8,128)(2,1)} async-done(((bf16[8,4,36,3456]{3,0,2,1:T(8,128)(2,1)}), bf16[8,1,36,3456]{3,0,2,1:T(8,128)(2,1)}) %reduce-scatter.31.cloned.1.call-update) | async-done | bytes 1990672 | tf_op jit(solution)/shard_map/reduce_scatter | solution.py:225
  1585.7 3.2 copy.67
  1589.0 267.2 %reduce-scatter.25.cloned.1.call-done = bf16[8,1,36,6912]{3,0,2,1:T(8,128)(2,1)} async-done(((bf16[8,4,36,6912]{3,0,2,1:T(8,128)(2,1)}), bf16[8,1,36,6912]{3,0,2,1:T(8,128)(2,1)}) %reduce-scatter.25.cloned.1.call-update) | async-done | bytes 3981328 | tf_op jit(solution)/shard_map/reduce_scatter | solution.py:213
  1856.3 4.8 copy.63
  1863.0 15.4 reduce-scatter.39.cloned.1.call-done
  1879.1 36.0 %reduce-scatter.45.cloned.1.call-done = bf16[1,1,36,1152]{3,2,1,0:T(8,128)(2,1)} async-done(((bf16[8,1,36,1152]{3,2,1,0:T(8,128)(2,1)}), bf16[1,1,36,1152]{3,2,1,0:T(8,128)(2,1)}) %reduce-scatter.45.cloned.1.call-update) | async-done | bytes 82960
  1918.5 19.1 all-reduce.14
  1939.6 22.5 %all-reduce.13 = (bf16[8,1,216]{2,1,0:T(2,128)(2,1)S(1)}, bf16[8,1,36]{2,1,0:T(2,128)(2,1)S(1)}, bf16[8,1,36]{2,1,0:T(2,128)(2,1)S(1)}, bf16[8,1,36]{2,1,0:T(2,1...) all-reduce(bf16[8,1,216]{2,1,0:T(2,128)(2,1)S(1)} %copy.65, ...), channel_id=7, replica_groups=mesh['bucket'=8,'seq'=4] {'bucket'}, use_global_device_ids=true, to_apply=%region_23.24.clone | all-reduce | flops 4032 | bytes 16128
  1968.8 13.4 reduce-scatter.41.cloned.1.call-done
  1984.0 47.1 %reduce-scatter.37.cloned.1.call-done = bf16[1,1,36,4608]{3,2,1,0:T(8,128)(2,1)} async-done(((bf16[8,1,36,4608]{3,2,1,0:T(8,128)(2,1)}), bf16[1,1,36,4608]{3,2,1,0:T(8,128)(2,1)}) %reduce-scatter.37.cloned.1.call-update) | async-done | bytes 331792 | tf_op jit(solution)/shard_map/reduce_scatter | solution.py:302
  2033.0 43.3 %reduce-scatter.43.cloned.1.call-done = bf16[1,1,36,3456]{3,2,1,0:T(8,128)(2,1)} async-done(((bf16[8,1,36,3456]{3,2,1,0:T(8,128)(2,1)}), bf16[1,1,36,3456]{3,2,1,0:T(8,128)(2,1)}) %reduce-scatter.43.cloned.1.call-update) | async-done | bytes 248848
  2078.1 54.7 %reduce-scatter.27.cloned.1.call-done = bf16[1,1,36,6912]{3,2,1,0:T(8,128)(2,1)} async-done(((bf16[8,1,36,6912]{3,2,1,0:T(8,128)(2,1)}), bf16[1,1,36,6912]{3,2,1,0:T(8,128)(2,1)}) %reduce-scatter.27.cloned.1.call-update) | async-done | bytes 497680 | tf_op jit(solution)/shard_map/reduce_scatter | solution.py:281
  (426 shorter events, 335.5 us)
Async XLA Ops:
  7.2 334.7 %copy-start = (bf16[1152,1152]{1,0:T(8,128)(2,1)S(1)}, bf16[1152,1152]{1,0:T(8,128)(2,1)}, u32[]{:S(2)}) copy-start(bf16[1152,1152]{1,0:T(8,128)(2,1)} %param.35) | copy-start | bytes 7962628
  7.2 124.5 %all-gather.5.cloned.1.call-start = ((), (), s32[]{:S(2)}) async-start(), calls=%async_computation.14 | async-start | bytes 5898240 | tf_op jit(solution)/shard_map/all_gather | solution.py:84
  8.9 16.1 copy-start.31
  8.9 21.7 %slice-start.3 = ((s8[7962624]{0:T(1024)(128)(4,1)}), s8[4194304]{0:T(1024)(128)(4,1)S(1)}, s32[]{:S(2)}) async-start(s8[7962624]{0:T(1024)(128)(4,1)} %bitcast.162), calls=%async_computation.32 | async-start | bytes 8388608
  11.4 13.6 copy-start.33
  11.4 7.9 copy-start.28
  11.4 19.3 slice-start.4
  19.2 10.8 copy-start.5
  25.0 5.1 copy-start.2
  30.7 5.1 copy-start.26
  30.7 5.1 copy-start.40
  30.7 5.1 copy-start.41
  35.8 3.6 copy-start.17
  39.4 3.6 copy-start.44
  39.4 3.7 copy-start.42
  39.4 4.0 copy-start.43
  39.4 181.7 %all-gather.3.cloned.1.call-start = ((), (), s32[]{:S(2)}) async-start(), calls=%async_computation.13 | async-start | bytes 5898240 | tf_op jit(solution)/shard_map/all_gather | solution.py:83
  42.3 712.2 %reduce-scatter.21.cloned.1.call-start = ((), (), s32[]{:S(2)}) async-start(), calls=%async_computation.15 | async-start | bytes 5898240 | tf_op jit(solution)/shard_map/reduce_scatter | solution.py:170
  339.9 2.0 copy-start.6
  339.9 2.0 copy-start.30
  341.9 5.8 copy-start.10
  341.9 9.6 slice-start
  342.0 9.6 slice-start.1
  347.7 42.7 %copy-start.3 = (f32[512,1152]{1,0:T(8,128)}, f32[512,1152]{1,0:T(8,128)S(1)}, u32[]{:S(2)}) copy-start(f32[512,1152]{1,0:T(8,128)S(1)} %get-tuple-element.231) | copy-start | bytes 7077892
  348.1 3.5 slice-start.2
  351.6 8.8 copy-start.21
  351.6 8.8 copy-start.23
  351.6 8.8 copy-start.45
  378.5 12.0 copy-start.46
  390.4 17.5 copy-start.12
  390.5 17.5 copy-start.8
  408.0 3.7 copy-start.15
  411.7 2.9 copy-start.25
  670.7 1.3 copy-start.11
  670.7 171.8 %reduce-scatter.23.cloned.1.call-start = ((), (), s32[]{:S(2)}) async-start(), calls=%async_computation.16 | async-start | bytes 5898240 | tf_op jit(solution)/shard_map/reduce_scatter | solution.py:173
  671.3 287.3 %reduce-scatter.33.cloned.1.call-start = ((), (), s32[]{:S(2)}) async-start(), calls=%async_computation.21 | async-start | bytes 3317760 | tf_op jit(solution)/shard_map/reduce_scatter | solution.py:243
  677.7 584.9 %all-reduce.17.cloned.1.call-start = ((), (), s32[]{:S(2)}) async-start(), calls=%async_computation.26 | async-start | bytes 21233664
  692.6 751.7 %reduce-scatter.35.cloned.1.call-start = ((), (), s32[]{:S(2)}) async-start(), calls=%async_computation.22 | async-start | bytes 13271040 | tf_op jit(solution)/shard_map/reduce_scatter | solution.py:255
  731.2 111.3 %copy-start.18 = (bf16[16,512,72]{1,2,0:T(8,128)(2,1)S(1)}, bf16[16,512,72]{1,2,0:T(8,128)(2,1)}, u32[]{:S(2)}) copy-start(bf16[16,512,72]{1,2,0:T(8,128)(2,1)} %get-tuple-element.117) | copy-start | bytes 3538948
  731.2 111.3 %copy-start.27 = (bf16[512,1152]{1,0:T(8,128)(2,1)S(1)}, bf16[512,1152]{1,0:T(8,128)(2,1)}, u32[]{:S(2)}) copy-start(bf16[512,1152]{1,0:T(8,128)(2,1)} %copy-done.26) | copy-start | bytes 3538948
  731.2 854.5 %reduce-scatter.31.cloned.1.call-start = ((), (), s32[]{:S(2)}) async-start(), calls=%async_computation.20 | async-start | bytes 9953280 | tf_op jit(solution)/shard_map/reduce_scatter | solution.py:225
  873.5 1.3 copy-start.7
  873.5 1.3 copy-start.32
  873.6 12.6 copy-start.36
  873.6 12.6 copy-start.34
  873.6 982.7 %reduce-scatter.25.cloned.1.call-start = ((), (), s32[]{:S(2)}) async-start(), calls=%async_computation.17 | async-start | bytes 19906560 | tf_op jit(solution)/shard_map/reduce_scatter | solution.py:213
  886.2 4.2 copy-start.9
  886.2 4.2 copy-start.14
  886.2 4.2 copy-start.16
  890.4 2.8 copy-start.13
  893.2 2.5 copy-start.4
  895.7 2.4 copy-start.20
  899.9 8.3 copy-start.29
  957.0 3.6 copy-start.48
  957.0 921.4 %reduce-scatter.39.cloned.1.call-start = ((), (), s32[]{:S(2)}) async-start(), calls=%async_computation.24 | async-start | bytes 20480 | tf_op jit(solution)/shard_map/reduce_scatter | solution.py:261
  958.5 956.6 %reduce-scatter.45.cloned.1.call-start = ((), (), s32[]{:S(2)}) async-start(), calls=%async_computation.28 | async-start | bytes 829440
  960.6 978.3 %reduce-scatter.29.cloned.1.call-start = ((), (), s32[]{:S(2)}) async-start(), calls=%async_computation.19 | async-start | bytes 20480 | tf_op jit(solution)/shard_map/reduce_scatter | solution.py:219
  962.0 1020.2 %reduce-scatter.41.cloned.1.call-start = ((), (), s32[]{:S(2)}) async-start(), calls=%async_computation.25 | async-start | bytes 2985984 | tf_op jit(solution)/shard_map/reduce_scatter | solution.py:308
  1266.8 764.4 %reduce-scatter.37.cloned.1.call-start = ((), (), s32[]{:S(2)}) async-start(), calls=%async_computation.23 | async-start | bytes 3317760 | tf_op jit(solution)/shard_map/reduce_scatter | solution.py:302
  1448.4 627.9 %reduce-scatter.43.cloned.1.call-start = ((), (), s32[]{:S(2)}) async-start(), calls=%async_computation.27 | async-start | bytes 2488320
  1589.0 543.8 %reduce-scatter.27.cloned.1.call-start = ((), (), s32[]{:S(2)}) async-start(), calls=%async_computation.18 | async-start | bytes 4976640 | tf_op jit(solution)/shard_map/reduce_scatter | solution.py:281
  1861.1 1.4 copy-start.37
  1861.1 1.5 copy-start.19
  1916.6 218.3 %copy-start.1 = (bf16[1152,1152]{1,0:T(8,128)(2,1)S(1)}, bf16[1152,1152]{1,0:T(8,128)(2,1)}, u32[]{:S(2)}) copy-start(bf16[1152,1152]{1,0:T(8,128)(2,1)} %param.35) | copy-start | bytes 7962628
  (6 other events, 5.7 us)
Sparse Core Ops, SparseCore 0:
  39.5 92.0 all-gather.4
  133.2 87.8 all-gather.2
  670.8 83.6 reduce-scatter.20
  756.7 85.7 reduce-scatter.22
  844.6 53.1 reduce-scatter.32
  900.2 362.3 all-reduce.16
  1265.1 179.1 reduce-scatter.34
  1446.6 139.0 reduce-scatter.30
  1588.2 268.0 reduce-scatter.24
  1858.9 19.4 reduce-scatter.38
  1882.5 32.4 reduce-scatter.44
  1917.8 18.8 reduce-scatter.28
  1940.2 41.8 reduce-scatter.40
  1985.8 45.2 reduce-scatter.36
  2034.8 41.5 reduce-scatter.42
  2080.1 52.6 reduce-scatter.26
where the time goes:
time: 2160 us; the launch traced here: 2140 us
  waiting for transfers between devices  1380 us (64%)
  matrix products  439 us (20%)
  local copies, waits for them, and re-layouts  147 us (7%)
  other arithmetic  67.7 us (3%)
  loops' own time  52.8 us (2%)
  blocking collectives  41.6 us (2%)
    unnamed x19, waiting for transfers between devices  381 us
    dot_general x88, matrix products, contract(): lax.dot_general(left, right, (((left_dim,), (right_dim,)), ((), ())), pre...  271 us
    reduce_scatter x1, waiting for transfers between devices, on_device(): lax.psum_scatter(rows_view(grad_ada_weight, group_count, seq_count).astyp...  267 us
    reduce_scatter x1, waiting for transfers between devices, on_device(): lax.psum_scatter(rows_view(grad_inner_weight, group_count, seq_count).ast...  177 us
    reduce_scatter x1, waiting for transfers between devices, on_device(): lax.psum_scatter(rows_view(grad_qkv_weight, group_count, seq_count).astyp...  137 us
    all_gather x1, waiting for transfers between devices, on_device(): lax.all_gather(key_rows, 'seq', axis=0, tiled=True)  89.5 us
    reduce_scatter x1, waiting for transfers between devices, on_device(): lax.psum_scatter(value_flat.astype(jnp.bfloat16), 'seq', scatter_dimensio...  88 us
    all_gather x1, waiting for transfers between devices, on_device(): lax.all_gather(value_rows, 'seq', axis=0, tiled=True)  83 us
  transfers between devices with their start and end apart: 16, of which 14 were waited for; matrix products, arithmetic and copies ran while one was open for 10% of the time, Pallas kernels for 0%

commit v1 on v0

v1 whole, which is shorter than its diff:
```python
import functools

import jax
import jax.numpy as jnp
from jax import lax
from jax.experimental import pallas as pl
from jax.experimental.pallas import tpu as pltpu
from jax.sharding import PartitionSpec as P

EPSILON = 1e-06
LOG2E = 1.4426950408889634
LANES = 128
GELU_A = 0.7978845608028654
GELU_B = 0.044715
F32 = jnp.float32
BF16 = jnp.bfloat16


def contract(left, right, left_dim, right_dim, out=F32):
    return lax.dot_general(
        left, right, (((left_dim,), (right_dim,)), ((), ())), preferred_element_type=out
    )


def swap(array, axis, bit):
    size = lax.axis_size(axis)
    return lax.ppermute(array, axis, [(i, i ^ bit) for i in range(size)])


def pick_kernel(which_ref, index_ref, own_ref, other_ref, out_ref):
    step = pl.program_id(0)

    @pl.when(which_ref[step] == 0)
    def _():
        out_ref[...] = own_ref[...].astype(out_ref.dtype)

    @pl.when(which_ref[step] != 0)
    def _():
        out_ref[...] = other_ref[...].astype(out_ref.dtype)


def pick_blocks(own, other, which, index, out_dtype):
    _, rows, width = own.shape
    count = index.shape[0]
    return pl.pallas_call(
        pick_kernel,
        grid_spec=pltpu.PrefetchScalarGridSpec(
            num_scalar_prefetch=2,
            grid=(count,),
            in_specs=[
                pl.BlockSpec(
                    (1, rows, width), lambda i, w, x: (jnp.where(w[i] == 0, x[i], 0), 0, 0)
                ),
                pl.BlockSpec(
                    (1, rows, width), lambda i, w, x: (jnp.where(w[i] == 0, 0, x[i]), 0, 0)
                ),
            ],
            out_specs=pl.BlockSpec((1, rows, width), lambda i, w, x: (i, 0, 0)),
        ),
        out_shape=jax.ShapeDtypeStruct((count, rows, width), out_dtype),
        cost_estimate=pl.CostEstimate(
            flops=0, bytes_accessed=count * rows * width * 8, transcendentals=0
        ),
        name="pick_blocks",
    )(which, index, own, other)


def head_columns(ref, start, head_width):
    part = ref[:, start : start + head_width]
    return jnp.concatenate(
        [part, jnp.zeros((part.shape[0], LANES - head_width), part.dtype)], axis=1
    )


def attend_kernel(
    heads, head_width, blocks, long_ref, keep_ref, q_ref, own_ref, other_ref, out_ref, lse_ref,
    qh, kh, vh, oh,
):
    rows, width = q_ref.shape
    block = rows // blocks
    factor = head_width**-0.5 * LOG2E
    is_long = long_ref[0] == 1
    for h in range(heads):
        start = h * head_width
        qh[h] = head_columns(q_ref, start, head_width)
        kh[h, :rows] = head_columns(own_ref, start, head_width)
        vh[h, :rows] = head_columns(own_ref, width + start, head_width)

    @pl.when(is_long)
    def _():
        for h in range(heads):
            start = h * head_width
            kh[h, rows:] = head_columns(other_ref, start, head_width)
            vh[h, rows:] = head_columns(other_ref, width + start, head_width)

    def one(h, first, count, key_first, key_count):
        queries = qh[h, pl.ds(first, count), :]
        keys = kh[h, pl.ds(key_first, key_count), :]
        values = vh[h, pl.ds(key_first, key_count), :]
        scores = contract(keys, queries, 1, 1)
        top = jnp.max(scores, 0, keepdims=True)
        exponent = jnp.exp2((scores - top) * factor)
        total = jnp.sum(exponent, 0, keepdims=True)
        mixed = contract(values, exponent.astype(BF16), 0, 0) * (1.0 / total)
        oh[h, pl.ds(first, count), :] = mixed.T.astype(BF16)
        lse_ref[h, :, pl.ds(first, count)] = top * factor + jnp.log2(total)

    def loop(index, first, count, key_first, key_count):
        def body(h, carry):
            keep = keep_ref[index * heads + h] == 1

            @pl.when(keep)
            def _():
                one(h, first, count, key_first, key_count)

            @pl.when(jnp.logical_not(keep))
            def _():
                oh[h, pl.ds(first, count), :] = jnp.zeros((count, LANES), BF16)

            return carry

        lax.fori_loop(0, heads, body, 0)

    @pl.when(is_long)
    def _():
        loop(0, 0, rows, 0, 2 * rows)

    @pl.when(jnp.logical_not(is_long))
    def _():
        for index in range(blocks):
            loop(index, index * block, block, index * block, block)

    for h in range(heads):
        out_ref[:, h * head_width : (h + 1) * head_width] = oh[h, :, :head_width]


def attend(queries, own, other, long_flag, keep, blocks):
    rows, width = queries.shape
    heads = keep.shape[0] // blocks
    head_width = width // heads
    vmem = pl.BlockSpec(memory_space=pltpu.VMEM)
    smem = pl.BlockSpec(memory_space=pltpu.SMEM)
    return pl.pallas_call(
        functools.partial(attend_kernel, heads, head_width, blocks),
        in_specs=[smem, smem, vmem, vmem, vmem],
        out_specs=[vmem, vmem],
        out_shape=[
            jax.ShapeDtypeStruct((rows, width), BF16),
            jax.ShapeDtypeStruct((heads, 1, rows), F32),
        ],
        scratch_shapes=[
            pltpu.VMEM((heads, rows, LANES), BF16),
            pltpu.VMEM((heads, 2 * rows, LANES), BF16),
            pltpu.VMEM((heads, 2 * rows, LANES), BF16),
            pltpu.VMEM((heads, rows, LANES), BF16),
        ],
        compiler_params=pltpu.CompilerParams(vmem_limit_bytes=56 * 1024 * 1024),
        cost_estimate=pl.CostEstimate(
            flops=8 * rows * rows * width,
            bytes_accessed=12 * rows * width,
            transcendentals=2 * rows * rows * heads,
        ),
        name="attend",
    )(long_flag, keep, queries, own, other)


def attend_back_kernel(
    heads, head_width, blocks, long_ref, keep_ref, q_ref, own_ref, other_ref, go_ref, lse_ref,
    delta_ref, gq_ref, gown_ref, gother_ref, qh, kh, vh, gh, gqh, gkh, gvh,
):
    rows, width = q_ref.shape
    block = rows // blocks
    scale = head_width**-0.5
    factor = scale * LOG2E
    is_long = long_ref[0] == 1
    for h in range(heads):
        start = h * head_width
        qh[h] = head_columns(q_ref, start, head_width)
        gh[h] = head_columns(go_ref, start, head_width)
        kh[h, :rows] = head_columns(own_ref, start, head_width)
        vh[h, :rows] = head_columns(own_ref, width + start, head_width)

    @pl.when(is_long)
    def _():
        for h in range(heads):
            start = h * head_width
            kh[h, rows:] = head_columns(other_ref, start, head_width)
            vh[h, rows:] = head_columns(other_ref, width + start, head_width)

    def one(h, first, count, key_first, key_count):
        queries = qh[h, pl.ds(first, count), :]
        grads = gh[h, pl.ds(first, count), :]
        keys = kh[h, pl.ds(key_first, key_count), :]
        values = vh[h, pl.ds(key_first, key_count), :]
        scores = contract(keys, queries, 1, 1)
        probs = jnp.exp2(scores * factor - lse_ref[h, :, pl.ds(first, count)])
        gvh[h, pl.ds(key_first, key_count), :] = contract(
            probs.astype(BF16), grads, 1, 0
        ).astype(BF16)
        grad_probs = contract(values, grads, 1, 1)
        grad_scores = (probs * (grad_probs - delta_ref[h, :, pl.ds(first, count)])).astype(BF16)
        gkh[h, pl.ds(key_first, key_count), :] = (
            contract(grad_scores, queries, 1, 0) * scale
        ).astype(BF16)
        gqh[h, pl.ds(first, count), :] = (
            (contract(keys, grad_scores, 0, 0) * scale).T
        ).astype(BF16)

    def loop(index, first, count, key_first, key_count):
        def body(h, carry):
            keep = keep_ref[index * heads + h] == 1

            @pl.when(keep)
            def _():
                one(h, first, count, key_first, key_count)

            @pl.when(jnp.logical_not(keep))
            def _():
                gqh[h, pl.ds(first, count), :] = jnp.zeros((count, LANES), BF16)
                gkh[h, pl.ds(key_first, key_count), :] = jnp.zeros((key_count, LANES), BF16)
                gvh[h, pl.ds(key_first, key_count), :] = jnp.zeros((key_count, LANES), BF16)

            return carry

        lax.fori_loop(0, heads, body, 0)

    @pl.when(is_long)
    def _():
        loop(0, 0, rows, 0, 2 * rows)
        for h in range(heads):
            start = h * head_width
            gother_ref[:, start : start + head_width] = gkh[h, rows:, :head_width]
            gother_ref[:, width + start : width + start + head_width] = gvh[h, rows:, :head_width]

    @pl.when(jnp.logical_not(is_long))
    def _():
        for index in range(blocks):
            loop(index, index * block, block, index * block, block)
        gother_ref[...] = jnp.zeros_like(gother_ref)

    for h in range(heads):
        start = h * head_width
        gq_ref[:, start : start + head_width] = gqh[h, :, :head_width]
        gown_ref[:, start : start + head_width] = gkh[h, :rows, :head_width]
        gown_ref[:, width + start : width + start + head_width] = gvh[h, :rows, :head_width]


def attend_back(queries, own, other, grad_out, lse, delta, long_flag, keep, blocks):
    rows, width = queries.shape
    heads = keep.shape[0] // blocks
    head_width = width // heads
    vmem = pl.BlockSpec(memory_space=pltpu.VMEM)
    smem = pl.BlockSpec(memory_space=pltpu.SMEM)
    return pl.pallas_call(
        functools.partial(attend_back_kernel, heads, head_width, blocks),
        in_specs=[smem, smem] + [vmem] * 6,
        out_specs=[vmem] * 3,
        out_shape=[
            jax.ShapeDtypeStruct((rows, width), BF16),
            jax.ShapeDtypeStruct((rows, 2 * width), BF16),
            jax.ShapeDtypeStruct((rows, 2 * width), BF16),
        ],
        scratch_shapes=[
            pltpu.VMEM((heads, rows, LANES), BF16),
            pltpu.VMEM((heads, 2 * rows, LANES), BF16),
            pltpu.VMEM((heads, 2 * rows, LANES), BF16),
            pltpu.VMEM((heads, rows, LANES), BF16),
            pltpu.VMEM((heads, rows, LANES), BF16),
            pltpu.VMEM((heads, 2 * rows, LANES), BF16),
            pltpu.VMEM((heads, 2 * rows, LANES), BF16),
        ],
        compiler_params=pltpu.CompilerParams(vmem_limit_bytes=60 * 1024 * 1024),
        cost_estimate=pl.CostEstimate(
            flops=20 * rows * rows * width,
            bytes_accessed=24 * rows * width,
            transcendentals=2 * rows * rows * heads,
        ),
        name="attend_back",
    )(long_flag, keep, queries, own, other, grad_out, lse, delta)


def feed_kernel(
    blocks, sub, share, core_ref, x_ref, g_ref, xk_ref, xs_ref, keep_ref, bias_ref, wi_ref,
    wo_ref, out_ref, gx_ref, wok_ref, wos_ref, wik_ref, wis_ref, gbias_ref, act, gbefore,
):
    rows, _ = x_ref.shape
    block = rows // blocks
    chunk = wi_ref.shape[1]
    core = core_ref[0]
    first = pl.program_id(0) == 0
    for lo in range(0, chunk, sub):
        cols = slice(lo, lo + sub)
        column_sum = jnp.zeros((1, sub), F32)
        for index in range(blocks):
            part = slice(index * block, (index + 1) * block)
            before = contract(x_ref[part], wi_ref[:, cols], 1, 0) + bias_ref[:, cols]
            grad_act = contract(g_ref[part], wo_ref[cols, :], 1, 1)
            keep = keep_ref[index : index + 1, cols]
            square = before * before
            bend = jnp.tanh(GELU_A * before * (1.0 + GELU_B * square))
            half = 0.5 * (1.0 + bend)
            slope = half + (0.5 * GELU_A) * before * (1.0 - bend * bend) * (
                1.0 + (3.0 * GELU_B) * square
            )
            act[part, cols] = (before * half * keep).astype(BF16)
            grad = (grad_act * keep * slope).astype(BF16)
            gbefore[part, cols] = grad
            column_sum += jnp.sum(grad.astype(F32), 0, keepdims=True)
        gbias_ref[:, cols] = column_sum
    out = contract(act[...], wo_ref[...], 1, 0)
    gx = contract(gbefore[...], wi_ref[...], 1, 1)

    @pl.when(first)
    def _():
        out_ref[...] = out
        gx_ref[...] = gx

    @pl.when(jnp.logical_not(first))
    def _():
        out_ref[...] += out
        gx_ref[...] += gx

    wik_ref[...] = contract(xk_ref[...], gbefore[...], 1, 0).astype(BF16)
    wis_ref[...] = contract(xs_ref[...], gbefore[...], 1, 0).astype(BF16)
    grad_wo = contract(act[...], g_ref[...], 0, 0).astype(BF16)
    for pair in range(chunk // (2 * share)):
        even = grad_wo[2 * pair * share : (2 * pair + 1) * share]
        odd = grad_wo[(2 * pair + 1) * share : (2 * pair + 2) * share]

        @pl.when(core == 0)
        def _():
            wok_ref[pair] = even
            wos_ref[pair] = odd

        @pl.when(core != 0)
        def _():
            wok_ref[pair] = odd
            wos_ref[pair] = even


def feed(core, x, grad, x_keep, x_send, keep, bias, wi, wo, blocks, share, chunk, sub):
    rows, width = x.shape
    hidden = wi.shape[1]
    half = x_keep.shape[0]
    pairs = chunk // (2 * share)
    once = pl.Buffered(1)
    whole = lambda shape: pl.BlockSpec(shape, lambda i: (0, 0), pipeline_mode=once)
    return pl.pallas_call(
        functools.partial(feed_kernel, blocks, sub, share),
        grid=(hidden // chunk,),
        in_specs=[
            pl.BlockSpec(memory_space=pltpu.SMEM),
            whole((rows, width)),
            whole((rows, width)),
            whole((half, rows)),
            whole((half, rows)),
            pl.BlockSpec((blocks, chunk), lambda i: (0, i)),
            pl.BlockSpec((1, chunk), lambda i: (0, i)),
            pl.BlockSpec((width, chunk), lambda i: (0, i)),
            pl.BlockSpec((chunk, width), lambda i: (i, 0)),
        ],
        out_specs=[
            pl.BlockSpec((rows, width), lambda i: (0, 0)),
            pl.BlockSpec((rows, width), lambda i: (0, 0)),
            pl.BlockSpec((pairs, share, width), lambda i: (i, 0, 0)),
            pl.BlockSpec((pairs, share, width), lambda i: (i, 0, 0)),
            pl.BlockSpec((half, chunk), lambda i: (0, i)),
            pl.BlockSpec((half, chunk), lambda i: (0, i)),
            pl.BlockSpec((1, chunk), lambda i: (0, i)),
        ],
        out_shape=[
            jax.ShapeDtypeStruct((rows, width), F32),
            jax.ShapeDtypeStruct((rows, width), F32),
            jax.ShapeDtypeStruct((hidden // (2 * share), share, width), BF16),
            jax.ShapeDtypeStruct((hidden // (2 * share), share, width), BF16),
            jax.ShapeDtypeStruct((half, hidden), BF16),
            jax.ShapeDtypeStruct((half, hidden), BF16),
            jax.ShapeDtypeStruct((1, hidden), F32),
        ],
        scratch_shapes=[pltpu.VMEM((rows, chunk), BF16), pltpu.VMEM((rows, chunk), BF16)],
        compiler_params=pltpu.CompilerParams(vmem_limit_bytes=62 * 1024 * 1024),
        cost_estimate=pl.CostEstimate(
            flops=12 * rows * width * hidden,
            bytes_accessed=8 * width * hidden,
            transcendentals=rows * hidden,
        ),
        name="feed",
    )(core, x, grad, x_keep, x_send, keep, bias, wi, wo)


def norm_parts(value):
    center = value - jnp.mean(value, -1, keepdims=True)
    spread = jnp.mean(center * center, -1, keepdims=True)
    inverse = lax.rsqrt(spread + EPSILON)
    return center * inverse, inverse


def norm_back(grad, normed, inverse, scale):
    scaled = grad * (1.0 + scale)
    mean_one = jnp.mean(scaled, -1, keepdims=True)
    mean_two = jnp.mean(scaled * normed, -1, keepdims=True)
    return inverse * (scaled - mean_one - normed * mean_two)


def add_low(left, right):
    return (left.astype(F32) + right.astype(F32)).astype(BF16)


def split_bit(array, dim, bit):
    keep = lax.dynamic_index_in_dim(array, bit, dim, keepdims=False)
    send = lax.dynamic_index_in_dim(array, 1 - bit, dim, keepdims=False)
    return keep, send


def reduce_rows(keep, send, bucket, seq):
    pairs, rows, columns = keep.shape
    seq_count = lax.axis_size("seq")
    current = add_low(keep, swap(send, "bucket", 1))
    bits = []
    while (1 << len(bits)) < pairs:
        bits.append(len(bits))
    count = len(bits)
    half = rows // 2
    halves = []
    for part in range(2):
        piece = current[:, part * half : (part + 1) * half]
        piece = piece.reshape((2,) * count + (half, columns))
        order = bits if part == 0 else bits[::-1]
        left = list(reversed(bits))
        for bit in order:
            dim = left.index(bit)
            mine, theirs = split_bit(piece, dim, (bucket >> (bit + 1)) & 1)
            left.remove(bit)
            piece = add_low(mine, swap(theirs, "bucket", 2 << bit))
        halves.append(piece)
    zbits = []
    while (1 << len(zbits)) < seq_count:
        zbits.append(len(zbits))
    piece = jnp.stack(halves).reshape((2,) * len(zbits) + (rows // seq_count, columns))
    left = list(reversed(zbits))
    for bit in zbits:
        mine, theirs = split_bit(piece, left.index(bit), (seq >> bit) & 1)
        left.remove(bit)
        got = swap(theirs, "seq", 1 << bit)
        if left:
            piece = add_low(mine, got)
        else:
            piece = mine.astype(F32) + got.astype(F32)
    return piece


def gather_all(array):
    bit = 1
    while bit < lax.axis_size("bucket"):
        array = jnp.concatenate([array, swap(array, "bucket", bit)], 0)
        bit *= 2
    parts = [array] + [swap(array, "seq", k) for k in range(1, lax.axis_size("seq"))]
    return jnp.concatenate(parts, 0)


def on_device(
    tokens,
    segment,
    keep_route,
    condition,
    group_bucket,
    head_mask,
    channel_mask,
    ada_weight,
    ada_bias,
    qkv_weight,
    query_bias,
    value_bias,
    proj_weight,
    proj_bias,
    inner_weight,
    inner_bias,
    outer_weight,
    outer_bias,
    cotangent,
):
    rows, width = tokens.shape
    slots = condition.shape[0]
    heads = head_mask.shape[1]
    head_width = width // heads
    hidden = inner_weight.shape[1]
    channel_groups = channel_mask.shape[1]
    group_count = lax.axis_size("bucket")
    seq_count = lax.axis_size("seq")
    bucket = lax.axis_index("bucket")
    seq = lax.axis_index("seq")
    core = bucket % 2
    piece = rows // slots
    block = piece * seq_count
    blocks = rows // block
    chip_blocks = 2 * blocks

    def pair(own, other):
        first = jnp.where(core == 0, own, other)
        second = jnp.where(core == 0, other, own)
        return jnp.stack([first, second])

    bucket_pick = (jnp.arange(head_mask.shape[0]) == group_bucket[0]).astype(F32)
    own_heads = jnp.sum(bucket_pick[:, None] * head_mask.astype(F32), 0)
    own_channels = jnp.sum(bucket_pick[:, None] * channel_mask.astype(F32), 0)
    ids_own = segment.reshape(slots, piece)[:, 0].astype(F32)
    small = jnp.concatenate([ids_own, own_heads, own_channels, keep_route.astype(F32)])
    small_pair = pair(small, swap(small, "bucket", 1))
    tokens_own = tokens.reshape(slots, piece, width)
    tokens_other = swap(tokens_own, "bucket", 1)
    cond_pair = pair(condition, swap(condition, "bucket", 1))
    grads_own = cotangent.reshape(slots, piece, width)
    grads_other = swap(grads_own, "bucket", 1)
    at = slots
    ids_pair = small_pair[:, :at]
    heads_pair = small_pair[:, at : at + heads]
    at += heads
    channels_pair = small_pair[:, at : at + channel_groups]
    at += channel_groups
    route_pair = small_pair[:, at:]

    total = 2 * slots
    same = ids_pair[:, :, None] == ids_pair[:, None, :]
    long = (jnp.sum(same.astype(jnp.int32), 2) > 1).reshape(total)
    numbers = jnp.arange(total)
    key = jnp.where(long, 0, total) + numbers
    rank = jnp.sum((key[None, :] < key[:, None]).astype(jnp.int32), 1)
    order = jnp.sum(jnp.where(rank[None, :] == numbers[:, None], numbers[None, :], 0), 1)
    ordered = order.reshape(seq_count, 2, blocks)
    core_order = lax.dynamic_index_in_dim(ordered, core, 1, keepdims=False)
    turns = jnp.arange(seq_count) ^ seq
    send_pick = core_order[turns].reshape(-1)
    send_which = (send_pick // slots != core).astype(jnp.int32)
    send_index = send_pick % slots
    mine = core_order[seq]
    mine_hot = (mine[:, None] == numbers[None, :]).astype(F32)
    long_flag = jnp.sum(mine_hot[0] * long.astype(F32)).astype(jnp.int32).reshape(1)
    group_hot = (mine[:, None] // slots == jnp.arange(2)[None, :]).astype(F32)
    own_ranks = lax.dynamic_slice_in_dim(rank, core * slots, slots, 0)
    back_which = ((own_ranks % chip_blocks) // blocks != core).astype(jnp.int32)
    back_index = ((own_ranks // chip_blocks) ^ seq) * blocks + own_ranks % blocks

    def bring(own, other):
        sent = pick_blocks(own, other, send_which, send_index, own.dtype)
        sent = sent.reshape(seq_count, blocks, 1, piece, width)
        parts = [sent[0]] + [swap(sent[k], "seq", k) for k in range(1, seq_count)]
        return jnp.concatenate(parts, 1).reshape(blocks, block, width)

    def take_back(array, out_dtype):
        array = array.reshape(blocks, seq_count, piece, width)
        parts = [array[:, 0]] + [swap(array[:, k], "seq", k) for k in range(1, seq_count)]
        own = jnp.stack(parts).reshape(seq_count * blocks, piece, width)
        other = swap(own, "bucket", 1)
        return pick_blocks(own, other, back_which, back_index, out_dtype).reshape(rows, width)

    x = bring(tokens_own, tokens_other).astype(F32)
    upstream = bring(grads_own, grads_other).astype(F32)
    route_all = jnp.stack([route_pair] + [swap(route_pair, "seq", k) for k in range(1, seq_count)])
    route_all = route_all.reshape(seq_count, total, piece)
    route = jnp.sum(mine_hot[:, None, :, None] * route_all[None], 2).reshape(blocks, block, 1)
    keep_heads = jnp.sum(group_hot[:, :, None] * heads_pair[None], 1)
    keep_channels = jnp.sum(group_hot[:, :, None] * channels_pair[None], 1)
    head_ints = keep_heads.astype(jnp.int32).reshape(-1)
    channel_cols = jnp.repeat(keep_channels, hidden // channel_groups, axis=1)
    head_cols = jnp.repeat(keep_heads, head_width, axis=1)[:, None, :]

    block_ids = jnp.sum(mine_hot * ids_pair.reshape(1, total), 1)
    block_groups = jnp.sum(group_hot * jnp.arange(2, dtype=F32)[None, :], 1)
    slot_hot = (
        (block_groups * slots + block_ids)[:, None] == jnp.arange(total, dtype=F32)[None, :]
    ).astype(F32)
    block_cond = jnp.sum(slot_hot[:, :, None] * cond_pair.reshape(1, total, width).astype(F32), 1)
    cond_act = jax.nn.silu(block_cond).astype(BF16)
    modulation = jnp.dot(cond_act, ada_weight, preferred_element_type=F32) + ada_bias
    shift_one, scale_one, gate_one, shift_two, scale_two, gate_two = (
        m[:, None, :] for m in jnp.split(modulation, 6, axis=1)
    )
    cond_all = gather_all(cond_act)

    def flat(array):
        return array.reshape(rows, width)

    def cube(array):
        return array.reshape(blocks, block, width)

    def row_shares(array):
        turned = array.T.reshape(group_count // 2, 2, width // group_count, rows)
        keep, send = split_bit(turned, 1, core)
        return keep.reshape(width // 2, rows), send.reshape(width // 2, rows)

    normed_x, inverse_x = norm_parts(x)
    normed_one = flat((normed_x * (1.0 + scale_one) + shift_one).astype(BF16))
    pair_bias = jnp.concatenate([jnp.zeros_like(value_bias), value_bias])
    own_kv = (
        jnp.dot(normed_one, qkv_weight[:, width:], preferred_element_type=F32) + pair_bias
    ).astype(BF16)
    other_kv = swap(own_kv, "bucket", 1)
    queries = (
        jnp.dot(normed_one, qkv_weight[:, :width], preferred_element_type=F32) + query_bias
    ).astype(BF16)
    attended, lse = attend(queries, own_kv, other_kv, long_flag, head_ints, blocks)
    branch_one = cube(jnp.dot(attended, proj_weight, preferred_element_type=F32) + proj_bias)
    middle = x + gate_one * branch_one

    normed_mid, inverse_mid = norm_parts(middle)
    normed_two = flat((normed_mid * (1.0 + scale_two) + shift_two).astype(BF16))
    grad_branch_two = flat((route * gate_two * upstream).astype(BF16))
    two_keep, two_send = row_shares(normed_two)
    core_ref = core.astype(jnp.int32).reshape(1)
    share = hidden // group_count
    branch_two, grad_two, wo_keep, wo_send, wi_keep, wi_send, grad_inner_bias = feed(
        core_ref,
        normed_two,
        grad_branch_two,
        two_keep,
        two_send,
        channel_cols,
        inner_bias[None, :],
        inner_weight,
        outer_weight,
        blocks,
        share,
        width,
        width // 3,
    )
    grad_outer_weight = reduce_rows(wo_keep, wo_send, bucket, seq)
    by_rows = (group_count // 2, width // group_count, hidden)
    grad_inner_weight = reduce_rows(
        wi_keep.reshape(by_rows), wi_send.reshape(by_rows), bucket, seq
    )
    branch_two = cube(branch_two) + outer_bias
    block_out = take_back((middle + route * gate_two * branch_two).astype(BF16), BF16)
    grad_outer_bias = jnp.sum(grad_branch_two.astype(F32), 0)
    grad_two = cube(grad_two)
    mod_gate_two = jnp.sum(route * branch_two * upstream, 1)
    mod_shift_two = jnp.sum(grad_two, 1)
    mod_scale_two = jnp.sum(grad_two * normed_mid, 1)
    grad_middle = upstream + norm_back(grad_two, normed_mid, inverse_mid, scale_two)
    mod_gate_one = jnp.sum(grad_middle * branch_one, 1)
    grad_branch_one = flat((gate_one * grad_middle).astype(BF16))
    grad_proj_bias = jnp.sum(grad_branch_one.astype(F32), 0)

    grad_attended = flat(
        (
            cube(contract(grad_branch_one, proj_weight, 1, 1).astype(BF16)).astype(F32) * head_cols
        ).astype(BF16)
    )
    head_hot = (jnp.arange(width)[:, None] // head_width == jnp.arange(heads)[None, :]).astype(F32)
    delta = lax.dot_general(
        head_hot,
        grad_attended.astype(F32) * attended.astype(F32),
        (((0,), (1,)), ((), ())),
        precision=lax.Precision.HIGHEST,
    ).reshape(heads, 1, rows)
    grad_queries, grad_own, grad_other = attend_back(
        queries, own_kv, other_kv, grad_attended, lse, delta, long_flag, head_ints, blocks
    )
    half_shape = (group_count // 2, width // group_count, width)
    att_keep, att_send = row_shares(attended)
    grad_proj_weight = reduce_rows(
        contract(att_keep, grad_branch_one, 1, 0, BF16).reshape(half_shape),
        contract(att_send, grad_branch_one, 1, 0, BF16).reshape(half_shape),
        bucket,
        seq,
    )
    grad_kv = add_low(grad_own, swap(grad_other, "bucket", 1))
    grad_columns = jnp.concatenate([grad_queries, grad_kv], 1)
    one_keep, one_send = row_shares(normed_one)
    qkv_shape = (group_count // 2, width // group_count, 3 * width)
    grad_qkv_weight = reduce_rows(
        contract(one_keep, grad_columns, 1, 0, BF16).reshape(qkv_shape),
        contract(one_send, grad_columns, 1, 0, BF16).reshape(qkv_shape),
        bucket,
        seq,
    )
    column_sums = jnp.sum(grad_columns.astype(F32), 0)
    grad_one = cube(contract(grad_columns, qkv_weight, 1, 1))
    mod_shift_one = jnp.sum(grad_one, 1)
    mod_scale_one = jnp.sum(grad_one * normed_x, 1)
    grad_x = grad_middle + norm_back(grad_one, normed_x, inverse_x, scale_one)
    grad_tokens = take_back(grad_x.astype(BF16), F32)

    early = jnp.concatenate(
        [mod_gate_one, mod_shift_two, mod_scale_two, mod_gate_two], 1
    ).reshape(1, -1)
    early_bias = jnp.concatenate([grad_proj_bias, grad_inner_bias[0], grad_outer_bias])[None, :]
    early_all = gather_all(jnp.concatenate([early, early_bias], 1).astype(BF16))
    late = jnp.concatenate([mod_shift_one, mod_scale_one], 1).reshape(1, -1)
    late_bias = jnp.concatenate([column_sums[:width], column_sums[2 * width :]])[None, :]
    late_all = gather_all(jnp.concatenate([late, late_bias], 1).astype(BF16))
    place = bucket * seq_count + seq
    device_count = group_count * seq_count
    early_mod = early_all[:, : 4 * blocks * width].reshape(-1, 4 * width)
    late_mod = late_all[:, : 2 * blocks * width].reshape(-1, 2 * width)
    cond_mine = lax.dynamic_slice_in_dim(
        cond_all, place * (width // device_count), width // device_count, 1
    )
    all_mod = jnp.concatenate([late_mod, early_mod], 1)
    grad_ada_weight = contract(cond_mine, all_mod, 0, 0)

    def own_sum(array):
        size = array.shape[1] // device_count
        own = lax.dynamic_slice_in_dim(array, place * size, size, 1)
        return jnp.sum(own.astype(F32), 0)

    early_rest = early_all[:, 4 * blocks * width :]
    late_rest = late_all[:, 2 * blocks * width :]
    return (
        block_out,
        grad_tokens,
        grad_ada_weight,
        own_sum(all_mod),
        grad_qkv_weight,
        own_sum(late_rest[:, :width]),
        own_sum(late_rest[:, width:]),
        grad_proj_weight,
        own_sum(early_rest[:, :width]),
        grad_inner_weight,
        own_sum(early_rest[:, width : width + hidden]),
        grad_outer_weight,
        own_sum(early_rest[:, width + hidden :]),
    )


def solution(mesh):
    split = P(("bucket", "seq"))
    split_rows = P(("bucket", "seq"), None)
    return jax.shard_map(
        on_device,
        mesh=mesh,
        in_specs=(split_rows, split, split, P("bucket", None), P("bucket"))
        + (P(),) * 13
        + (split_rows,),
        out_specs=(
            split_rows,
            split_rows,
            split_rows,
            split,
            split_rows,
            split,
            split,
            split_rows,
            split,
            split_rows,
            split,
            split_rows,
            split,
        ),
        check_vma=False,
    )
```

time: 2160 us -> 714 us (0.33)
  waiting for transfers between devices: 1380 us -> 218 us
  matrix products: 439 us -> 51.8 us
  Pallas kernels: 0 us -> 134 us
  starting transfers between devices: 0.66 us -> 85.2 us
  loops' own time: 52.8 us -> 0 us
  blocking collectives: 41.6 us -> 0 us
  local copies, waits for them, and re-layouts: 147 us -> 114 us
  other arithmetic: 67.7 us -> 97.9 us
    reduce_scatter x11 -> x0, waiting for transfers between devices: 824 us -> none  [the longest x1 267 us: on_device(): lax.psum_scatter(rows_view(grad_ada_weight, group_count, seq_count).astyp...]
    unnamed x19 -> x0, waiting for transfers between devices: 381 us -> none
    dot_general x88 -> x7, matrix products: 271 us -> 27.4 us  [contract(): lax.dot_general(left, right, (((left_dim,), (right_dim,)), ((), ())), pre...]
    ppermute x0 -> x69, waiting for transfers between devices: none -> 218 us  [swap(): return lax.ppermute(array, axis, [(i, i ^ bit) for i in range(size)])]
    all_gather x2 -> x0, waiting for transfers between devices: 172 us -> none  [the longest x1 89.5 us: on_device(): lax.all_gather(key_rows, 'seq', axis=0, tiled=True)]
    dot_general x40 -> x5, matrix products: 168 us -> 24.4 us  [the longest x1 7.7 us: on_device(): jnp.dot(cond_act, ada_weight, preferred_element_type=F32) + ada_bias]
    pallas_call x0 -> x7, Pallas kernels: none -> 134 us  [the longest x1 53.8 us: feed(): pl.pallas_call(functools.partial(feed_kernel, blocks, sub, share), grid=(...]
    ppermute x0 -> x69, starting transfers between devices: none -> 85.2 us  [swap(): return lax.ppermute(array, axis, [(i, i ^ bit) for i in range(size)])]
  transfers between devices with their start and end apart: 16 -> 69, of which waited for: 14 -> 26; matrix products, arithmetic and copies ran while one was open for 10% -> 35% of each run, Pallas kernels for 0% -> 19%
where the time goes in v1:
time: 714 us; the launch traced here: 705 us
  waiting for transfers between devices  218 us (31%)
  Pallas kernels  134 us (19%)
  local copies, waits for them, and re-layouts  114 us (16%)
  other arithmetic  97.9 us (14%)
  starting transfers between devices  85.2 us (12%)
  matrix products  51.8 us (7%)
    ppermute x69, waiting for transfers between devices, swap(): return lax.ppermute(array, axis, [(i, i ^ bit) for i in range(size)])  218 us
    ppermute x69, starting transfers between devices, swap(): return lax.ppermute(array, axis, [(i, i ^ bit) for i in range(size)])  85.2 us
    pallas_call x1, Pallas kernels, feed(): pl.pallas_call(functools.partial(feed_kernel, blocks, sub, share), grid=(...  53.8 us
    pallas_call x1, Pallas kernels, attend_back(): pl.pallas_call(functools.partial(attend_back_kernel, heads, head_width, b...  32.6 us
    convert_element_type x23, other arithmetic, add_low(): return (left.astype(F32) + right.astype(F32)).astype(BF16)  32.3 us
    dot_general x7, matrix products, contract(): lax.dot_general(left, right, (((left_dim,), (right_dim,)), ((), ())), pre...  27.4 us
    pallas_call x4, Pallas kernels, pick_blocks(): pl.pallas_call(pick_kernel, grid_spec=pltpu.PrefetchScalarGridSpec(num_sc...  25 us
    pallas_call x1, Pallas kernels, attend(): pl.pallas_call(functools.partial(attend_kernel, heads, head_width, blocks...  23 us
  transfers between devices with their start and end apart: 69, of which 26 were waited for; matrix products, arithmetic and copies ran while one was open for 35% of the time, Pallas kernels for 19%

profile of v1, /device:TPU:0, one launch (start us, length us, event | category | flops | bytes accessed | tf_op | source)
XLA Modules:
  0.0 705.2 jit_solution(332735431759949776)
XLA Ops:
  13.8 3.0 collective-permute-start.7
  20.2 7.7 %convolution_add_fusion = f32[2,6912]{1,0:T(2,128)S(1)} fusion(bf16[2,1152]{1,0:T(2,128)(2,1)} %fusion.104, bf16[1152,6912]{1,0:T(8,128)(2,1)} %param.26, f32[6912]{0:T(1024)} %param.27), kind=kOutput, calls=%fused_computation.5 | convolution fusion | flops 31864320 | bytes 16012800 | tf_op jit(solution)/shard_map/dot_general | solution.py:574
  28.9 6.2 pick_blocks.4
  36.7 3.0 collective-permute-start.3
  41.6 10.1 %collective-permute-done.2 = bf16[2,1,64,1152]{3,2,0,1:T(8,128)(2,1)S(1)} collective-permute-done((bf16[2,1,64,1152]{3,2,0,1:T(8,128)(2,1)S(1)}, bf16[2,1,64,1152]{3,2,0,1:T(8,128)(2,1)S(1)}, u32[]{:S(2)}, u32[]{:S(2)}) %collective-permute-start.2) | collective-permute-done | bytes 294944 | tf_op jit(solution)/shard_map/ppermute | solution.py:27
  51.6 8.7 %collective-permute-done.3 = bf16[2,1,64,1152]{3,2,0,1:T(8,128)(2,1)S(1)} collective-permute-done((bf16[2,1,64,1152]{3,2,0,1:T(8,128)(2,1)S(1)}, bf16[2,1,64,1152]{3,2,0,1:T(8,128)(2,1)S(1)}, u32[]{:S(2)}, u32[]{:S(2)}) %collective-permute-start.3) | collective-permute-done | bytes 294944 | tf_op jit(solution)/shard_map/ppermute | solution.py:27
  60.3 3.9 collective-permute-start.9
  67.8 7.4 %fusion.6.own_ref = bf16[512,2304]{1,0:T(8,128)(2,1)} fusion(bf16[512,1152]{1,0:T(8,128)(2,1)S(1)} %fusion.25, bf16[1152,3456]{1,0:T(8,128)(2,1)} %param.28, f32[2304]{0:T(1024)S(1)} %copy-done.86), kind=kOutput, calls=%fused_computation.10 | convolution fusion | flops 2720268288 | bytes 8856576 | tf_op jit(solution)/shard_map/dot_general | solution.py:595
  96.3 6.0 pick_blocks.5
  102.3 2.3 slice_bitcast_fusion.11
  104.6 2.3 collective-permute-start.11
  114.2 4.7 collective-permute-done.11
  119.3 12.2 %collective-permute-done.12 = bf16[2,1,64,1152]{3,2,0,1:T(8,128)(2,1)} collective-permute-done((bf16[2,1,64,1152]{3,2,0,1:T(8,128)(2,1)}, bf16[2,1,64,1152]{3,2,0,1:T(8,128)(2,1)}, u32[]{:S(2)}, u32[]{:S(2)}) %collective-permute-start.12) | collective-permute-done | bytes 294944 | tf_op jit(solution)/shard_map/ppermute | solution.py:27
  131.5 2.2 fusion.68
  136.0 4.6 fusion.12.q_ref
  140.6 23.0 %attend.1 = (bf16[512,1152]{1,0:T(8,128)(2,1)}, f32[16,1,512]{2,1,0:T(1,128)}) custom-call(s32[1]{0:T(128)} %bitcast.13.long_ref, s32[32]{0:T(128)} %convert_element_type.566.keep_ref, bf16[512,1152]{1,0:T(8,128)(2,1)} %fusion.12.q_ref, bf16[512,2304]{1,0:T(8,128)(2,1)} %fusion.6.own_ref, bf16[512,2304]{1,0:T(8,128)(2,1)} %collective-permute-done.6.other_ref), custom_call_target="tpu_custom_call" | custom-call | flops 2415919104 | bytes 7077888 | tf_op jit(solution)/shard_map/attend/pallas_call | solution.py:143
  163.6 3.2 fusion.77
  168.3 2.6 fusion.31
  175.3 53.8 %feed.1 = (f32[512,1152]{1,0:T(8,128)}, f32[512,1152]{1,0:T(8,128)}, bf16[4,576,1152]{2,1,0:T(8,128)(2,1)}, bf16[4,576,1152]{2,1,0:T(8,128)(2,1)}, bf16[576,4608...) custom-call(s32[1]{0:T(128)} %bitcast.19.core_ref, bf16[512,1152]{1,0:T(8,128)(2,1)} %get-tuple-element.49.x_ref, ...), custom_call_target="tpu_custom_call" | custom-call | flops 32614907904 | bytes 42467328 | tf_op jit(solution)/shard_map/feed/pallas_call | solution.py:348
  229.2 3.0 fusion.59
  233.0 3.3 fusion.120
  245.9 3.8 collective-permute-start.14
  251.6 32.6 %attend_back.1 = (bf16[512,1152]{1,0:T(8,128)(2,1)}, bf16[512,2304]{1,0:T(8,128)(2,1)}, bf16[512,2304]{1,0:T(8,128)(2,1)}) custom-call(s32[1]{0:T(128)} %bitcast.13.long_ref, s32[32]{0:T(128)} %convert_element_type.566.keep_ref, bf16[512,1152]{1,0:T(8,128)(2,1)} %fusion.12.q_ref, bf16[512,2304]{1,0:T(8,128)(2,1)} %fusion.6.own_ref, ...), custom_call_target="tpu_custom_call" | custom-call | flops 6039797760 | bytes 14155776 | tf_op jit(solution)/shard_map/attend_back/pallas_call | solution.py:254
  284.2 2.5 add_convert_fusion.3
  286.8 3.9 collective-permute-start.28
  290.7 4.5 collective-permute-done.16
  295.2 2.2 pad_maximum_fusion.2
  297.5 5.7 collective-permute-done.51
  304.3 7.1 %collective-permute-done.49 = bf16[2,72,1152]{2,1,0:T(8,128)(2,1)S(1)} collective-permute-done((bf16[2,72,1152]{2,1,0:T(8,128)(2,1)S(1)}, bf16[2,72,1152]{2,1,0:T(8,128)(2,1)S(1)}, u32[]{:S(2)}, u32[]{:S(2)}) %collective-permute-start.49) | collective-permute-done | bytes 331808 | tf_op jit(solution)/shard_map/ppermute | solution.py:27
  312.6 4.2 collective-permute-done.52
  317.5 4.6 collective-permute-done.50
  329.4 6.3 collective-permute-start.53
  337.6 6.8 concatenate.124
  364.1 6.2 pick_blocks.6
  371.0 3.1 add_convert_fusion.2
  374.4 9.6 %fusion.58 = (f32[512]{0:T(512)S(1)}, f32[512]{0:T(512)}, f32[512,1152]{1,0:T(8,128)S(1)}) fusion(f32[2,1152]{1,0:T(2,128)S(1)} %copy-done.59, f32[512]{0:T(512)S(1)} %copy-done.84, f32[512]{0:T(512)S(1)} %copy-done.82, f32[2,4,64,1152]{3,2,1,0:T(8,128)S(1)} %copy-done.1, bf16[1152,3456]{1,0:T(8,128)(2,1)} %param.28, ...), kind=kOutput, calls=%fused_computation.98 | convolution fusion | flops 4087479296 | bytes 16237568 | tf_op jit(solution)/shard_map/dot_general | solution.py:20
  386.7 3.2 fusion.33
  399.6 4.5 fusion.48
  408.1 4.2 fusion.9
  414.9 2.5 collective-permute-done.31
  425.6 3.4 collective-permute-done.33
  429.0 2.4 collective-permute-done.34
  439.0 2.4 collective-permute-start.38
  441.4 12.2 %collective-permute-done.20 = bf16[2,64,1152]{2,1,0:T(8,128)(2,1)} collective-permute-done((bf16[2,64,1152]{2,1,0:T(8,128)(2,1)}, bf16[2,64,1152]{2,1,0:T(8,128)(2,1)}, u32[]{:S(2)}, u32[]{:S(2)}) %collective-permute-start.20) | collective-permute-done | bytes 294944 | tf_op jit(solution)/shard_map/ppermute | solution.py:27
  453.6 9.7 %collective-permute-start.40 = (bf16[8,16128]{1,0:T(8,128)(2,1)S(1)}, bf16[8,16128]{1,0:T(8,128)(2,1)}, u32[]{:S(2)}, u32[]{:S(2)}) collective-permute-start(bf16[8,16128]{1,0:T(8,128)(2,1)S(1)} %pad_maximum_fusion.4), channel_id=1, source_target_pairs={{0,3},{1,2},{2,1},{3,0},{4,7},{5,6},{6,5},{7,4},{8,11},{9,10},{10,... | collective-permute-start | bytes 774152 | tf_op jit(solution)/shard_map/ppermute | solution.py:27
  464.7 10.5 %collective-permute-done.39 = bf16[8,16128]{1,0:T(8,128)(2,1)S(1)} collective-permute-done((bf16[8,16128]{1,0:T(8,128)(2,1)S(1)}, bf16[8,16128]{1,0:T(8,128)(2,1)S(1)}, u32[]{:S(2)}, u32[]{:S(2)}) %collective-permute-start.39) | collective-permute-done | bytes 258080 | tf_op jit(solution)/shard_map/ppermute | solution.py:27
  475.9 6.8 concatenate.142
  486.3 2.1 reshape.831
  495.3 2.6 fusion.103
  497.9 6.6 pick_blocks.7
  504.6 5.3 add_convert_fusion
  514.6 5.4 fusion
  523.0 4.5 add_convert_fusion.1
  530.3 13.6 %collective-permute-done.65 = bf16[2,288,1152]{2,1,0:T(8,128)(2,1)} collective-permute-done((bf16[2,288,1152]{2,1,0:T(8,128)(2,1)}, bf16[2,288,1152]{2,1,0:T(8,128)(2,1)}, u32[]{:S(2)}, u32[]{:S(2)}) %collective-permute-start.65) | collective-permute-done | bytes 1327136 | tf_op jit(solution)/shard_map/ppermute | solution.py:27
  549.4 22.8 %collective-permute-done.58 = bf16[2,72,4608]{2,1,0:T(8,128)(2,1)S(1)} collective-permute-done((bf16[2,72,4608]{2,1,0:T(8,128)(2,1)S(1)}, bf16[2,72,4608]{2,1,0:T(8,128)(2,1)S(1)}, u32[]{:S(2)}, u32[]{:S(2)}) %collective-permute-start.58) | collective-permute-done | bytes 1327136 | tf_op jit(solution)/shard_map/ppermute | solution.py:27
  576.5 32.8 %collective-permute-done.66 = bf16[288,1152]{1,0:T(8,128)(2,1)S(1)} collective-permute-done((bf16[288,1152]{1,0:T(8,128)(2,1)S(1)}, bf16[288,1152]{1,0:T(8,128)(2,1)S(1)}, u32[]{:S(2)}, u32[]{:S(2)}) %collective-permute-start.66) | collective-permute-done | bytes 663584 | tf_op jit(solution)/shard_map/ppermute | solution.py:27
  612.3 3.5 collective-permute-start.67
  615.8 6.9 collective-permute-done.59
  623.7 2.2 stack.119
  625.9 2.3 fusion.67
  643.2 6.4 collective-permute-done.45
  651.6 2.7 collective-permute-done.43
  665.4 26.1 %collective-permute-done.61 = bf16[36,4608]{1,0:T(8,128)(2,1)S(1)} collective-permute-done((bf16[36,4608]{1,0:T(8,128)(2,1)S(1)}, bf16[36,4608]{1,0:T(8,128)(2,1)S(1)}, u32[]{:S(2)}, u32[]{:S(2)}) %collective-permute-start.61) | collective-permute-done | bytes 331808 | tf_op jit(solution)/shard_map/ppermute | solution.py:27
  692.6 8.6 %collective-permute-done.68 = bf16[144,1152]{1,0:T(8,128)(2,1)S(1)} collective-permute-done((bf16[144,1152]{1,0:T(8,128)(2,1)S(1)}, bf16[144,1152]{1,0:T(8,128)(2,1)S(1)}, u32[]{:S(2)}, u32[]{:S(2)}) %collective-permute-start.68) | collective-permute-done | bytes 331808 | tf_op jit(solution)/shard_map/ppermute | solution.py:27
  (528 shorter events, 209.4 us)
Async XLA Ops:
  5.0 23.0 %collective-permute-start.1 = (bf16[8,64,1152]{2,1,0:T(8,128)(2,1)}, bf16[8,64,1152]{2,1,0:T(8,128)(2,1)S(1)}, u32[]{:S(2)}, u32[]{:S(2)}) collective-permute-start(bf16[8,64,1152]{2,1,0:T(8,128)(2,1)} %bitcast.425), channel_id=1, source_target_pairs={{0,4},{4,0},{8,12},{12,8},{16,20},{20,16},{24,28},{28,24},{1,5},{5... | collective-permute-start | bytes 3538952 | tf_op jit(solution)/shard_map/ppermute | solution.py:27
  5.0 13.7 %collective-permute-start.5 = (bf16[8,1152]{1,0:T(8,128)(2,1)}, bf16[8,1152]{1,0:T(8,128)(2,1)S(1)}, u32[]{:S(2)}, u32[]{:S(2)}) collective-permute-start(bf16[8,1152]{1,0:T(8,128)(2,1)} %param.22), channel_id=1, source_target_pairs={{0,4},{4,0},{8,12},{12,8},{16,20},{20,16},{24,28},{28,24},{1,5},{5... | collective-permute-start | bytes 55304 | tf_op jit(solution)/shard_map/ppermute | solution.py:27
  5.5 90.8 %collective-permute-start.10 = (bf16[8,64,1152]{2,1,0:T(8,128)(2,1)}, bf16[8,64,1152]{2,1,0:T(8,128)(2,1)}, u32[]{:S(2)}, u32[]{:S(2)}) collective-permute-start(bf16[8,64,1152]{2,1,0:T(8,128)(2,1)} %bitcast.427), channel_id=1, source_target_pairs={{0,4},{4,0},{8,12},{12,8},{16,20},{20,16},{24,28},{28,24},{1,5},{5... | collective-permute-start | bytes 3538952 | tf_op jit(solution)/shard_map/ppermute | solution.py:27
  13.8 62.0 %collective-permute-start.7 = (f32[2,512]{1,0:T(2,128)}, f32[2,512]{1,0:T(2,128)}, u32[]{:S(2)}, u32[]{:S(2)}) collective-permute-start(f32[2,512]{1,0:T(2,128)} %fusion.108), channel_id=1, source_target_pairs={{0,1},{1,0},{2,3},{3,2},{4,5},{5,4},{6,7},{7,6},{8,9},{9,8},{10,11... | collective-permute-start | bytes 12296 | tf_op jit(solution)/shard_map/ppermute | solution.py:27
  36.5 15.1 %collective-permute-start.2 = (bf16[2,1,64,1152]{3,2,0,1:T(8,128)(2,1)S(1)}, bf16[2,1,64,1152]{3,2,0,1:T(8,128)(2,1)S(1)}, u32[]{:S(2)}, u32[]{:S(2)}) collective-permute-start(bf16[2,1,64,1152]{3,2,0,1:T(8,128)(2,1)S(1)} %get-tuple-element.80), channel_id=1, source_target_pairs={{0,1},{1,0},{2,3},{3,2},{4,5},{5,4},{6,7},{7,6},{8,9},{9,8},{10,11... | collective-permute-start | bytes 884744 | tf_op jit(solution)/shard_map/ppermute | solution.py:27
  36.7 23.6 %collective-permute-start.3 = (bf16[2,1,64,1152]{3,2,0,1:T(8,128)(2,1)S(1)}, bf16[2,1,64,1152]{3,2,0,1:T(8,128)(2,1)S(1)}, u32[]{:S(2)}, u32[]{:S(2)}) collective-permute-start(bf16[2,1,64,1152]{3,2,0,1:T(8,128)(2,1)S(1)} %get-tuple-element.79), channel_id=1, source_target_pairs={{0,2},{1,3},{2,0},{3,1},{4,6},{5,7},{6,4},{7,5},{8,10},{9,11},{10,... | collective-permute-start | bytes 884744 | tf_op jit(solution)/shard_map/ppermute | solution.py:27
  39.7 24.5 %collective-permute-start.4 = (bf16[2,1,64,1152]{3,2,0,1:T(8,128)(2,1)S(1)}, bf16[2,1,64,1152]{3,2,0,1:T(8,128)(2,1)S(1)}, u32[]{:S(2)}, u32[]{:S(2)}) collective-permute-start(bf16[2,1,64,1152]{3,2,0,1:T(8,128)(2,1)S(1)} %get-tuple-element.78), channel_id=1, source_target_pairs={{0,3},{1,2},{2,1},{3,0},{4,7},{5,6},{6,5},{7,4},{8,11},{9,10},{10,... | collective-permute-start | bytes 884744 | tf_op jit(solution)/shard_map/ppermute | solution.py:27
  51.6 34.0 %collective-permute-start.8 = (f32[2,512]{1,0:T(2,128)}, f32[2,512]{1,0:T(2,128)}, u32[]{:S(2)}, u32[]{:S(2)}) collective-permute-start(f32[2,512]{1,0:T(2,128)} %fusion.108), channel_id=1, source_target_pairs={{0,2},{1,3},{2,0},{3,1},{4,6},{5,7},{6,4},{7,5},{8,10},{9,11},{10,... | collective-permute-start | bytes 12296 | tf_op jit(solution)/shard_map/ppermute | solution.py:27
  60.3 26.7 %collective-permute-start.9 = (f32[2,512]{1,0:T(2,128)}, f32[2,512]{1,0:T(2,128)}, u32[]{:S(2)}, u32[]{:S(2)}) collective-permute-start(f32[2,512]{1,0:T(2,128)} %fusion.108), channel_id=1, source_target_pairs={{0,3},{1,2},{2,1},{3,0},{4,7},{5,6},{6,5},{7,4},{8,11},{9,10},{10,... | collective-permute-start | bytes 12296 | tf_op jit(solution)/shard_map/ppermute | solution.py:27
  75.2 65.4 %collective-permute-start.6 = (bf16[512,2304]{1,0:T(8,128)(2,1)}, bf16[512,2304]{1,0:T(8,128)(2,1)}, u32[]{:S(2)}, u32[]{:S(2)}) collective-permute-start(bf16[512,2304]{1,0:T(8,128)(2,1)} %fusion.6.own_ref), channel_id=1, source_target_pairs={{0,4},{4,0},{8,12},{12,8},{16,20},{20,16},{24,28},{28,24},{1,5},{5... | collective-permute-start | bytes 7077896 | tf_op jit(solution)/shard_map/ppermute | solution.py:27
  75.8 12.6 %collective-permute-start.23 = (bf16[2,1152]{1,0:T(2,128)(2,1)}, bf16[2,1152]{1,0:T(2,128)(2,1)}, u32[]{:S(2)}, u32[]{:S(2)}) collective-permute-start(bf16[2,1152]{1,0:T(2,128)(2,1)} %fusion.104), channel_id=1, source_target_pairs={{0,4},{4,0},{8,12},{12,8},{16,20},{20,16},{24,28},{28,24},{1,5},{5... | collective-permute-start | bytes 13832 | tf_op jit(solution)/shard_map/ppermute | solution.py:27
  94.7 17.5 %collective-permute-start.25 = (bf16[8,1152]{1,0:T(8,128)(2,1)}, bf16[8,1152]{1,0:T(8,128)(2,1)}, u32[]{:S(2)}, u32[]{:S(2)}) collective-permute-start(bf16[8,1152]{1,0:T(8,128)(2,1)} %pad_maximum_fusion.11), channel_id=1, source_target_pairs={{0,16},{4,20},{8,24},{12,28},{16,0},{20,4},{24,8},{28,12},{1,17},{... | collective-permute-start | bytes 55304 | tf_op jit(solution)/shard_map/ppermute | solution.py:27
  104.6 14.3 %collective-permute-start.11 = (bf16[2,1,64,1152]{3,2,0,1:T(8,128)(2,1)}, bf16[2,1,64,1152]{3,2,0,1:T(8,128)(2,1)}, u32[]{:S(2)}, u32[]{:S(2)}) collective-permute-start(bf16[2,1,64,1152]{3,2,0,1:T(8,128)(2,1)} %get-tuple-element.76), channel_id=1, source_target_pairs={{0,1},{1,0},{2,3},{3,2},{4,5},{5,4},{6,7},{7,6},{8,9},{9,8},{10,11... | collective-permute-start | bytes 884744 | tf_op jit(solution)/shard_map/ppermute | solution.py:27
  106.9 24.6 %collective-permute-start.12 = (bf16[2,1,64,1152]{3,2,0,1:T(8,128)(2,1)}, bf16[2,1,64,1152]{3,2,0,1:T(8,128)(2,1)}, u32[]{:S(2)}, u32[]{:S(2)}) collective-permute-start(bf16[2,1,64,1152]{3,2,0,1:T(8,128)(2,1)} %get-tuple-element.75), channel_id=1, source_target_pairs={{0,2},{1,3},{2,0},{3,1},{4,6},{5,7},{6,4},{7,5},{8,10},{9,11},{10,... | collective-permute-start | bytes 884744 | tf_op jit(solution)/shard_map/ppermute | solution.py:27
  108.7 22.8 %collective-permute-start.13 = (bf16[2,1,64,1152]{3,2,0,1:T(8,128)(2,1)}, bf16[2,1,64,1152]{3,2,0,1:T(8,128)(2,1)}, u32[]{:S(2)}, u32[]{:S(2)}) collective-permute-start(bf16[2,1,64,1152]{3,2,0,1:T(8,128)(2,1)} %get-tuple-element.74), channel_id=1, source_target_pairs={{0,3},{1,2},{2,1},{3,0},{4,7},{5,6},{6,5},{7,4},{8,11},{9,10},{10,... | collective-permute-start | bytes 884744 | tf_op jit(solution)/shard_map/ppermute | solution.py:27
  113.6 215.8 %collective-permute-start.26 = (bf16[16,1152]{1,0:T(8,128)(2,1)}, bf16[16,1152]{1,0:T(8,128)(2,1)}, u32[]{:S(2)}, u32[]{:S(2)}) collective-permute-start(bf16[16,1152]{1,0:T(8,128)(2,1)} %pad_maximum_fusion.9), channel_id=1, source_target_pairs={{0,1},{1,0},{2,3},{3,2},{4,5},{5,4},{6,7},{7,6},{8,9},{9,8},{10,11... | collective-permute-start | bytes 110600 | tf_op jit(solution)/shard_map/ppermute | solution.py:27
  118.9 218.8 %collective-permute-start.27 = (bf16[16,1152]{1,0:T(8,128)(2,1)}, bf16[16,1152]{1,0:T(8,128)(2,1)}, u32[]{:S(2)}, u32[]{:S(2)}) collective-permute-start(bf16[16,1152]{1,0:T(8,128)(2,1)} %pad_maximum_fusion.9), channel_id=1, source_target_pairs={{0,2},{1,3},{2,0},{3,1},{4,6},{5,7},{6,4},{7,5},{8,10},{9,11},{10,... | collective-permute-start | bytes 110600 | tf_op jit(solution)/shard_map/ppermute | solution.py:27
  238.4 45.8 %collective-permute-start.48 = (bf16[4,144,1152]{2,1,0:T(8,128)(2,1)}, bf16[4,144,1152]{2,1,0:T(8,128)(2,1)}, u32[]{:S(2)}, u32[]{:S(2)}) collective-permute-start(bf16[4,144,1152]{2,1,0:T(8,128)(2,1)} %fusion.69), channel_id=1, source_target_pairs={{0,4},{4,0},{8,12},{12,8},{16,20},{20,16},{24,28},{28,24},{1,5},{5... | collective-permute-start | bytes 3981320 | tf_op jit(solution)/shard_map/ppermute | solution.py:27
  245.9 40.9 %collective-permute-start.14 = (bf16[2,64,1152]{2,1,0:T(8,128)(2,1)}, bf16[2,64,1152]{2,1,0:T(8,128)(2,1)}, u32[]{:S(2)}, u32[]{:S(2)}) collective-permute-start(bf16[2,64,1152]{2,1,0:T(8,128)(2,1)} %get-tuple-element.70), channel_id=1, source_target_pairs={{0,1},{1,0},{2,3},{3,2},{4,5},{5,4},{6,7},{7,6},{8,9},{9,8},{10,11... | collective-permute-start | bytes 884744 | tf_op jit(solution)/shard_map/ppermute | solution.py:27
  249.7 41.0 %collective-permute-start.15 = (bf16[2,64,1152]{2,1,0:T(8,128)(2,1)}, bf16[2,64,1152]{2,1,0:T(8,128)(2,1)}, u32[]{:S(2)}, u32[]{:S(2)}) collective-permute-start(bf16[2,64,1152]{2,1,0:T(8,128)(2,1)} %get-tuple-element.69), channel_id=1, source_target_pairs={{0,2},{1,3},{2,0},{3,1},{4,6},{5,7},{6,4},{7,5},{8,10},{9,11},{10,... | collective-permute-start | bytes 884744 | tf_op jit(solution)/shard_map/ppermute | solution.py:27
  284.2 11.0 %collective-permute-start.16 = (bf16[2,64,1152]{2,1,0:T(8,128)(2,1)}, bf16[2,64,1152]{2,1,0:T(8,128)(2,1)S(1)}, u32[]{:S(2)}, u32[]{:S(2)}) collective-permute-start(bf16[2,64,1152]{2,1,0:T(8,128)(2,1)} %get-tuple-element.68), channel_id=1, source_target_pairs={{0,3},{1,2},{2,1},{3,0},{4,7},{5,6},{6,5},{7,4},{8,11},{9,10},{10,... | collective-permute-start | bytes 884744 | tf_op jit(solution)/shard_map/ppermute | solution.py:27
  286.8 50.8 %collective-permute-start.28 = (bf16[16,1152]{1,0:T(8,128)(2,1)}, bf16[16,1152]{1,0:T(8,128)(2,1)}, u32[]{:S(2)}, u32[]{:S(2)}) collective-permute-start(bf16[16,1152]{1,0:T(8,128)(2,1)} %pad_maximum_fusion.9), channel_id=1, source_target_pairs={{0,3},{1,2},{2,1},{3,0},{4,7},{5,6},{6,5},{7,4},{8,11},{9,10},{10,... | collective-permute-start | bytes 110600 | tf_op jit(solution)/shard_map/ppermute | solution.py:27
  290.7 80.3 %collective-permute-start.18 = (bf16[512,2304]{1,0:T(8,128)(2,1)}, bf16[512,2304]{1,0:T(8,128)(2,1)}, u32[]{:S(2)}, u32[]{:S(2)}) collective-permute-start(bf16[512,2304]{1,0:T(8,128)(2,1)} %get-tuple-element.31), channel_id=1, source_target_pairs={{0,4},{4,0},{8,12},{12,8},{16,20},{20,16},{24,28},{28,24},{1,5},{5... | collective-permute-start | bytes 7077896 | tf_op jit(solution)/shard_map/ppermute | solution.py:27
  295.2 8.0 %collective-permute-start.51 = (bf16[2,72,1152]{2,1,0:T(8,128)(2,1)S(1)}, bf16[2,72,1152]{2,1,0:T(8,128)(2,1)S(1)}, u32[]{:S(2)}, u32[]{:S(2)}) collective-permute-start(bf16[2,72,1152]{2,1,0:T(8,128)(2,1)S(1)} %dynamic-slice_bitcast_fusion.14), channel_id=1, source_target_pairs={{0,16},{4,20},{8,24},{12,28},{16,0},{20,4},{24,8},{28,12},{1,17},{... | collective-permute-start | bytes 995336 | tf_op jit(solution)/shard_map/ppermute | solution.py:27
  303.2 8.3 %collective-permute-start.49 = (bf16[2,72,1152]{2,1,0:T(8,128)(2,1)S(1)}, bf16[2,72,1152]{2,1,0:T(8,128)(2,1)S(1)}, u32[]{:S(2)}, u32[]{:S(2)}) collective-permute-start(bf16[2,72,1152]{2,1,0:T(8,128)(2,1)S(1)} %dynamic-slice_bitcast_fusion.15), channel_id=1, source_target_pairs={{0,8},{4,12},{8,0},{12,4},{16,24},{20,28},{24,16},{28,20},{1,9},{5... | collective-permute-start | bytes 995336 | tf_op jit(solution)/shard_map/ppermute | solution.py:27
  311.4 5.3 collective-permute-start.52
  322.1 42.0 %collective-permute-start.17 = (bf16[8,64,1152]{2,1,0:T(8,128)(2,1)}, bf16[8,64,1152]{2,1,0:T(8,128)(2,1)}, u32[]{:S(2)}, u32[]{:S(2)}) collective-permute-start(bf16[8,64,1152]{2,1,0:T(8,128)(2,1)} %bitcast.43.own_ref), channel_id=1, source_target_pairs={{0,4},{4,0},{8,12},{12,8},{16,20},{20,16},{24,28},{28,24},{1,5},{5... | collective-permute-start | bytes 3538952 | tf_op jit(solution)/shard_map/ppermute | solution.py:27
  329.4 32.2 %collective-permute-start.53 = (bf16[2,36,1152]{2,1,0:T(8,128)(2,1)}, bf16[2,36,1152]{2,1,0:T(8,128)(2,1)}, u32[]{:S(2)}, u32[]{:S(2)}) collective-permute-start(bf16[2,36,1152]{2,1,0:T(8,128)(2,1)} %dynamic-slice_bitcast_fusion.17), channel_id=1, source_target_pairs={{0,1},{1,0},{2,3},{3,2},{4,5},{5,4},{6,7},{7,6},{8,9},{9,8},{10,11... | collective-permute-start | bytes 497672 | tf_op jit(solution)/shard_map/ppermute | solution.py:27
  357.9 146.6 %collective-permute-start.62 = (bf16[4,576,1152]{2,1,0:T(8,128)(2,1)}, bf16[4,576,1152]{2,1,0:T(8,128)(2,1)}, u32[]{:S(2)}, u32[]{:S(2)}) collective-permute-start(bf16[4,576,1152]{2,1,0:T(8,128)(2,1)} %get-tuple-element.36), channel_id=1, source_target_pairs={{0,4},{4,0},{8,12},{12,8},{16,20},{20,16},{24,28},{28,24},{1,5},{5... | collective-permute-start | bytes 15925256 | tf_op jit(solution)/shard_map/ppermute | solution.py:27
  358.2 156.4 %collective-permute-start.55 = (bf16[4,144,4608]{2,1,0:T(8,128)(2,1)}, bf16[4,144,4608]{2,1,0:T(8,128)(2,1)}, u32[]{:S(2)}, u32[]{:S(2)}) collective-permute-start(bf16[4,144,4608]{2,1,0:T(8,128)(2,1)} %bitcast.439), channel_id=1, source_target_pairs={{0,4},{4,0},{8,12},{12,8},{16,20},{20,16},{24,28},{28,24},{1,5},{5... | collective-permute-start | bytes 15925256 | tf_op jit(solution)/shard_map/ppermute | solution.py:27
  362.7 7.6 %collective-permute-start.54 = (bf16[36,1152]{1,0:T(8,128)(2,1)S(1)}, bf16[36,1152]{1,0:T(8,128)(2,1)S(1)}, u32[]{:S(2)}, u32[]{:S(2)}) collective-permute-start(bf16[36,1152]{1,0:T(8,128)(2,1)S(1)} %dynamic-slice_bitcast_fusion.20), channel_id=1, source_target_pairs={{0,2},{1,3},{2,0},{3,1},{4,6},{5,7},{6,4},{7,5},{8,10},{9,11},{10,... | collective-permute-start | bytes 248840 | tf_op jit(solution)/shard_map/ppermute | solution.py:27
  391.2 22.3 %collective-permute-start.35 = (bf16[1,16128]{1,0:T(2,128)(2,1)}, bf16[1,16128]{1,0:T(2,128)(2,1)}, u32[]{:S(2)}, u32[]{:S(2)}) collective-permute-start(bf16[1,16128]{1,0:T(2,128)(2,1)} %reshape_dynamic-update-slice_fusion), channel_id=1, source_target_pairs={{0,4},{4,0},{8,12},{12,8},{16,20},{20,16},{24,28},{28,24},{1,5},{5... | collective-permute-start | bytes 96776 | tf_op jit(solution)/shard_map/ppermute | solution.py:27
  392.6 12.5 %collective-permute-start.29 = (bf16[1,6912]{1,0:T(2,128)(2,1)}, bf16[1,6912]{1,0:T(2,128)(2,1)}, u32[]{:S(2)}, u32[]{:S(2)}) collective-permute-start(bf16[1,6912]{1,0:T(2,128)(2,1)} %constant_dynamic-update-slice_fusion), channel_id=1, source_target_pairs={{0,4},{4,0},{8,12},{12,8},{16,20},{20,16},{24,28},{28,24},{1,5},{5... | collective-permute-start | bytes 41480 | tf_op jit(solution)/shard_map/ppermute | solution.py:27
  406.0 6.3 collective-permute-start.30
  414.6 6.7 collective-permute-start.36
  418.3 6.2 collective-permute-start.32
  419.7 9.3 %collective-permute-start.33 = (bf16[8,6912]{1,0:T(8,128)(2,1)S(1)}, bf16[8,6912]{1,0:T(8,128)(2,1)S(1)}, u32[]{:S(2)}, u32[]{:S(2)}) collective-permute-start(bf16[8,6912]{1,0:T(8,128)(2,1)S(1)} %pad_maximum_fusion.6), channel_id=1, source_target_pairs={{0,2},{1,3},{2,0},{3,1},{4,6},{5,7},{6,4},{7,5},{8,10},{9,11},{10,... | collective-permute-start | bytes 331784 | tf_op jit(solution)/shard_map/ppermute | solution.py:27
  421.3 10.1 %collective-permute-start.34 = (bf16[8,6912]{1,0:T(8,128)(2,1)S(1)}, bf16[8,6912]{1,0:T(8,128)(2,1)S(1)}, u32[]{:S(2)}, u32[]{:S(2)}) collective-permute-start(bf16[8,6912]{1,0:T(8,128)(2,1)S(1)} %pad_maximum_fusion.6), channel_id=1, source_target_pairs={{0,3},{1,2},{2,1},{3,0},{4,7},{5,6},{6,5},{7,4},{8,11},{9,10},{10,... | collective-permute-start | bytes 331784 | tf_op jit(solution)/shard_map/ppermute | solution.py:27
  424.5 14.5 %collective-permute-start.19 = (bf16[2,64,1152]{2,1,0:T(8,128)(2,1)}, bf16[2,64,1152]{2,1,0:T(8,128)(2,1)}, u32[]{:S(2)}, u32[]{:S(2)}) collective-permute-start(bf16[2,64,1152]{2,1,0:T(8,128)(2,1)} %get-tuple-element.66), channel_id=1, source_target_pairs={{0,1},{1,0},{2,3},{3,2},{4,5},{5,4},{6,7},{7,6},{8,9},{9,8},{10,11... | collective-permute-start | bytes 884744 | tf_op jit(solution)/shard_map/ppermute | solution.py:27
  429.0 24.6 %collective-permute-start.20 = (bf16[2,64,1152]{2,1,0:T(8,128)(2,1)}, bf16[2,64,1152]{2,1,0:T(8,128)(2,1)}, u32[]{:S(2)}, u32[]{:S(2)}) collective-permute-start(bf16[2,64,1152]{2,1,0:T(8,128)(2,1)} %get-tuple-element.65), channel_id=1, source_target_pairs={{0,2},{1,3},{2,0},{3,1},{4,6},{5,7},{6,4},{7,5},{8,10},{9,11},{10,... | collective-permute-start | bytes 884744 | tf_op jit(solution)/shard_map/ppermute | solution.py:27
  436.6 16.9 %collective-permute-start.21 = (bf16[2,64,1152]{2,1,0:T(8,128)(2,1)}, bf16[2,64,1152]{2,1,0:T(8,128)(2,1)S(1)}, u32[]{:S(2)}, u32[]{:S(2)}) collective-permute-start(bf16[2,64,1152]{2,1,0:T(8,128)(2,1)} %get-tuple-element.64), channel_id=1, source_target_pairs={{0,3},{1,2},{2,1},{3,0},{4,7},{5,6},{6,5},{7,4},{8,11},{9,10},{10,... | collective-permute-start | bytes 884744 | tf_op jit(solution)/shard_map/ppermute | solution.py:27
  439.0 25.6 %collective-permute-start.38 = (bf16[8,16128]{1,0:T(8,128)(2,1)S(1)}, bf16[8,16128]{1,0:T(8,128)(2,1)S(1)}, u32[]{:S(2)}, u32[]{:S(2)}) collective-permute-start(bf16[8,16128]{1,0:T(8,128)(2,1)S(1)} %pad_maximum_fusion.4), channel_id=1, source_target_pairs={{0,1},{1,0},{2,3},{3,2},{4,5},{5,4},{6,7},{7,6},{8,9},{9,8},{10,11... | collective-permute-start | bytes 774152 | tf_op jit(solution)/shard_map/ppermute | solution.py:27
  453.6 21.6 %collective-permute-start.39 = (bf16[8,16128]{1,0:T(8,128)(2,1)S(1)}, bf16[8,16128]{1,0:T(8,128)(2,1)S(1)}, u32[]{:S(2)}, u32[]{:S(2)}) collective-permute-start(bf16[8,16128]{1,0:T(8,128)(2,1)S(1)} %pad_maximum_fusion.4), channel_id=1, source_target_pairs={{0,2},{1,3},{2,0},{3,1},{4,6},{5,7},{6,4},{7,5},{8,10},{9,11},{10,... | collective-permute-start | bytes 774152 | tf_op jit(solution)/shard_map/ppermute | solution.py:27
  453.6 22.3 %collective-permute-start.40 = (bf16[8,16128]{1,0:T(8,128)(2,1)S(1)}, bf16[8,16128]{1,0:T(8,128)(2,1)}, u32[]{:S(2)}, u32[]{:S(2)}) collective-permute-start(bf16[8,16128]{1,0:T(8,128)(2,1)S(1)} %pad_maximum_fusion.4), channel_id=1, source_target_pairs={{0,3},{1,2},{2,1},{3,0},{4,7},{5,6},{6,5},{7,4},{8,11},{9,10},{10,... | collective-permute-start | bytes 774152 | tf_op jit(solution)/shard_map/ppermute | solution.py:27
  464.6 58.3 %collective-permute-start.41 = (bf16[4,144,3456]{2,1,0:T(8,128)(2,1)}, bf16[4,144,3456]{2,1,0:T(8,128)(2,1)}, u32[]{:S(2)}, u32[]{:S(2)}) collective-permute-start(bf16[4,144,3456]{2,1,0:T(8,128)(2,1)} %fusion.9), channel_id=1, source_target_pairs={{0,4},{4,0},{8,12},{12,8},{16,20},{20,16},{24,28},{28,24},{1,5},{5... | collective-permute-start | bytes 11943944 | tf_op jit(solution)/shard_map/ppermute | solution.py:27
  475.9 22.0 %collective-permute-start.22 = (bf16[8,64,1152]{2,1,0:T(8,128)(2,1)S(1)}, bf16[8,64,1152]{2,1,0:T(8,128)(2,1)}, u32[]{:S(2)}, u32[]{:S(2)}) collective-permute-start(bf16[8,64,1152]{2,1,0:T(8,128)(2,1)S(1)} %bitcast.410), channel_id=1, source_target_pairs={{0,4},{4,0},{8,12},{12,8},{16,20},{20,16},{24,28},{28,24},{1,5},{5... | collective-permute-start | bytes 3538952 | tf_op jit(solution)/shard_map/ppermute | solution.py:27
  511.6 32.2 %collective-permute-start.65 = (bf16[2,288,1152]{2,1,0:T(8,128)(2,1)}, bf16[2,288,1152]{2,1,0:T(8,128)(2,1)}, u32[]{:S(2)}, u32[]{:S(2)}) collective-permute-start(bf16[2,288,1152]{2,1,0:T(8,128)(2,1)} %dynamic-slice_bitcast_fusion), channel_id=1, source_target_pairs={{0,16},{4,20},{8,24},{12,28},{16,0},{20,4},{24,8},{28,12},{1,17},{... | collective-permute-start | bytes 3981320 | tf_op jit(solution)/shard_map/ppermute | solution.py:27
  513.1 33.1 %collective-permute-start.63 = (bf16[2,288,1152]{2,1,0:T(8,128)(2,1)}, bf16[2,288,1152]{2,1,0:T(8,128)(2,1)}, u32[]{:S(2)}, u32[]{:S(2)}) collective-permute-start(bf16[2,288,1152]{2,1,0:T(8,128)(2,1)} %dynamic-slice_bitcast_fusion.1), channel_id=1, source_target_pairs={{0,8},{4,12},{8,0},{12,4},{16,24},{20,28},{24,16},{28,20},{1,9},{5... | collective-permute-start | bytes 3981320 | tf_op jit(solution)/shard_map/ppermute | solution.py:27
  520.5 51.7 %collective-permute-start.58 = (bf16[2,72,4608]{2,1,0:T(8,128)(2,1)S(1)}, bf16[2,72,4608]{2,1,0:T(8,128)(2,1)S(1)}, u32[]{:S(2)}, u32[]{:S(2)}) collective-permute-start(bf16[2,72,4608]{2,1,0:T(8,128)(2,1)S(1)} %dynamic-slice_bitcast_fusion.2), channel_id=1, source_target_pairs={{0,16},{4,20},{8,24},{12,28},{16,0},{20,4},{24,8},{28,12},{1,17},{... | collective-permute-start | bytes 3981320 | tf_op jit(solution)/shard_map/ppermute | solution.py:27
  521.5 52.2 %collective-permute-start.56 = (bf16[2,72,4608]{2,1,0:T(8,128)(2,1)S(1)}, bf16[2,72,4608]{2,1,0:T(8,128)(2,1)S(1)}, u32[]{:S(2)}, u32[]{:S(2)}) collective-permute-start(bf16[2,72,4608]{2,1,0:T(8,128)(2,1)S(1)} %dynamic-slice_bitcast_fusion.3), channel_id=1, source_target_pairs={{0,8},{4,12},{8,0},{12,4},{16,24},{20,28},{24,16},{28,20},{1,9},{5... | collective-permute-start | bytes 3981320 | tf_op jit(solution)/shard_map/ppermute | solution.py:27
  528.9 107.5 %collective-permute-start.44 = (bf16[2,72,3456]{2,1,0:T(8,128)(2,1)}, bf16[2,72,3456]{2,1,0:T(8,128)(2,1)}, u32[]{:S(2)}, u32[]{:S(2)}) collective-permute-start(bf16[2,72,3456]{2,1,0:T(8,128)(2,1)} %dynamic-slice_bitcast_fusion.4), channel_id=1, source_target_pairs={{0,16},{4,20},{8,24},{12,28},{16,0},{20,4},{24,8},{28,12},{1,17},{... | collective-permute-start | bytes 2985992 | tf_op jit(solution)/shard_map/ppermute | solution.py:27
  543.9 95.2 %collective-permute-start.42 = (bf16[2,72,3456]{2,1,0:T(8,128)(2,1)}, bf16[2,72,3456]{2,1,0:T(8,128)(2,1)}, u32[]{:S(2)}, u32[]{:S(2)}) collective-permute-start(bf16[2,72,3456]{2,1,0:T(8,128)(2,1)} %dynamic-slice_bitcast_fusion.5), channel_id=1, source_target_pairs={{0,8},{4,12},{8,0},{12,4},{16,24},{20,28},{24,16},{28,20},{1,9},{5... | collective-permute-start | bytes 2985992 | tf_op jit(solution)/shard_map/ppermute | solution.py:27
  546.2 63.1 %collective-permute-start.66 = (bf16[288,1152]{1,0:T(8,128)(2,1)S(1)}, bf16[288,1152]{1,0:T(8,128)(2,1)S(1)}, u32[]{:S(2)}, u32[]{:S(2)}) collective-permute-start(bf16[288,1152]{1,0:T(8,128)(2,1)S(1)} %dynamic-slice_bitcast_fusion.6), channel_id=1, source_target_pairs={{0,8},{4,12},{8,0},{12,4},{16,24},{20,28},{24,16},{28,20},{1,9},{5... | collective-permute-start | bytes 1990664 | tf_op jit(solution)/shard_map/ppermute | solution.py:27
  572.2 39.0 %collective-permute-start.64 = (bf16[288,1152]{1,0:T(8,128)(2,1)S(1)}, bf16[288,1152]{1,0:T(8,128)(2,1)S(1)}, u32[]{:S(2)}, u32[]{:S(2)}) collective-permute-start(bf16[288,1152]{1,0:T(8,128)(2,1)S(1)} %dynamic-slice_bitcast_fusion.7), channel_id=1, source_target_pairs={{0,16},{4,20},{8,24},{12,28},{16,0},{20,4},{24,8},{28,12},{1,17},{... | collective-permute-start | bytes 1990664 | tf_op jit(solution)/shard_map/ppermute | solution.py:27
  573.7 49.0 %collective-permute-start.59 = (bf16[72,4608]{1,0:T(8,128)(2,1)S(1)}, bf16[72,4608]{1,0:T(8,128)(2,1)S(1)}, u32[]{:S(2)}, u32[]{:S(2)}) collective-permute-start(bf16[72,4608]{1,0:T(8,128)(2,1)S(1)} %dynamic-slice_bitcast_fusion.8), channel_id=1, source_target_pairs={{0,8},{4,12},{8,0},{12,4},{16,24},{20,28},{24,16},{28,20},{1,9},{5... | collective-permute-start | bytes 1990664 | tf_op jit(solution)/shard_map/ppermute | solution.py:27
  609.3 16.6 %collective-permute-start.57 = (bf16[72,4608]{1,0:T(8,128)(2,1)}, bf16[72,4608]{1,0:T(8,128)(2,1)}, u32[]{:S(2)}, u32[]{:S(2)}) collective-permute-start(bf16[72,4608]{1,0:T(8,128)(2,1)} %dynamic-slice_bitcast_fusion.9), channel_id=1, source_target_pairs={{0,16},{4,20},{8,24},{12,28},{16,0},{20,4},{24,8},{28,12},{1,17},{... | collective-permute-start | bytes 1990664 | tf_op jit(solution)/shard_map/ppermute | solution.py:27
  612.3 50.5 %collective-permute-start.67 = (bf16[2,144,1152]{2,1,0:T(8,128)(2,1)}, bf16[2,144,1152]{2,1,0:T(8,128)(2,1)}, u32[]{:S(2)}, u32[]{:S(2)}) collective-permute-start(bf16[2,144,1152]{2,1,0:T(8,128)(2,1)} %fusion.79), channel_id=1, source_target_pairs={{0,1},{1,0},{2,3},{3,2},{4,5},{5,4},{6,7},{7,6},{8,9},{9,8},{10,11... | collective-permute-start | bytes 1990664 | tf_op jit(solution)/shard_map/ppermute | solution.py:27
  635.3 24.5 %collective-permute-start.60 = (bf16[2,36,4608]{2,0,1:T(2,128)(2,1)}, bf16[2,36,4608]{2,0,1:T(2,128)(2,1)}, u32[]{:S(2)}, u32[]{:S(2)}) collective-permute-start(bf16[2,36,4608]{2,0,1:T(2,128)(2,1)} %bitcast.383), channel_id=1, source_target_pairs={{0,1},{1,0},{2,3},{3,2},{4,5},{5,4},{6,7},{7,6},{8,9},{9,8},{10,11... | collective-permute-start | bytes 1990664 | tf_op jit(solution)/shard_map/ppermute | solution.py:27
  637.9 11.6 %collective-permute-start.45 = (bf16[72,3456]{1,0:T(8,128)(2,1)S(1)}, bf16[72,3456]{1,0:T(8,128)(2,1)S(1)}, u32[]{:S(2)}, u32[]{:S(2)}) collective-permute-start(bf16[72,3456]{1,0:T(8,128)(2,1)S(1)} %dynamic-slice_bitcast_fusion.10), channel_id=1, source_target_pairs={{0,8},{4,12},{8,0},{12,4},{16,24},{20,28},{24,16},{28,20},{1,9},{5... | collective-permute-start | bytes 1493000 | tf_op jit(solution)/shard_map/ppermute | solution.py:27
  642.3 12.0 %collective-permute-start.43 = (bf16[72,3456]{1,0:T(8,128)(2,1)}, bf16[72,3456]{1,0:T(8,128)(2,1)}, u32[]{:S(2)}, u32[]{:S(2)}) collective-permute-start(bf16[72,3456]{1,0:T(8,128)(2,1)} %dynamic-slice_bitcast_fusion.11), channel_id=1, source_target_pairs={{0,16},{4,20},{8,24},{12,28},{16,0},{20,4},{24,8},{28,12},{1,17},{... | collective-permute-start | bytes 1493000 | tf_op jit(solution)/shard_map/ppermute | solution.py:27
  658.0 34.5 %collective-permute-start.46 = (bf16[2,36,3456]{2,0,1:T(2,128)(2,1)S(1)}, bf16[2,36,3456]{2,0,1:T(2,128)(2,1)S(1)}, u32[]{:S(2)}, u32[]{:S(2)}) collective-permute-start(bf16[2,36,3456]{2,0,1:T(2,128)(2,1)S(1)} %bitcast.432), channel_id=1, source_target_pairs={{0,1},{1,0},{2,3},{3,2},{4,5},{5,4},{6,7},{7,6},{8,9},{9,8},{10,11... | collective-permute-start | bytes 1493000 | tf_op jit(solution)/shard_map/ppermute | solution.py:27
  661.0 30.5 %collective-permute-start.61 = (bf16[36,4608]{1,0:T(8,128)(2,1)S(1)}, bf16[36,4608]{1,0:T(8,128)(2,1)S(1)}, u32[]{:S(2)}, u32[]{:S(2)}) collective-permute-start(bf16[36,4608]{1,0:T(8,128)(2,1)S(1)} %dynamic-slice_bitcast_fusion.12), channel_id=1, source_target_pairs={{0,2},{1,3},{2,0},{3,1},{4,6},{5,7},{6,4},{7,5},{8,10},{9,11},{10,... | collective-permute-start | bytes 995336 | tf_op jit(solution)/shard_map/ppermute | solution.py:27
  664.1 37.1 %collective-permute-start.68 = (bf16[144,1152]{1,0:T(8,128)(2,1)S(1)}, bf16[144,1152]{1,0:T(8,128)(2,1)S(1)}, u32[]{:S(2)}, u32[]{:S(2)}) collective-permute-start(bf16[144,1152]{1,0:T(8,128)(2,1)S(1)} %dynamic-slice_bitcast_fusion.13), channel_id=1, source_target_pairs={{0,2},{1,3},{2,0},{3,1},{4,6},{5,7},{6,4},{7,5},{8,10},{9,11},{10,... | collective-permute-start | bytes 995336 | tf_op jit(solution)/shard_map/ppermute | solution.py:27
  692.6 11.6 %collective-permute-start.47 = (bf16[36,3456]{1,0:T(8,128)(2,1)S(1)}, bf16[36,3456]{1,0:T(8,128)(2,1)S(1)}, u32[]{:S(2)}, u32[]{:S(2)}) collective-permute-start(bf16[36,3456]{1,0:T(8,128)(2,1)S(1)} %dynamic-slice_bitcast_fusion.16), channel_id=1, source_target_pairs={{0,2},{1,3},{2,0},{3,1},{4,6},{5,7},{6,4},{7,5},{8,10},{9,11},{10,... | collective-permute-start | bytes 746504 | tf_op jit(solution)/shard_map/ppermute | solution.py:27
  (108 other events, 915.6 us)

commit v2 on v1

v2 whole, which is shorter than its diff:
```python
import functools

import jax
import jax.numpy as jnp
from jax import lax
from jax.experimental import pallas as pl
from jax.experimental.pallas import tpu as pltpu
from jax.sharding import PartitionSpec as P

EPSILON = 1e-06
LOG2E = 1.4426950408889634
LANES = 128
NOTES = 16
FEED_VMEM = 60
FEED_SUB = 768
GELU_A = 0.7978845608028654
GELU_B = 0.044715
F32 = jnp.float32
BF16 = jnp.bfloat16


def contract(left, right, left_dim, right_dim, out=F32):
    return lax.dot_general(
        left, right, (((left_dim,), (right_dim,)), ((), ())), preferred_element_type=out
    )


def swap(array, axis, bit):
    size = lax.axis_size(axis)
    return lax.ppermute(array, axis, [(i, i ^ bit) for i in range(size)])


def launch(
    body, out_shape, *, in_specs, out_specs, name, after=(), grid=(), prefetch=0, scratch=(),
    aliases=None, vmem=56, micros=1,
):
    lead = prefetch + len(in_specs)
    waits, outs = len(after), len(out_shape)

    def kernel(*refs):
        rest = refs[lead + waits :]
        body(*refs[:lead], *rest[:outs], *rest[outs + 1 :])
        rest[outs][...] = jnp.zeros(rest[outs].shape, F32)

    token = (8, LANES)
    specs = dict(
        in_specs=list(in_specs) + [pl.BlockSpec(memory_space=pl.ANY)] * waits,
        scratch_shapes=list(scratch),
    )
    if grid:
        specs = dict(
            grid_spec=pltpu.PrefetchScalarGridSpec(
                num_scalar_prefetch=prefetch,
                grid=grid,
                out_specs=list(out_specs) + [pl.BlockSpec(token, lambda *i: (0, 0))],
                **specs,
            )
        )
    else:
        specs["out_specs"] = list(out_specs) + [pl.BlockSpec(memory_space=pltpu.VMEM)]
    call = pl.pallas_call(
        kernel,
        out_shape=list(out_shape) + [jax.ShapeDtypeStruct(token, F32)],
        input_output_aliases=aliases or {},
        compiler_params=pltpu.CompilerParams(vmem_limit_bytes=vmem * 1024 * 1024),
        cost_estimate=pl.CostEstimate(
            flops=int(micros * 1000000000), bytes_accessed=0, transcendentals=0
        ),
        name=name,
        **specs,
    )

    def run(*operands):
        *results, mark = call(*operands, *after)
        return results, mark

    return run


def vmem_specs(count):
    return [pl.BlockSpec(memory_space=pltpu.VMEM)] * count


def smem_specs(count):
    return [pl.BlockSpec(memory_space=pltpu.SMEM)] * count


def like(dtype, *shape):
    return jax.ShapeDtypeStruct(shape, dtype)


def plan_kernel(
    slots, piece, chips, blocks, place_ref, seg_own, seg_other, bucket_own, bucket_other,
    head_mask, channel_mask, send_which, send_index, back_which, back_index, cond_which,
    cond_row, flags, keep_heads, keep_channels, order_ref, rank_ref, id_ref, long_ref,
):
    core = place_ref[0]
    seq = place_ref[1]
    total = 2 * slots
    ids, keys = [], []
    for i in range(total):
        at = (i % slots) * piece
        ids.append(jnp.where(core == i // slots, seg_own[at], seg_other[at]))
    for i in range(total):
        base = (i // slots) * slots
        equal = jnp.int32(0)
        for j in range(slots):
            equal += jnp.where(ids[base + j] == ids[i], 1, 0)
        is_long = jnp.where(equal > 1, 1, 0)
        id_ref[i] = ids[i]
        long_ref[i] = is_long
        keys.append(jnp.where(is_long == 1, i, total + i))
    for i in range(total):
        rank = jnp.int32(0)
        for j in range(total):
            rank += jnp.where(keys[j] < keys[i], 1, 0)
        rank_ref[i] = rank
        order_ref[rank] = jnp.int32(i)
    for k in range(chips):
        for s in range(blocks):
            item = order_ref[((seq ^ k) * 2 + core) * blocks + s]
            send_which[k * blocks + s] = jnp.where(item // slots == core, 0, 1)
            send_index[k * blocks + s] = item % slots
    for j in range(slots):
        rank = rank_ref[core * slots + j]
        back_which[j] = jnp.where((rank // blocks) % 2 == core, 0, 1)
        back_index[j] = ((rank // (2 * blocks)) ^ seq) * blocks + rank % blocks
    flags[0] = long_ref[order_ref[seq * 2 * blocks]]
    flags[1] = core
    heads = head_mask.shape[1]
    groups = channel_mask.shape[1]
    for s in range(blocks):
        item = order_ref[(seq * 2 + core) * blocks + s]
        other = jnp.where(item // slots == core, 0, 1)
        cond_which[s] = other
        cond_row[s] = id_ref[item]
        step = jnp.where(other == 0, bucket_own[0], bucket_other[0])
        for h in range(heads):
            keep_heads[s * heads + h] = head_mask[step, h]
        for f in range(groups):
            keep_channels[s * groups + f] = channel_mask[step, f]


def make_plan(place, segment, seg_other, bucket, bucket_other, head_mask, channel_mask, slots, piece,
              chips, blocks):
    smem = pl.BlockSpec(memory_space=pltpu.SMEM)
    sizes = [chips * blocks] * 2 + [slots] * 2 + [blocks] * 2 + [2]
    sizes += [blocks * head_mask.shape[1], blocks * channel_mask.shape[1]]
    return pl.pallas_call(
        functools.partial(plan_kernel, slots, piece, chips, blocks),
        in_specs=[smem] * 7,
        out_specs=[smem] * 9,
        out_shape=[jax.ShapeDtypeStruct((n,), jnp.int32) for n in sizes],
        scratch_shapes=[pltpu.SMEM((2 * slots,), jnp.int32)] * 4,
        cost_estimate=pl.CostEstimate(flops=0, bytes_accessed=8000000, transcendentals=0),
        name="make_plan",
    )(place, segment, seg_other, bucket, bucket_other, head_mask, channel_mask)


def send_kernel(blocks, which_ref, index_ref, own_ref, other_ref, *outs):
    for m in range(len(outs) * blocks):

        @pl.when(which_ref[m] == 0)
        def _():
            outs[m // blocks][m % blocks] = own_ref[index_ref[m]]

        @pl.when(which_ref[m] != 0)
        def _():
            outs[m // blocks][m % blocks] = other_ref[index_ref[m]]


def send_blocks(own, other, which, index, chips, blocks, after=()):
    _, rows, width = own.shape
    return launch(
        functools.partial(send_kernel, blocks),
        [like(own.dtype, blocks, rows, width)] * chips,
        in_specs=smem_specs(2) + vmem_specs(2),
        out_specs=vmem_specs(chips),
        after=after,
        vmem=16,
        name="send_blocks",
    )(which, index, own, other)


def pick_kernel(which_ref, index_ref, own_ref, other_ref, out_ref):
    for m in range(out_ref.shape[0]):

        @pl.when(which_ref[m] == 0)
        def _():
            out_ref[m] = own_ref[index_ref[m]].astype(out_ref.dtype)

        @pl.when(which_ref[m] != 0)
        def _():
            out_ref[m] = other_ref[index_ref[m]].astype(out_ref.dtype)


def pick_blocks(own, other, which, index, out_dtype, after=()):
    _, rows, width = own.shape
    (out,), mark = launch(
        pick_kernel,
        [like(out_dtype, index.shape[0], rows, width)],
        in_specs=smem_specs(2) + vmem_specs(2),
        out_specs=vmem_specs(1),
        after=after,
        vmem=16,
        micros=3,
        name="pick_blocks",
    )(which, index, own, other)
    return out, mark


def leaving(k, s, value, stay_ref, odd_ref, even_ref):
    rows = value.shape[0]
    if k == 0:
        stay_ref[s] = value
        return
    target = even_ref if k == 2 else odd_ref
    first = ((k // 2 if k % 2 else 0) * stay_ref.shape[0] + s) * rows
    target[first : first + rows] = value


def leaving_shapes(blocks, piece, width):
    count = blocks * piece
    return [
        like(BF16, blocks, piece, width),
        like(BF16, 2 * count + NOTES, width),
        like(BF16, count, width),
    ]


def relay_kernel(even_ref, odd_ref, near_ref, out_ref):
    count = even_ref.shape[0]
    out_ref[:count] = even_ref[...]
    out_ref[count : 2 * count] = near_ref[count : 2 * count]
    out_ref[2 * count : 2 * count + NOTES] = odd_ref[2 * count :]
    out_ref[2 * count + NOTES :] = near_ref[2 * count :]


def relay(even, odd, near, after=()):
    count, width = even.shape
    (out,), mark = launch(
        relay_kernel,
        [like(BF16, 2 * count + 2 * NOTES, width)],
        in_specs=vmem_specs(3),
        out_specs=vmem_specs(1),
        after=after,
        vmem=16,
        name="relay",
    )(even, odd, near)
    return out, mark


def collect_kernel(stay_ref, odd_ref, near_ref, far_ref, out_ref, notes_ref):
    blocks, rows, width = stay_ref.shape
    count = blocks * rows
    out_ref[:blocks] = stay_ref[...]
    for k, part in enumerate((near_ref[:count], far_ref[:count], far_ref[count : 2 * count])):
        out_ref[(k + 1) * blocks : (k + 2) * blocks] = part.reshape(blocks, rows, width)
    notes_ref[:NOTES] = odd_ref[2 * count :]
    notes_ref[NOTES : 2 * NOTES] = near_ref[2 * count :]
    notes_ref[2 * NOTES :] = far_ref[2 * count :]


def collect(stay, odd, near, far, after=()):
    blocks, rows, width = stay.shape
    return launch(
        collect_kernel,
        [like(BF16, 4 * blocks, rows, width), like(BF16, 4 * NOTES, width)],
        in_specs=vmem_specs(4),
        out_specs=vmem_specs(2),
        after=after,
        vmem=16,
        micros=2,
        name="collect",
    )(stay, odd, near, far)


def modulate_kernel(
    blocks, which_ref, row_ref, own_ref, other_ref, weight_ref, bias_ref, out_ref, act_ref, held
):
    @pl.when(pl.program_id(0) == 0)
    def _():
        slots, width = own_ref.shape
        picked = []
        for s in range(blocks):
            hot = lax.broadcasted_iota(jnp.int32, (slots, width), 0) == row_ref[s]
            source = jnp.where(which_ref[s] == 0, own_ref[...].astype(F32), other_ref[...].astype(F32))
            picked.append(jnp.sum(jnp.where(hot, source, 0.0), 0, keepdims=True))
        picked.append(jnp.zeros((16 - blocks, width), F32))
        value = jnp.concatenate(picked, 0)
        held[...] = (value / (1.0 + jnp.exp(-value))).astype(BF16)
        act_ref[...] = held[...]

    out_ref[...] = (contract(held[...], weight_ref[...], 1, 0) + bias_ref[...])[:8]


def modulate(which, row, own, other, weight, bias, blocks, chunk):
    slots, width = own.shape
    columns = weight.shape[1]
    smem = pl.BlockSpec(memory_space=pltpu.SMEM)
    return pl.pallas_call(
        functools.partial(modulate_kernel, blocks),
        grid=(columns // chunk,),
        in_specs=[
            smem,
            smem,
            pl.BlockSpec((slots, width), lambda i: (0, 0)),
            pl.BlockSpec((slots, width), lambda i: (0, 0)),
            pl.BlockSpec((width, chunk), lambda i: (0, i)),
            pl.BlockSpec((1, chunk), lambda i: (0, i)),
        ],
        out_specs=[
            pl.BlockSpec((8, chunk), lambda i: (0, i)),
            pl.BlockSpec((16, width), lambda i: (0, 0)),
        ],
        out_shape=[
            jax.ShapeDtypeStruct((8, columns), F32),
            jax.ShapeDtypeStruct((16, width), BF16),
        ],
        scratch_shapes=[pltpu.VMEM((16, width), BF16)],
        compiler_params=pltpu.CompilerParams(vmem_limit_bytes=32 * 1024 * 1024),
        cost_estimate=pl.CostEstimate(
            flops=0, bytes_accessed=3 * width * columns, transcendentals=0
        ),
        name="modulate",
    )(which, row, own, other, weight, bias[None, :])


def norm_parts(value):
    center = value - jnp.mean(value, -1, keepdims=True)
    spread = jnp.mean(center * center, -1, keepdims=True)
    inverse = lax.rsqrt(spread + EPSILON)
    return center * inverse, inverse


def norm_back(grad, normed, inverse, scale):
    scaled = grad * (1.0 + scale)
    mean_one = jnp.mean(scaled, -1, keepdims=True)
    mean_two = jnp.mean(scaled * normed, -1, keepdims=True)
    return inverse * (scaled - mean_one - normed * mean_two)


def mod_row(mod_ref, index, part, width):
    return mod_ref[index : index + 1, part * width : (part + 1) * width]


def enter_kernel(blocks, *refs):
    parts = refs[:-8]
    mod_ref, weight_ref, bias_ref, x_ref, one_ref, turned_ref, kv_ref, held = refs[-8:]
    _, piece, width = parts[0].shape
    block = held.shape[0] // blocks

    @pl.when(pl.program_id(0) == 0)
    def _():
        for s in range(blocks):
            for k, part in enumerate(parts):
                first = s * block + k * piece
                x = part[s]
                x_ref[first : first + piece] = x
                normed, _ = norm_parts(x.astype(F32))
                one = normed * (1.0 + mod_row(mod_ref, s, 1, width)) + mod_row(mod_ref, s, 0, width)
                held[first : first + piece] = one.astype(BF16)
        one_ref[...] = held[...]
        turned_ref[...] = held[...].T

    kv_ref[...] = (contract(held[...], weight_ref[...], 1, 0) + bias_ref[...]).astype(BF16)


def enter(parts, mod, weight, bias, blocks):
    _, piece, width = parts[0].shape
    rows = piece * blocks * len(parts)
    const = lambda shape: pl.BlockSpec(shape, lambda i: (0,) * len(shape))
    return pl.pallas_call(
        functools.partial(enter_kernel, blocks),
        grid=(2,),
        in_specs=[const(p.shape) for p in parts]
        + [
            const((8, 2 * width)),
            pl.BlockSpec((width, width), lambda i: (0, 1 + i)),
            pl.BlockSpec((1, width), lambda i: (0, i)),
        ],
        out_specs=[
            const((rows, width)),
            const((rows, width)),
            const((width, rows)),
            pl.BlockSpec((rows, width), lambda i: (0, i)),
        ],
        out_shape=[
            jax.ShapeDtypeStruct((rows, width), BF16),
            jax.ShapeDtypeStruct((rows, width), BF16),
            jax.ShapeDtypeStruct((width, rows), BF16),
            jax.ShapeDtypeStruct((rows, 2 * width), BF16),
        ],
        scratch_shapes=[pltpu.VMEM((rows, width), BF16)],
        compiler_params=pltpu.CompilerParams(vmem_limit_bytes=48 * 1024 * 1024),
        cost_estimate=pl.CostEstimate(
            flops=8 * rows * width * width, bytes_accessed=12 * width * width, transcendentals=0
        ),
        name="enter",
    )(*parts, mod, weight, bias)


def linear_kernel(x_ref, weight_ref, bias_ref, out_ref):
    out_ref[...] = (contract(x_ref[...], weight_ref[...], 1, 0) + bias_ref[...]).astype(out_ref.dtype)


def linear(x, weight, bias, columns, chunk):
    rows, width = x.shape
    return pl.pallas_call(
        linear_kernel,
        grid=(columns // chunk,),
        in_specs=[
            pl.BlockSpec((rows, width), lambda i: (0, 0)),
            pl.BlockSpec((width, chunk), lambda i: (0, i)),
            pl.BlockSpec((1, chunk), lambda i: (0, i)),
        ],
        out_specs=pl.BlockSpec((rows, chunk), lambda i: (0, i)),
        out_shape=jax.ShapeDtypeStruct((rows, columns), BF16),
        compiler_params=pltpu.CompilerParams(vmem_limit_bytes=32 * 1024 * 1024),
        cost_estimate=pl.CostEstimate(
            flops=4 * rows * width * columns, bytes_accessed=8 * width * columns, transcendentals=0
        ),
        name="linear",
    )(x, weight, bias[None, :])


def middle_kernel(blocks, *refs):
    parts = refs[:-12]
    (
        att_ref, weight_ref, bias_ref, x_ref, mod_ref,
        branch_ref, middle_ref, two_ref, two_turned, att_turned, grad_ref, bias_grad,
    ) = refs[-12:]
    rows, width = x_ref.shape
    block = rows // blocks
    piece = parts[0].shape[1]
    att_turned[...] = att_ref[...].T
    total = jnp.zeros((1, width), F32)
    for s in range(blocks):
        part = slice(s * block, (s + 1) * block)
        branch = contract(att_ref[part], weight_ref[...], 1, 0) + bias_ref[...]
        branch_ref[part] = branch
        middle = x_ref[part].astype(F32) + mod_row(mod_ref, s, 2, width) * branch
        middle_ref[part] = middle
        normed, _ = norm_parts(middle)
        two_ref[part] = (
            normed * (1.0 + mod_row(mod_ref, s, 4, width)) + mod_row(mod_ref, s, 3, width)
        ).astype(BF16)
        for k, source in enumerate(parts):
            first = s * block + k * piece
            payload = source[s].astype(F32)
            grad = (payload[:, width : width + 1] * mod_row(mod_ref, s, 5, width) * payload[:, :width]).astype(BF16)
            grad_ref[first : first + piece] = grad
            total += jnp.sum(grad.astype(F32), 0, keepdims=True)
    two_turned[...] = two_ref[...].T
    bias_grad[...] = total


def middle_part(parts, attended, weight, bias, x, mod, blocks):
    rows, width = x.shape
    vmem = pl.BlockSpec(memory_space=pltpu.VMEM)
    return pl.pallas_call(
        functools.partial(middle_kernel, blocks),
        in_specs=[vmem] * (len(parts) + 5),
        out_specs=[vmem] * 7,
        out_shape=[
            jax.ShapeDtypeStruct((rows, width), F32),
            jax.ShapeDtypeStruct((rows, width), F32),
            jax.ShapeDtypeStruct((rows, width), BF16),
            jax.ShapeDtypeStruct((width, rows), BF16),
            jax.ShapeDtypeStruct((width, rows), BF16),
            jax.ShapeDtypeStruct((rows, width), BF16),
            jax.ShapeDtypeStruct((1, width), F32),
        ],
        compiler_params=pltpu.CompilerParams(vmem_limit_bytes=48 * 1024 * 1024),
        cost_estimate=pl.CostEstimate(
            flops=8 * rows * width * width, bytes_accessed=24 * rows * width, transcendentals=0
        ),
        name="middle_part",
    )(*parts, attended, weight, bias[None, :], x, mod)


def turn_kernel(blocks, heads, *refs):
    count = 4
    parts = refs[:count]
    (
        keep_ref, out_ref, gx_ref, middle_ref, branch_ref, att_ref, mod_ref, bias_ref, weight_ref,
        act_ref, outer_sum, *hidden_sums,
    ) = refs[count:-7]
    stay_ref, odd_ref, even_ref, grad_middle, grad_one, grad_att, delta_ref = refs[-7:]
    notes = []
    rows, width = middle_ref.shape
    block = rows // blocks
    piece = parts[0].shape[1]
    head_width = width // heads
    column_head = lax.broadcasted_iota(jnp.int32, (heads, width), 1) // head_width
    hot = (column_head == lax.broadcasted_iota(jnp.int32, (heads, width), 0)).astype(F32)
    bias_total = jnp.zeros((1, width), F32)
    for s in range(blocks):
        sums = [jnp.zeros((1, width), F32) for _ in range(4)]
        gate_one = mod_row(mod_ref, s, 2, width)
        scale_two = mod_row(mod_ref, s, 4, width)
        gate_two = mod_row(mod_ref, s, 5, width)
        for k, source in enumerate(parts):
            first = s * block + k * piece
            part = slice(first, first + piece)
            payload = source[s].astype(F32)
            upstream = payload[:, :width]
            route = payload[:, width : width + 1]
            middle = middle_ref[part]
            branch_two = route * (out_ref[part] + bias_ref[...])
            leaving(k, s, (middle + gate_two * branch_two).astype(BF16), stay_ref, odd_ref, even_ref)
            sums[3] += jnp.sum(branch_two * upstream, 0, keepdims=True)
            grad_two = gx_ref[part]
            normed, inverse = norm_parts(middle)
            sums[1] += jnp.sum(grad_two, 0, keepdims=True)
            sums[2] += jnp.sum(grad_two * normed, 0, keepdims=True)
            grad = upstream + norm_back(grad_two, normed, inverse, scale_two)
            grad_middle[part] = grad
            sums[0] += jnp.sum(grad * branch_ref[part], 0, keepdims=True)
            low = (gate_one * grad).astype(BF16)
            grad_one[part] = low
            bias_total += jnp.sum(low.astype(F32), 0, keepdims=True)
        notes += sums
        part = slice(s * block, (s + 1) * block)
        row = jnp.zeros((1, width), F32)
        for h in range(heads):
            row = jnp.where(
                hot[h : h + 1] > 0.5, keep_ref[s * heads + h].astype(F32), row
            )
        low = contract(grad_one[part], weight_ref[...], 1, 1).astype(BF16).astype(F32) * row
        grad_att[part] = low.astype(BF16)
        delta_ref[:, part] = lax.dot_general(
            hot,
            low * att_ref[part].astype(F32),
            (((1,), (1,)), ((), ())),
            precision=lax.Precision.HIGHEST,
            preferred_element_type=F32,
        )
    notes.append(bias_total)
    notes.append(outer_sum[...])
    for ref in hidden_sums:
        notes += [ref[:, lo : lo + width] for lo in range(0, ref.shape[1], width)]
    notes.append(act_ref[:blocks].astype(F32))
    odd_ref[2 * blocks * piece :] = jnp.concatenate(notes, 0).astype(BF16)


def turn_part(
    parts, keep, out, gx, middle, branch, attended, mod, bias, weight, act, sums, blocks, after=()
):
    rows, width = middle.shape
    heads = keep.shape[0] // blocks
    return launch(
        functools.partial(turn_kernel, blocks, heads),
        leaving_shapes(blocks, parts[0].shape[1], width)
        + [
            like(F32, rows, width),
            like(BF16, rows, width),
            like(BF16, rows, width),
            like(F32, heads, rows),
        ],
        in_specs=vmem_specs(len(parts)) + smem_specs(1) + vmem_specs(9 + len(sums)),
        out_specs=vmem_specs(7),
        after=after,
        vmem=48,
        micros=13,
        name="turn_part",
    )(*parts, keep, out, gx, middle, branch, attended, mod, bias[None, :], weight, act, *sums)


def query_back_kernel(
    core_ref, proj_keep, proj_send, one_keep, one_send, grad_one, grad_q, weight_ref, *refs
):
    keep_ref, send_ref, gx_ref, sum_ref = refs[-4:]
    width = grad_q.shape[1]
    half = keep_ref.shape[0]
    rows = grad_q.shape[0]
    turned = lambda ref: ref[...].reshape(half, rows)
    keep_ref[:, :width] = contract(turned(proj_keep), grad_one[...], 1, 0).astype(BF16)
    send_ref[:, :width] = contract(turned(proj_send), grad_one[...], 1, 0).astype(BF16)
    keep_ref[:, width:] = contract(turned(one_keep), grad_q[...], 1, 0).astype(BF16)
    send_ref[:, width:] = contract(turned(one_send), grad_q[...], 1, 0).astype(BF16)
    gx_ref[...] = contract(grad_q[...], weight_ref[...], 1, 1)
    sum_ref[...] = jnp.sum(grad_q[...].astype(F32), 0, keepdims=True)


def turned_specs(array):
    pairs, _, share, rows = array.shape
    keep = pl.BlockSpec((pairs, None, share, rows), lambda i, c: (0, c[0], 0, 0))
    send = pl.BlockSpec((pairs, None, share, rows), lambda i, c: (0, 1 - c[0], 0, 0))
    return [keep, send]


def query_back(core, att_turned, one_turned, grad_one, grad_q, weight, after=()):
    rows, width = grad_q.shape
    half = width // 2
    const = lambda shape: pl.BlockSpec(shape, lambda i, c: (0,) * len(shape))
    return launch(
        query_back_kernel,
        [
            like(BF16, half, 2 * width),
            like(BF16, half, 2 * width),
            like(F32, rows, width),
            like(F32, 1, width),
        ],
        prefetch=1,
        grid=(1,),
        in_specs=turned_specs(att_turned)
        + turned_specs(one_turned)
        + [const((rows, width)), const((rows, width)), const((width, width))],
        out_specs=[
            const((half, 2 * width)),
            const((half, 2 * width)),
            const((rows, width)),
            const((1, width)),
        ],
        after=after,
        micros=10,
        name="query_back",
    )(core, att_turned, att_turned, one_turned, one_turned, grad_one, grad_q, weight)


def leave_kernel(
    blocks, core_ref, one_keep, one_send, own_ref, got_ref, weight_ref, gx_in, x_ref, middle_ref,
    mod_ref, query_sum, keep_ref, send_ref, stay_ref, odd_ref, even_ref, total, grads,
):
    piece = stay_ref.shape[1]
    rows, width = x_ref.shape
    half = keep_ref.shape[0]
    block = rows // blocks
    step = pl.program_id(0)
    turned = lambda ref: ref[...].reshape(half, rows)
    grads[...] = (own_ref[...].astype(F32) + got_ref[...].astype(F32)).astype(BF16)
    keep_ref[...] = contract(turned(one_keep), grads[...], 1, 0).astype(BF16)
    send_ref[...] = contract(turned(one_send), grads[...], 1, 0).astype(BF16)

    @pl.when(step == 0)
    def _():
        total[...] = gx_in[...] + contract(grads[...], weight_ref[...], 1, 1)

    @pl.when(step == 1)
    def _():
        notes = []
        for s in range(blocks):
            part = slice(s * block, (s + 1) * block)
            grad = total[part] + contract(grads[part], weight_ref[...], 1, 1)
            normed, inverse = norm_parts(x_ref[part].astype(F32))
            notes.append(jnp.sum(grad, 0, keepdims=True))
            notes.append(jnp.sum(grad * normed, 0, keepdims=True))
            back = norm_back(grad, normed, inverse, mod_row(mod_ref, s, 1, width))
            low = (middle_ref[part] + back).astype(BF16)
            for k in range(block // piece):
                leaving(k, s, low[k * piece : (k + 1) * piece], stay_ref, odd_ref, even_ref)
        notes.append(query_sum[...])
        notes.append(jnp.sum(grads[...].astype(F32), 0, keepdims=True))
        notes.append(jnp.zeros((NOTES - 2 * blocks - 2, width), F32))
        odd_ref[2 * blocks * piece :] = jnp.concatenate(notes, 0).astype(BF16)


def leave(
    core, one_turned, own, got, weight, gx, x, grad_middle, mod, query_sum, blocks, piece, after=()
):
    rows, width = x.shape
    half = width // 2
    const = lambda shape: pl.BlockSpec(shape, lambda i, c: (0,) * len(shape))
    once = lambda shape: pl.BlockSpec(
        shape, lambda i, c: (0,) * len(shape), pipeline_mode=pl.Buffered(1)
    )
    shapes = leaving_shapes(blocks, piece, width)
    return launch(
        functools.partial(leave_kernel, blocks),
        [like(BF16, half, 2 * width), like(BF16, half, 2 * width)] + shapes,
        prefetch=1,
        grid=(2,),
        in_specs=turned_specs(one_turned)
        + [
            pl.BlockSpec((rows, width), lambda i, c: (0, i)),
            pl.BlockSpec((rows, width), lambda i, c: (0, i)),
            pl.BlockSpec((width, width), lambda i, c: (0, 1 + i)),
            once((rows, width)),
            once((rows, width)),
            once((rows, width)),
            once((8, 2 * width)),
            once((1, width)),
        ],
        out_specs=[
            pl.BlockSpec((half, width), lambda i, c: (0, i)),
            pl.BlockSpec((half, width), lambda i, c: (0, i)),
        ]
        + [const(s.shape) for s in shapes],
        scratch=[pltpu.VMEM((rows, width), F32), pltpu.VMEM((rows, width), BF16)],
        after=after,
        micros=15,
        name="leave",
    )(core, one_turned, one_turned, own, got, weight, gx, x, grad_middle, mod, query_sum)


def head_columns(ref, start, head_width):
    part = ref[:, start : start + head_width]
    return jnp.concatenate(
        [part, jnp.zeros((part.shape[0], LANES - head_width), part.dtype)], axis=1
    )


def attend_kernel(
    heads, head_width, blocks, long_ref, keep_ref, q_ref, own_ref, other_ref, out_ref, lse_ref,
    qh, kh, vh, oh,
):
    rows, width = q_ref.shape
    block = rows // blocks
    factor = head_width**-0.5 * LOG2E
    is_long = long_ref[0] == 1
    for h in range(heads):
        start = h * head_width
        qh[h] = head_columns(q_ref, start, head_width)
        kh[h, :rows] = head_columns(own_ref, start, head_width)
        vh[h, :rows] = head_columns(own_ref, width + start, head_width)

    @pl.when(is_long)
    def _():
        for h in range(heads):
            start = h * head_width
            kh[h, rows:] = head_columns(other_ref, start, head_width)
            vh[h, rows:] = head_columns(other_ref, width + start, head_width)

    def one(h, first, count, key_first, key_count):
        queries = qh[h, pl.ds(first, count), :]
        keys = kh[h, pl.ds(key_first, key_count), :]
        values = vh[h, pl.ds(key_first, key_count), :]
        scores = contract(keys, queries, 1, 1)
        top = jnp.max(scores, 0, keepdims=True)
        exponent = jnp.exp2((scores - top) * factor)
        total = jnp.sum(exponent, 0, keepdims=True)
        mixed = contract(values, exponent.astype(BF16), 0, 0) * (1.0 / total)
        oh[h, pl.ds(first, count), :] = mixed.T.astype(BF16)
        lse_ref[pl.ds(h, 1), pl.ds(first, count)] = top * factor + jnp.log2(total)

    def loop(index, first, count, key_first, key_count):
        def body(h, carry):
            keep = keep_ref[index * heads + h] == 1

            @pl.when(keep)
            def _():
                one(h, first, count, key_first, key_count)

            @pl.when(jnp.logical_not(keep))
            def _():
                oh[h, pl.ds(first, count), :] = jnp.zeros((count, LANES), BF16)

            return carry

        lax.fori_loop(0, heads, body, 0)

    @pl.when(is_long)
    def _():
        loop(0, 0, rows, 0, 2 * rows)

    @pl.when(jnp.logical_not(is_long))
    def _():
        for index in range(blocks):
            loop(index, index * block, block, index * block, block)

    for h in range(heads):
        out_ref[:, h * head_width : (h + 1) * head_width] = oh[h, :, :head_width]


def attend(queries, own, other, long_flag, keep, blocks):
    rows, width = queries.shape
    heads = keep.shape[0] // blocks
    head_width = width // heads
    vmem = pl.BlockSpec(memory_space=pltpu.VMEM)
    smem = pl.BlockSpec(memory_space=pltpu.SMEM)
    return pl.pallas_call(
        functools.partial(attend_kernel, heads, head_width, blocks),
        in_specs=[smem, smem, vmem, vmem, vmem],
        out_specs=[vmem, vmem],
        out_shape=[
            jax.ShapeDtypeStruct((rows, width), BF16),
            jax.ShapeDtypeStruct((heads, rows), F32),
        ],
        scratch_shapes=[
            pltpu.VMEM((heads, rows, LANES), BF16),
            pltpu.VMEM((heads, 2 * rows, LANES), BF16),
            pltpu.VMEM((heads, 2 * rows, LANES), BF16),
            pltpu.VMEM((heads, rows, LANES), BF16),
        ],
        compiler_params=pltpu.CompilerParams(vmem_limit_bytes=56 * 1024 * 1024),
        cost_estimate=pl.CostEstimate(
            flops=100 * rows * rows * width,
            bytes_accessed=12 * rows * width,
            transcendentals=2 * rows * rows * heads,
        ),
        name="attend",
    )(long_flag, keep, queries, own, other)


def attend_back_kernel(
    heads, head_width, blocks, long_ref, keep_ref, q_ref, own_ref, other_ref, go_ref, lse_ref,
    delta_ref, *refs,
):
    gq_ref, gown_ref, gother_ref, qh, kh, vh, gh, gqh, gkh, gvh = refs[-10:]
    rows, width = q_ref.shape
    block = rows // blocks
    scale = head_width**-0.5
    factor = scale * LOG2E
    is_long = long_ref[0] == 1
    for h in range(heads):
        start = h * head_width
        qh[h] = head_columns(q_ref, start, head_width)
        gh[h] = head_columns(go_ref, start, head_width)
        kh[h, :rows] = head_columns(own_ref, start, head_width)
        vh[h, :rows] = head_columns(own_ref, width + start, head_width)

    @pl.when(is_long)
    def _():
        for h in range(heads):
            start = h * head_width
            kh[h, rows:] = head_columns(other_ref, start, head_width)
            vh[h, rows:] = head_columns(other_ref, width + start, head_width)

    def one(h, first, count, key_first, key_count):
        queries = qh[h, pl.ds(first, count), :]
        grads = gh[h, pl.ds(first, count), :]
        keys = kh[h, pl.ds(key_first, key_count), :]
        values = vh[h, pl.ds(key_first, key_count), :]
        scores = contract(keys, queries, 1, 1)
        probs = jnp.exp2(scores * factor - lse_ref[pl.ds(h, 1), pl.ds(first, count)])
        gvh[h, pl.ds(key_first, key_count), :] = contract(
            probs.astype(BF16), grads, 1, 0
        ).astype(BF16)
        grad_probs = contract(values, grads, 1, 1)
        grad_scores = (probs * (grad_probs - delta_ref[pl.ds(h, 1), pl.ds(first, count)])).astype(BF16)
        gkh[h, pl.ds(key_first, key_count), :] = (
            contract(grad_scores, queries, 1, 0) * scale
        ).astype(BF16)
        gqh[h, pl.ds(first, count), :] = (
            (contract(keys, grad_scores, 0, 0) * scale).T
        ).astype(BF16)

    def loop(index, first, count, key_first, key_count):
        def body(h, carry):
            keep = keep_ref[index * heads + h] == 1

            @pl.when(keep)
            def _():
                one(h, first, count, key_first, key_count)

            @pl.when(jnp.logical_not(keep))
            def _():
                gqh[h, pl.ds(first, count), :] = jnp.zeros((count, LANES), BF16)
                gkh[h, pl.ds(key_first, key_count), :] = jnp.zeros((key_count, LANES), BF16)
                gvh[h, pl.ds(key_first, key_count), :] = jnp.zeros((key_count, LANES), BF16)

            return carry

        lax.fori_loop(0, heads, body, 0)

    @pl.when(is_long)
    def _():
        loop(0, 0, rows, 0, 2 * rows)
        for h in range(heads):
            start = h * head_width
            gother_ref[:, start : start + head_width] = gkh[h, rows:, :head_width]
            gother_ref[:, width + start : width + start + head_width] = gvh[h, rows:, :head_width]

    @pl.when(jnp.logical_not(is_long))
    def _():
        for index in range(blocks):
            loop(index, index * block, block, index * block, block)
        gother_ref[...] = jnp.zeros_like(gother_ref)

    for h in range(heads):
        start = h * head_width
        gq_ref[:, start : start + head_width] = gqh[h, :, :head_width]
        gown_ref[:, start : start + head_width] = gkh[h, :rows, :head_width]
        gown_ref[:, width + start : width + start + head_width] = gvh[h, :rows, :head_width]


def attend_back(queries, own, other, grad_out, lse, delta, long_flag, keep, blocks, after=()):
    rows, width = queries.shape
    heads = keep.shape[0] // blocks
    head_width = width // heads
    short = pltpu.VMEM((heads, rows, LANES), BF16)
    full = pltpu.VMEM((heads, 2 * rows, LANES), BF16)
    return launch(
        functools.partial(attend_back_kernel, heads, head_width, blocks),
        [like(BF16, rows, width), like(BF16, rows, 2 * width), like(BF16, rows, 2 * width)],
        in_specs=smem_specs(2) + vmem_specs(6),
        out_specs=vmem_specs(3),
        scratch=[short, full, full, short, short, full, full],
        after=after,
        vmem=60,
        micros=33,
        name="attend_back",
    )(long_flag, keep, queries, own, other, grad_out, lse, delta)


def feed_kernel(
    blocks, sub, group, first, resume, core_ref, keep_ref, x_ref, g_ref, xk_ref, xs_ref, bias_ref,
    wi_ref, wo_ref, *refs,
):
    act, gbefore = refs[-2:]
    out_ref, gx_ref, act_ref, wik_ref, wis_ref, gbias_ref = refs[-8:-2]
    rows, _ = x_ref.shape
    block = rows // blocks
    chunk = wi_ref.shape[1]
    half = wik_ref.shape[0]
    step = pl.program_id(0)
    groups = keep_ref.shape[0] // blocks
    turned = lambda ref: ref[...].reshape(half, rows)
    for lo in range(0, chunk, sub):
        cols = slice(lo, lo + sub)
        column_sum = jnp.zeros((1, sub), F32)
        for index in range(blocks):
            part = slice(index * block, (index + 1) * block)
            before = contract(x_ref[part], wi_ref[:, cols], 1, 0) + bias_ref[:, cols]
            grad_act = contract(g_ref[part], wo_ref[cols, :], 1, 1)
            base = index * groups + ((first + step) * chunk + lo) // group
            keep = jnp.concatenate(
                [
                    jnp.full((1, group), keep_ref[base + m].astype(F32))
                    for m in range(sub // group)
                ],
                axis=1,
            )
            square = before * before
            bend = jnp.tanh(GELU_A * before * (1.0 + GELU_B * square))
            gate = 0.5 * (1.0 + bend)
            slope = gate + (0.5 * GELU_A) * before * (1.0 - bend * bend) * (
                1.0 + (3.0 * GELU_B) * square
            )
            act[part, cols] = (before * gate * keep).astype(BF16)
            grad = (grad_act * keep * slope).astype(BF16)
            gbefore[part, cols] = grad
            column_sum += jnp.sum(grad.astype(F32), 0, keepdims=True)
        gbias_ref[:, cols] = column_sum
    out = contract(act[...], wo_ref[...], 1, 0)
    gx = contract(gbefore[...], wi_ref[...], 1, 1)

    @pl.when(step == 0)
    def _():
        if resume:
            out_ref[...] = refs[0][...] + out
            gx_ref[...] = refs[1][...] + gx
        else:
            out_ref[...] = out
            gx_ref[...] = gx

    @pl.when(step != 0)
    def _():
        out_ref[...] += out
        gx_ref[...] += gx

    act_ref[...] = act[...]
    wik_ref[...] = contract(turned(xk_ref), gbefore[...], 1, 0).astype(BF16)
    wis_ref[...] = contract(turned(xs_ref), gbefore[...], 1, 0).astype(BF16)


def feed(core, keep, x, grad, turned, bias, wi, wo, blocks, chunk, sub, first, count, before=()):
    rows, width = x.shape
    hidden = wi.shape[1]
    half = width // 2
    group = hidden * blocks // keep.shape[0]
    single = pl.Buffered(1)
    once = lambda shape: pl.BlockSpec(shape, lambda i, *c: (0, 0), pipeline_mode=single)
    tpairs, _, tshare, _ = turned.shape
    spec = lambda lead: pl.BlockSpec((tpairs, None, tshare, rows), lead, pipeline_mode=single)
    return launch(
        functools.partial(feed_kernel, blocks, sub, group, first, bool(before)),
        [
            like(F32, rows, width),
            like(F32, rows, width),
            like(BF16, rows, count * chunk),
            like(BF16, half, count * chunk),
            like(BF16, half, count * chunk),
            like(F32, 1, count * chunk),
        ],
        prefetch=2,
        grid=(count,),
        in_specs=[
            once((rows, width)),
            once((rows, width)),
            spec(lambda i, c, k: (0, c[0], 0, 0)),
            spec(lambda i, c, k: (0, 1 - c[0], 0, 0)),
            pl.BlockSpec((1, chunk), lambda i, *c: (0, first + i)),
            pl.BlockSpec((width, chunk), lambda i, *c: (0, first + i)),
            pl.BlockSpec((chunk, width), lambda i, *c: (first + i, 0)),
        ]
        + [once((rows, width))] * len(before),
        out_specs=[
            pl.BlockSpec((rows, width), lambda i, *c: (0, 0)),
            pl.BlockSpec((rows, width), lambda i, *c: (0, 0)),
            pl.BlockSpec((rows, chunk), lambda i, *c: (0, i)),
            pl.BlockSpec((half, chunk), lambda i, *c: (0, i)),
            pl.BlockSpec((half, chunk), lambda i, *c: (0, i)),
            pl.BlockSpec((1, chunk), lambda i, *c: (0, i)),
        ],
        scratch=[pltpu.VMEM((rows, chunk), BF16), pltpu.VMEM((rows, chunk), BF16)],
        vmem=FEED_VMEM,
        micros=25,
        name="feed",
    )(core, keep, x, grad, turned, turned, bias, wi, wo, *before)


def outer_kernel(share, starts, core_ref, *refs):
    acts = refs[: len(starts)]
    g_ref = refs[len(starts)]
    keep_ref, send_ref = refs[-2:]
    core = core_ref[0]
    step = pl.program_id(0)
    for act_ref, (lo, hi) in zip(acts, starts):

        @pl.when((step >= lo) & (step < hi))
        def _():
            grad = contract(act_ref[...], g_ref[...], 0, 0).astype(BF16)
            for pair in range(keep_ref.shape[0]):
                even = grad[2 * pair * share : (2 * pair + 1) * share]
                odd = grad[(2 * pair + 1) * share : (2 * pair + 2) * share]

                @pl.when(core == 0)
                def _():
                    keep_ref[pair] = even
                    send_ref[pair] = odd

                @pl.when(core != 0)
                def _():
                    keep_ref[pair] = odd
                    send_ref[pair] = even


def outer_part(core, acts, grad, share, chunk, after=()):
    rows, width = grad.shape
    pairs = chunk // (2 * share)
    specs, starts, at = [], [], 0
    for act in acts:
        count = act.shape[1] // chunk
        starts.append((at, at + count))
        specs.append(
            pl.BlockSpec(
                (rows, chunk), lambda i, lo=at, n=count: (0, jnp.clip(i - lo, 0, n - 1))
            )
        )
        at += count
    return launch(
        functools.partial(outer_kernel, share, starts),
        [like(BF16, at * pairs, share, width)] * 2,
        grid=(at,),
        in_specs=smem_specs(1) + specs + [pl.BlockSpec((rows, width), lambda i: (0, 0))],
        out_specs=[pl.BlockSpec((pairs, share, width), lambda i: (i, 0, 0))] * 2,
        after=after,
        micros=10,
        name="outer_part",
    )(core, *acts, grad)


def split_bit(array, dim, bit):
    keep = lax.dynamic_index_in_dim(array, bit, dim, keepdims=False)
    send = lax.dynamic_index_in_dim(array, 1 - bit, dim, keepdims=False)
    return keep, send


def split_kernel(units, place_ref, *refs):
    outs = refs[-4:]
    at = 0
    for member, count in enumerate(units):
        ins = refs[8 * member : 8 * member + 8]
        for m, out in enumerate(outs):
            left, right = ins[2 * m], ins[2 * m + 1]
            total = (left[0].astype(F32) + right[0].astype(F32)).astype(BF16)
            if count == 1 and len(total.shape) == 2:
                out[0, at] = total
            else:
                out[0, at : at + count] = total
        at += count


def split_call(place, arrays, blocks, spots, units, tail, count, low_bit, high_bit, after, name):
    low = lambda p: (p[2] >> low_bit) & 1
    high = lambda p: (p[2] >> high_bit) & 1
    leads = [
        lambda j, p: j * 2 + low(p),
        lambda j, p: j * 2 + 1 - low(p),
        lambda j, p: high(p) * count + j,
        lambda j, p: (1 - high(p)) * count + j,
    ]
    specs = []
    for block, spot in zip(blocks, spots):
        for m, lead in enumerate(leads):
            index = lambda j, p, lead=lead, spot=spot[m // 2]: (lead(j, p),) + spot
            specs += [pl.BlockSpec((1,) + block, index)] * 2
    shape = (sum(units),) + tail
    return launch(
        functools.partial(split_kernel, units),
        [like(BF16, count, *shape)] * 4,
        prefetch=1,
        grid=(count,),
        in_specs=specs,
        out_specs=[pl.BlockSpec((1,) + shape, lambda j, p: (j, 0, 0, 0))] * 4,
        after=after,
        micros=3,
        name=name,
    )(place, *arrays)


def cross_kernel(kinds, place_ref, *refs):
    keep_ref, send_ref = refs[-2:]
    share = keep_ref.shape[2]
    bit = place_ref[1] & 1

    def write(out_ref, low):
        tile = 0
        for n, members in enumerate(kinds):
            am, ag, bm, bg = refs[4 * n : 4 * n + 4]
            at = 0
            for by_rows in members:
                if by_rows:
                    for high, (m, g) in enumerate(((am, ag), (bm, bg))):
                        total = m[0, at + low].astype(F32) + g[0, at + low].astype(F32)
                        for q in range(4):
                            out_ref[high, tile + q] = total[q * share : (q + 1) * share].astype(BF16)
                    at += 2
                    tile += 4
                else:
                    for side, (m, g) in enumerate(((am, ag), (bm, bg))):
                        total = m[0, at].astype(F32) + g[0, at].astype(F32)
                        for high in range(2):
                            first = (2 * high + low) * share
                            out_ref[high, tile + side] = total[first : first + share].astype(BF16)
                    at += 1
                    tile += 2

    @pl.when(bit == 0)
    def _():
        write(keep_ref, 0)
        write(send_ref, 1)

    @pl.when(bit == 1)
    def _():
        write(keep_ref, 1)
        write(send_ref, 0)


def last_kernel(place_ref, mine_ref, got_ref, *refs):
    keep_ref, send_ref = refs[-2:]
    bit = place_ref[1] >> 1
    add = lambda i: (mine_ref[i].astype(F32) + got_ref[i].astype(F32)).astype(BF16)
    keep_ref[...] = add(bit)
    send_ref[...] = add(1 - bit)


def small_call(body, place, arrays, shape, after, name):
    return launch(
        body,
        [shape, shape],
        in_specs=smem_specs(1) + vmem_specs(len(arrays)),
        out_specs=vmem_specs(2),
        after=after,
        vmem=24,
        name=name,
    )(place, *arrays)


class Package:
    def __init__(self, place, *members):
        self.place = place
        self.keeps = [keep for keep, _ in members]
        self.flight = [swap(send, "bucket", 1) for _, send in members]
        self.kinds = [keep.ndim == 4 for keep in self.keeps]

    def first(self, *after):
        pairs = self.keeps[0].shape[0]
        self.bits = pairs.bit_length() - 1
        self.count = pairs // 2
        self.turn = 0
        arrays, blocks, spots, units = [], [], [], []
        for keep, got, by_rows in zip(self.keeps, self.flight, self.kinds):
            arrays += [keep, got] * 4
            if by_rows:
                blocks.append((2,) + keep.shape[2:])
                spots.append([(0, 0, 0), (1, 0, 0)])
                units.append(2)
                tail = keep.shape[2:]
            else:
                tail = (keep.shape[1], keep.shape[2] // 2)
                blocks.append(tail)
                spots.append([(0, 0), (0, 1)])
                units.append(1)
        self.unit_count, self.tail = sum(units), tail
        return self.depart(arrays, blocks, spots, units, after, "sum_first")

    def depart(self, arrays, blocks, spots, units, after, name):
        low_bit, high_bit = 1 + self.turn, self.bits - self.turn
        (a_keep, a_send, b_keep, b_send), self.done = split_call(
            self.place, arrays, blocks, spots, units, self.tail, self.count, low_bit, high_bit,
            after, name,
        )
        self.mine = [a_keep, b_keep]
        self.flight = [swap(a_send, "bucket", 1 << low_bit), swap(b_send, "bucket", 1 << high_bit)]
        self.turn += 1
        self.count //= 2
        return self.done

    def second(self, *after):
        while self.turn < self.bits:
            (am, bm), (ag, bg) = self.mine, self.flight
            spots = [[(0, 0, 0), (0, 0, 0)]]
            block = (self.unit_count,) + self.tail
            arrays = [am, ag, am, ag, bm, bg, bm, bg]
            self.depart(arrays, [block], spots, [self.unit_count], after, "sum_second")
        return self.done


class Cross:
    def __init__(self, packages, *after):
        self.place = packages[0].place
        self.kinds = [p.kinds for p in packages]
        unit, width = packages[0].tail
        self.tiles = sum(4 if by_rows else 2 for kinds in self.kinds for by_rows in kinds)
        self.tail = (unit // 4, width)
        arrays = []
        for p in packages:
            arrays += [p.mine[0], p.flight[0], p.mine[1], p.flight[1]]
        shape = jax.ShapeDtypeStruct((2, self.tiles) + self.tail, BF16)
        (self.mine, send), self.done = small_call(
            functools.partial(cross_kernel, self.kinds), self.place, arrays, shape, after, "cross"
        )
        self.flight = swap(send, "seq", 1)

    def last(self, *after):
        shape = jax.ShapeDtypeStruct((self.tiles,) + self.tail, BF16)
        (self.mine, send), self.done = small_call(
            last_kernel, self.place, [self.mine, self.flight], shape, after, "last"
        )
        self.flight = swap(send, "seq", 2)
        return self.done

    def results(self):
        total = self.mine.astype(F32) + self.flight.astype(F32)
        out, tile = [], 0
        for kinds in self.kinds:
            for by_rows in kinds:
                if by_rows:
                    out.append(total[tile : tile + 4].reshape(-1, self.tail[1]))
                    tile += 4
                else:
                    out.append(jnp.concatenate([total[tile], total[tile + 1]], 1))
                    tile += 2
        return out


def notes_kernel(blocks, early_ref, late_ref, early_cond, late_cond, out_ref, early_sum, late_sum):
    width = early_ref.shape[1]
    for part in range(6):
        if part < 2:
            ref, cond, count, which = late_ref, late_cond, 2, part
        else:
            ref, cond, count, which = early_ref, early_cond, 4, part - 2
        inside = lax.broadcasted_iota(jnp.int32, cond.shape, 0) % ref_pitch(ref, early_ref, late_ref)
        mine = (inside % count == which) & (inside < count * blocks)
        picked = jnp.where(mine, cond[...].astype(F32), 0.0).astype(BF16)
        out_ref[:, part * width : (part + 1) * width] = contract(picked, ref[...], 0, 0)
    for ref, total in ((early_ref, early_sum), (late_ref, late_sum)):
        pitch = ref_pitch(ref, early_ref, late_ref)
        shape = (NOTES, ref.shape[0])
        kind = lax.broadcasted_iota(jnp.int32, shape, 0)
        row = lax.broadcasted_iota(jnp.int32, shape, 1) % pitch
        total[...] = contract(jnp.where(kind == row, 1.0, 0.0).astype(BF16), ref[...], 1, 0)


def ref_pitch(ref, early_ref, late_ref):
    return NOTES if ref is early_ref else NOTES * late_ref.shape[0] // early_ref.shape[0]


def notes_part(early, late, early_cond, late_cond, blocks):
    width = early.shape[1]
    return launch(
        functools.partial(notes_kernel, blocks),
        [
            like(F32, early_cond.shape[1], 6 * width),
            like(F32, NOTES, width),
            like(F32, NOTES, width),
        ],
        in_specs=vmem_specs(4),
        out_specs=vmem_specs(3),
        vmem=32,
        micros=3,
        name="notes_part",
    )(early, late, early_cond, late_cond)[0]


def on_device(
    tokens,
    segment,
    keep_route,
    condition,
    group_bucket,
    head_mask,
    channel_mask,
    ada_weight,
    ada_bias,
    qkv_weight,
    query_bias,
    value_bias,
    proj_weight,
    proj_bias,
    inner_weight,
    inner_bias,
    outer_weight,
    outer_bias,
    cotangent,
):
    rows, width = tokens.shape
    slots = condition.shape[0]
    hidden = inner_weight.shape[1]
    group_count = lax.axis_size("bucket")
    seq_count = lax.axis_size("seq")
    bucket = lax.axis_index("bucket")
    seq = lax.axis_index("seq")
    core = bucket % 2
    piece = rows // slots
    block = piece * seq_count
    blocks = rows // block
    place = jnp.stack([core, seq, bucket]).astype(jnp.int32)
    row_share = width // group_count
    aligned = row_share % 16 == 0

    def turned(array):
        split = array.reshape(group_count // 2, 2, row_share, rows)
        if aligned:
            return split
        keep, send = split_bit(split, 1, core)
        return jnp.stack([keep, send]).reshape(1, 2, width // 2, rows)

    turned_core = place[:1] if aligned else jnp.zeros((1,), jnp.int32)

    seg_other = swap(segment, "bucket", 1)
    bucket_other = swap(group_bucket, "bucket", 1)
    tokens_own = tokens.reshape(slots, piece, width)
    tokens_other = swap(tokens_own, "bucket", 1)
    cond_other = swap(condition, "bucket", 1)
    route_columns = jnp.broadcast_to(keep_route.astype(BF16)[:, None], (rows, LANES))
    payload = jnp.concatenate([cotangent, route_columns], 1).reshape(slots, piece, width + LANES)
    payload_other = swap(payload, "bucket", 1)

    (
        send_which, send_index, back_which, back_index, cond_which, cond_row, flags, keep_heads,
        keep_channels,
    ) = make_plan(
        place, segment, seg_other, group_bucket, bucket_other, head_mask, channel_mask, slots,
        piece, seq_count, blocks,
    )

    def bring(pieces):
        return [pieces[0]] + [swap(pieces[k], "seq", k) for k in range(1, seq_count)]

    x_sent, x_mark = send_blocks(tokens_own, tokens_other, send_which, send_index, seq_count, blocks)
    x_parts = bring(x_sent)
    mod, cond_act = modulate(
        cond_which, cond_row, condition, cond_other, ada_weight, ada_bias, blocks, width
    )
    payload_sent, _ = send_blocks(
        payload, payload_other, send_which, send_index, seq_count, blocks, (x_parts[3],)
    )
    payload_parts = bring(payload_sent)
    pair_bias = jnp.concatenate([jnp.zeros_like(value_bias), value_bias])[None, :]
    x, normed_one, one_turned, own_kv = enter(x_parts, mod, qkv_weight, pair_bias, blocks)
    other_kv = swap(own_kv, "bucket", 1)
    queries = linear(normed_one, qkv_weight, query_bias, width, width // 3)
    attended, lse = attend(queries, own_kv, other_kv, flags, keep_heads, blocks)
    branch_one, middle, normed_two, two_turned, att_turned, grad_branch_two, grad_outer_bias = (
        middle_part(payload_parts, attended, proj_weight, proj_bias, x, mod, blocks)
    )

    share = hidden // group_count
    by_rows = (group_count // 2, row_share, -1)
    chunk = 2 * width // 3
    feed_args = (
        turned_core, keep_channels, normed_two, grad_branch_two, turned(two_turned),
        inner_bias[None, :], inner_weight, outer_weight, blocks, chunk, FEED_SUB,
    )
    (branch_two, grad_two, act_a, wi_keep, wi_send, hidden_a), _ = feed(*feed_args, 0, 3)
    inner = Package(place, (wi_keep.reshape(by_rows), wi_send.reshape(by_rows)))
    (branch_two, grad_two, act_b, wi_keep, wi_send, hidden_b), mark = feed(
        *feed_args, 3, 3, (branch_two, grad_two)
    )
    mark = inner.first(mark)
    (wo_keep, wo_send), mark = outer_part(
        place[:1], [act_a, act_b], grad_branch_two, share, width, (mark,)
    )
    by_units = (group_count // 2, 4, share // 4, width)
    rest = Package(
        place,
        (wi_keep.reshape(by_rows), wi_send.reshape(by_rows)),
        (wo_keep.reshape(by_units), wo_send.reshape(by_units)),
    )
    (out_stay, out_odd, out_even, grad_middle, grad_branch_one, grad_attended, delta), mark = (
        turn_part(
            payload_parts, keep_heads, branch_two, grad_two, middle, branch_one, attended, mod,
            outer_bias, proj_weight, cond_act, (grad_outer_bias, hidden_a, hidden_b), blocks,
            (mark,),
        )
    )
    mark = inner.second(mark)
    mark = rest.first(mark)
    out_near = swap(out_odd, "seq", 1)

    (grad_queries, grad_own, grad_other), mark = attend_back(
        queries, own_kv, other_kv, grad_attended, lse, delta, flags, keep_heads, blocks, (mark,)
    )
    grad_got = swap(grad_other, "bucket", 1)
    out_relay, mark = relay(out_even, out_odd, out_near, (mark,))
    out_far = swap(out_relay, "seq", 2)
    inner_cross = Cross([inner], mark)
    (pq_keep, pq_send, grad_one_part, query_sum), mark = query_back(
        turned_core, turned(att_turned), turned(one_turned), grad_branch_one, grad_queries,
        qkv_weight, (inner_cross.done,),
    )
    pq = Package(place, (pq_keep.reshape(by_rows), pq_send.reshape(by_rows)))
    mark = rest.second(mark)
    mark = inner_cross.last(mark)
    (kv_keep, kv_send, x_stay, x_odd, x_even), mark = leave(
        turned_core, turned(one_turned), grad_own, grad_got, qkv_weight, grad_one_part, x,
        grad_middle, mod, query_sum, blocks, piece, (mark,),
    )
    kv = Package(place, (kv_keep.reshape(by_rows), kv_send.reshape(by_rows)))
    x_near = swap(x_odd, "seq", 1)

    mark = pq.first(mark)
    (out_own, early), mark = collect(out_stay, out_odd, out_near, out_far, (mark,))
    out_other = swap(out_own, "bucket", 1)
    early_all = lax.all_gather(early, "bucket", axis=0, tiled=True)
    mark = kv.first(mark)
    x_relay, mark = relay(x_even, x_odd, x_near, (mark,))
    x_far = swap(x_relay, "seq", 2)
    rest_cross = Cross([rest], mark)
    mark = pq.second(rest_cross.done)
    block_out, mark = pick_blocks(out_own, out_other, back_which, back_index, BF16, (mark,))
    mark = kv.second(mark)
    mark = rest_cross.last(mark)
    (x_own, late), mark = collect(x_stay, x_odd, x_near, x_far, (mark,))
    x_other = swap(x_own, "bucket", 1)
    pq_cross = Cross([pq], mark)
    half = NOTES // 2
    late = late.reshape(seq_count, NOTES, width)[:, :half].reshape(seq_count * half, width)
    late_all = lax.all_gather(late, "bucket", axis=0, tiled=True)
    kv_cross = Cross([kv], pq_cross.done)
    grad_tokens, mark = pick_blocks(
        x_own, x_other, back_which, back_index, F32, (kv_cross.done,)
    )
    mark = pq_cross.last(mark)
    mark = kv_cross.last(mark)
    block_out = block_out.reshape(rows, width)
    grad_tokens = grad_tokens.reshape(rows, width)
    (inner_a,) = inner_cross.results()
    inner_b, grad_outer_weight = rest_cross.results()
    grad_inner_weight = jnp.concatenate([inner_a, inner_b], 1)
    (proj_query,) = pq_cross.results()
    grad_proj_weight = proj_query[:, :width]
    grad_qkv_weight = jnp.concatenate([proj_query[:, width:], *kv_cross.results()], 1)

    spot = bucket * seq_count + seq
    device_count = group_count * seq_count
    columns = width // device_count
    cond_mine = lax.dynamic_slice_in_dim(early_all, spot * columns, columns, 1)
    cond_mine = cond_mine.reshape(device_count, NOTES, columns)[:, NOTES - blocks :]

    def at_rows(parts, pitch):
        spread = jnp.broadcast_to(
            cond_mine[:, :, None, :], (device_count, blocks, parts, columns)
        ).reshape(device_count, blocks * parts, columns)
        rest = jnp.zeros((device_count, pitch - blocks * parts, columns), BF16)
        return jnp.concatenate([spread, rest], 1).reshape(device_count * pitch, columns)

    grad_ada_weight, early_sum, late_sum = notes_part(
        early_all, late_all, at_rows(4, NOTES), at_rows(2, half), blocks
    )

    def own_part(array):
        array = array.reshape(-1)
        size = array.shape[0] // device_count
        return lax.dynamic_slice_in_dim(array, spot * size, size, 0)

    ada_rows = jnp.concatenate(
        [
            sum(late_sum[2 * s : 2 * s + 2] for s in range(blocks)),
            sum(early_sum[4 * s : 4 * s + 4] for s in range(blocks)),
        ],
        0,
    )
    at = 4 * blocks
    return (
        block_out,
        grad_tokens,
        grad_ada_weight,
        own_part(ada_rows),
        grad_qkv_weight,
        own_part(late_sum[2 * blocks]),
        own_part(late_sum[2 * blocks + 1]),
        grad_proj_weight,
        own_part(early_sum[at]),
        grad_inner_weight,
        own_part(early_sum[at + 2 : at + 6]),
        grad_outer_weight,
        own_part(early_sum[at + 1]),
    )


def solution(mesh):
    split = P(("bucket", "seq"))
    split_rows = P(("bucket", "seq"), None)
    return jax.shard_map(
        on_device,
        mesh=mesh,
        in_specs=(split_rows, split, split, P("bucket", None), P("bucket"))
        + (P(),) * 13
        + (split_rows,),
        out_specs=(
            split_rows,
            split_rows,
            split_rows,
            split,
            split_rows,
            split,
            split,
            split_rows,
            split,
            split_rows,
            split,
            split_rows,
            split,
        ),
        check_vma=False,
    )
```

time: 714 us -> 500 us (0.70)
  Pallas kernels: 134 us -> 239 us
  other arithmetic: 97.9 us -> 4.39 us
  waiting for transfers between devices: 218 us -> 135 us
  local copies, waits for them, and re-layouts: 114 us -> 38.5 us
  matrix products: 51.8 us -> 0 us
  starting transfers between devices: 85.2 us -> 48.1 us
  between operations: 3.62 us -> 15.9 us
  blocking collectives: 0 us -> 10.3 us
    pallas_call x6 -> x37, Pallas kernels: 111 us -> 218 us  [the longest x32 192 us: run(): *results, mark = call(*operands, *after)]
    ppermute x69 -> x48, waiting for transfers between devices: 218 us -> 135 us  [swap(): return lax.ppermute(array, axis, [(i, i ^ bit) for i in range(size)])]
    dot_general x12 -> x0, matrix products: 51.8 us -> none  [the longest x7 27.4 us: contract(): lax.dot_general(left, right, (((left_dim,), (right_dim,)), ((), ())), pre...]
    convert_element_type x40 -> x1, other arithmetic: 47 us -> 0.01 us  [on_device(): keep_route.astype(BF16)[:, None]]
    ppermute x69 -> x48, starting transfers between devices: 85.2 us -> 48.1 us  [swap(): return lax.ppermute(array, axis, [(i, i ^ bit) for i in range(size)])]
    reduce_sum x26 -> x0, other arithmetic: 23.4 us -> none  [the longest x6 5.28 us: own_sum(): return jnp.sum(own.astype(F32), 0)]
    another operation x17 -> x0, local copies, waits for them, and re-layouts: 19.5 us -> none  [the longest x9 12.1 us: reduce_rows(): jnp.stack(halves).reshape((2,) * len(zbits) + (rows // seq_count, columns))]
    concatenate x7 -> x2, local copies, waits for them, and re-layouts: 18.9 us -> 0.03 us  [the longest x1 0.03 us: at_rows(): jnp.concatenate([spread, rest], 1).reshape(device_count * pitch, columns)]
  transfers between devices with their start and end apart: 69 -> 49, of which waited for: 26 -> 21; matrix products, arithmetic and copies ran while one was open for 35% -> 3% of each run, Pallas kernels for 19% -> 37%
where the time goes in v2:
time: 500 us; the launch traced here: 492 us
  Pallas kernels  239 us (48%)
  waiting for transfers between devices  135 us (27%)
  starting transfers between devices  48.1 us (10%)
  local copies, waits for them, and re-layouts  38.5 us (8%)
  between operations  15.9 us (3%)
  blocking collectives  10.3 us (2%)
    pallas_call x32, Pallas kernels, run(): *results, mark = call(*operands, *after)  192 us
    ppermute x48, waiting for transfers between devices, swap(): return lax.ppermute(array, axis, [(i, i ^ bit) for i in range(size)])  135 us
    ppermute x48, starting transfers between devices, swap(): return lax.ppermute(array, axis, [(i, i ^ bit) for i in range(size)])  48.1 us
    unnamed x176, local copies, waits for them, and re-layouts  28.5 us
    pallas_call x1, Pallas kernels, attend(): pl.pallas_call(functools.partial(attend_kernel, heads, head_width, blocks...  21.6 us
    all_gather x1, blocking collectives, on_device(): late_all = lax.all_gather(late, 'bucket', axis=0, tiled=True)  10.3 us
  transfers between devices with their start and end apart: 49, of which 21 were waited for; matrix products, arithmetic and copies ran while one was open for 3% of the time, Pallas kernels for 37%

profile of v2, /device:TPU:0, one launch (start us, length us, event | category | flops | bytes accessed | tf_op | source)
XLA Modules:
  0.0 491.8 jit_solution(10357607409382146113)
XLA Ops:
  11.0 3.0 make_plan.1
  18.0 5.0 %collective-permute-start.4 = (bf16[2,64,1152]{2,1,0:T(8,128)(2,1)S(1)}, bf16[2,64,1152]{2,1,0:T(8,128)(2,1)S(1)}, u32[]{:S(2)}, u32[]{:S(2)}) collective-permute-start(bf16[2,64,1152]{2,1,0:T(8,128)(2,1)S(1)} %get-tuple-element.168), channel_id=1, source_target_pairs={{0,3},{1,2},{2,1},{3,0},{4,7},{5,6},{6,5},{7,4},{8,11},{9,10},{10,... | collective-permute-start | bytes 884744 | tf_op jit(solution)/shard_map/ppermute | solution.py:30
  24.7 5.5 %copy-done = bf16[1152,6912]{1,0:T(8,128)(2,1)S(1)} copy-done((bf16[1152,6912]{1,0:T(8,128)(2,1)S(1)}, bf16[1152,6912]{1,0:T(8,128)(2,1)}, u32[]{:S(2)}) %copy-start) | copy-done | bytes 15925272
  30.3 4.5 modulate.1
  34.8 3.0 collective-permute-done.8.refs_1_
  37.8 10.7 %collective-permute-done.9.refs_2_ = bf16[2,64,1152]{2,1,0:T(8,128)(2,1)S(1)} collective-permute-done((bf16[2,64,1152]{2,1,0:T(8,128)(2,1)S(1)}, bf16[2,64,1152]{2,1,0:T(8,128)(2,1)S(1)}, u32[]{:S(2)}, u32[]{:S(2)}) %collective-permute-start.9) | collective-permute-done | bytes 294944 | tf_op jit(solution)/shard_map/ppermute | solution.py:30
  48.4 7.9 %enter.1 = (bf16[512,1152]{1,0:T(8,128)(2,1)S(1)}, bf16[512,1152]{1,0:T(8,128)(2,1)S(1)}, bf16[1152,512]{1,0:T(8,128)(2,1)S(1)}, bf16[512,2304]{1,0:T(8,128)(2,1)}) custom-call(bf16[2,64,1152]{2,1,0:T(8,128)(2,1)S(1)} %get-tuple-element.176.refs_0_, bf16[2,64,1152]{2,1,0:T(8,128)(2,1)S(1)} %collective-permute-done.8.refs_1_, ...), custom_call_target="tpu_custom_call" | custom-call | flops 5435817984 | bytes 15925248 | tf_op jit(solution)/shard_map/enter/pallas_call | solution.py:373
  58.0 4.8 collective-permute-done.2.refs_3_
  64.2 3.0 collective-permute-start.6
  68.6 2.8 linear.1.q_ref.refs_2_
  72.4 21.6 %attend.1 = (bf16[512,1152]{1,0:T(8,128)(2,1)}, f32[16,512]{1,0:T(8,128)}) custom-call(s32[2]{0:T(128)} %get-tuple-element.175.long_ref.refs_0_, s32[32]{0:T(128)} %get-tuple-element.173.keep_ref.refs_4_.refs_1_, bf16[512,1152]{1,0:T(8,128)(2,1)} %copy-done.1, bf16[512,2304]{1,0:T(8,128)(2,1)} %get-tuple-element.183.own_ref.refs_3_, ...), custom_call_target="tpu_custom_call" | custom-call | flops 30198988800 | bytes 7077888 | tf_op jit(solution)/shard_map/attend/pallas_call | solution.py:772
  94.0 7.5 %middle_part.1 = (f32[512,1152]{1,0:T(8,128)}, f32[512,1152]{1,0:T(8,128)}, bf16[512,1152]{1,0:T(8,128)(2,1)S(1)}, bf16[1152,512]{1,0:T(8,128)(2,1)S(1)}, bf16[1...) custom-call(bf16[2,64,1280]{2,1,0:T(8,128)(2,1)S(1)} %get-tuple-element.169.refs_0_, ...), custom_call_target="tpu_custom_call" | custom-call | flops 5435817984 | bytes 14155776 | tf_op jit(solution)/shard_map/middle_part/pallas_call | solution.py:461
  104.6 23.3 %feed.2 = (f32[512,1152]{1,0:T(8,128)}, f32[512,1152]{1,0:T(8,128)}, bf16[512,2304]{1,0:T(8,128)(2,1)}, bf16[576,2304]{1,0:T(8,128)(2,1)}, bf16[576,2304]{1,0:T(...) custom-call(s32[1]{0:T(128)} %bitcast.refs_0_, s32[72]{0:T(128)} %get-tuple-element.174.refs_1_, ...), custom_call_target="tpu_custom_call" | custom-call | flops 24999999488 | tf_op jit(solution)/shard_map/feed/pallas_call | solution.py:74
  128.0 24.8 %feed.3 = (f32[512,1152]{1,0:T(8,128)}, f32[512,1152]{1,0:T(8,128)}, bf16[512,2304]{1,0:T(8,128)(2,1)}, bf16[576,2304]{1,0:T(8,128)(2,1)}, bf16[576,2304]{1,0:T(...) custom-call(s32[1]{0:T(128)} %bitcast.refs_0_, s32[72]{0:T(128)} %get-tuple-element.174.refs_1_, ...), custom_call_target="tpu_custom_call" | custom-call | flops 24999999488 | tf_op jit(solution)/shard_map/feed/pallas_call | solution.py:74
  152.8 4.6 sum_first.4
  157.5 12.2 %outer_part.1 = (bf16[4,576,1152]{2,1,0:T(8,128)(2,1)}, bf16[4,576,1152]{2,1,0:T(8,128)(2,1)}, f32[8,128]{1,0:T(8,128)}) custom-call(s32[1]{0:T(128)} %bitcast.refs_0_, bf16[512,2304]{1,0:T(8,128)(2,1)} %get-tuple-element.199.refs_1_, bf16[512,2304]{1,0:T(8,128)(2,1)} %get-tuple-element.200.refs_2_, bf16[512,1152]{1,0:T(8,128)(2,1)} %get-tuple-element.187.refs_3_, ...), custom_call_target="tpu_custom_call" | custom-call | flops 10000000000 | tf_op jit(solution)/shard_map/outer_part/pallas_call | solution.py:74
  170.4 3.0 collective-permute-start.17
  174.1 12.6 %turn_part.1 = (bf16[2,64,1152]{2,1,0:T(8,128)(2,1)S(1)}, bf16[272,1152]{1,0:T(8,128)(2,1)S(1)}, bf16[128,1152]{1,0:T(8,128)(2,1)S(1)}, f32[512,1152]{1,0:T(8,12...) custom-call(bf16[2,64,1280]{2,1,0:T(8,128)(2,1)S(1)} %get-tuple-elem, ...), custom_call_target="tpu_custom_call" | custom-call | flops 12999999488 | tf_op jit(solution)/shard_map/turn_part/pallas_call | solution.py:74
  188.8 2.6 collective-permute-start.13
  192.4 3.5 sum_second.4
  195.9 1.5 copy-done.64
  197.4 10.4 %sum_first.5 = (bf16[2,3,144,1152]{3,2,1,0:T(8,128)(2,1)}, bf16[2,3,144,1152]{3,2,1,0:T(8,128)(2,1)}, bf16[2,3,144,1152]{3,2,1,0:T(8,128)(2,1)}, bf16[2,3,144,1152]{3,2,1,0:T(8,128)(2,1)}, f32[8,128]{1,0:T(8,128)}) custom-call(s32[3]{0:T(128)} %pad_add_fusion.place_ref.refs_0_, bf16[4,144,2304]{2,1,0:T(8,128)(2,1)} %bitcast.75, ...), custom_call_target="tpu_custom_call" | custom-call | flops 3000000000 | tf_op jit(solution)/shard_map/sum_first/pallas_call | solution.py:74
  208.4 1.5 collective-permute-start.25
  209.9 31.2 %attend_back.1 = (bf16[512,1152]{1,0:T(8,128)(2,1)}, bf16[512,2304]{1,0:T(8,128)(2,1)}, bf16[512,2304]{1,0:T(8,128)(2,1)}, f32[8,128]{1,0:T(8,128)}) custom-call(s32[2]{0:T(128)} %get-tuple-element.175.long_ref.refs_0_, s32[32]{0:T(128)} %get-tuple-element.173.keep_ref.refs_4_.refs_1_, bf16[512,1152]{1,0:T(8,128)(2,1)} %copy-done.1, ...), custom_call_target="tpu_custom_call" | custom-call | flops 32999999488 | tf_op jit(solution)/shard_map/attend_back/pallas_call | solution.py:74
  241.8 1.6 collective-permute-start.20
  244.1 16.3 %collective-permute-done.19.refs_2_ = bf16[1,1,144,1152]{3,2,1,0:T(8,128)(2,1)S(1)} collective-permute-done((bf16[1,1,144,1152]{3,2,1,0:T(8,128)(2,1)S(1)}, bf16[1,1,144,1152]{3,2,1,0:T(8,128)(2,1)S(1)}, u32[]{:S(2)}, u32[]{:S(2)}) %collective-permute-start.19) | collective-permute-done | bytes 331808 | tf_op jit(solution)/shard_map/ppermute | solution.py:30
  261.8 9.8 %query_back.1 = (bf16[576,2304]{1,0:T(8,128)(2,1)}, bf16[576,2304]{1,0:T(8,128)(2,1)}, f32[512,1152]{1,0:T(8,128)}, f32[1,1152]{1,0:T(1,128)}, f32[8,128]{1,0:T(8,128)}) custom-call(s32[1]{0:T(128)} %bitcast.refs_0_, bf16[4,2,144,512]{3,2,1,0:T(8,128)(2,1)} %bitcast.65, bf16[4,2,144,512]{3,2,1,0:T(8,128)(2,1)} %bitcast.66, ...), custom_call_target="tpu_custom_call" | custom-call | flops 10000000000 | tf_op jit(solution)/shard_map/query_back/pallas_call | solution.py:74
  272.9 6.3 %sum_second.5 = (bf16[1,3,144,1152]{3,2,1,0:T(8,128)(2,1)}, bf16[1,3,144,1152]{3,2,1,0:T(8,128)(2,1)}, bf16[1,3,144,1152]{3,2,1,0:T(8,128)(2,1)}, bf16[1,3,144,1152]{3,2,1,0:T(8,128)(2,1)}, f32[8,128]{1,0:T(8,128)}) custom-call(s32[3]{0:T(128)} %pad_add_fusion.place_ref.refs_0_, bf16[2,3,144,1152]{3,2,1,0:T(8,128)(2,1)} %get-tuple-element.244.refs_1_.refs_3_, ...), custom_call_target="tpu_custom_call" | custom-call | flops 3000000000 | tf_op jit(solution)/shard_map/sum_second/pallas_call | solution.py:74
  279.2 3.4 collective-permute-done.23.refs_2_
  284.6 15.2 %leave.1 = (bf16[576,2304]{1,0:T(8,128)(2,1)}, bf16[576,2304]{1,0:T(8,128)(2,1)}, bf16[2,64,1152]{2,1,0:T(8,128)(2,1)}, bf16[272,1152]{1,0:T(8,128)(2,1)}, bf16[128,1152]{1,0:T(8,128)(2,1)}, /*index=5*/f32[8,128]{1,0:T(8,128)}) custom-call(s32[1]{0:T(128)} %bitcast.refs_0_, bf16[4,2,144,512]{3,2,1,0:T(8,128)(2,1)} %bitcast.63, ...), custom_call_target="tpu_custom_call" | custom-call | flops 15000000512 | tf_op jit(solution)/shard_map/leave/pallas_call | solution.py:74
  299.9 2.2 collective-permute-start.18
  302.1 1.6 copy-done.65
  303.7 4.6 sum_first.6
  308.3 24.0 %collective-permute-done.18.refs_3_ = bf16[288,1152]{1,0:T(8,128)(2,1)S(1)} collective-permute-done((bf16[288,1152]{1,0:T(8,128)(2,1)S(1)}, bf16[288,1152]{1,0:T(8,128)(2,1)S(1)}, u32[]{:S(2)}, u32[]{:S(2)}) %collective-permute-start.18) | collective-permute-done | bytes 663584 | tf_op jit(solution)/shard_map/ppermute | solution.py:30
  334.4 2.9 collective-permute-start.31
  338.8 1.7 collective-permute-start.30
  340.5 4.9 collective-permute-done.46
  345.5 9.6 %collective-permute-done.31.refs_2_ = bf16[272,1152]{1,0:T(8,128)(2,1)} collective-permute-done((bf16[272,1152]{1,0:T(8,128)(2,1)S(1)}, bf16[272,1152]{1,0:T(8,128)(2,1)}, u32[]{:S(2)}, u32[]{:S(2)}) %collective-permute-start.31) | collective-permute-done | bytes 626720 | tf_op jit(solution)/shard_map/ppermute | solution.py:30
  355.1 1.8 collective-permute-start.27
  357.6 1.7 collective-permute-start.28
  359.3 4.7 sum_first.7
  369.9 1.7 copy.32
  372.8 1.7 collective-permute-start.35
  374.6 8.5 %collective-permute-done.27.refs_2_.refs_4_ = bf16[2,1,144,1152]{3,2,1,0:T(8,128)(2,1)} collective-permute-done((bf16[2,1,144,1152]{3,2,1,0:T(8,128)(2,1)}, bf16[2,1,144,1152]{3,2,1,0:T(8,128)(2,1)}, u32[]{:S(2)}, u32[]{:S(2)}) %collective-permute-start.27) | collective-permute-done | bytes 663584 | tf_op jit(solution)/shard_map/ppermute | solution.py:30
  383.8 3.6 sum_second.6
  389.6 2.0 pick_blocks.2
  391.6 3.7 collective-permute-done.35.refs_2_.refs_4_
  395.3 1.7 collective-permute-start.41
  397.0 3.1 collective-permute-done.36.refs_6_.refs_8_
  400.9 3.6 sum_second.7
  404.9 1.7 collective-permute-start.39
  407.9 1.5 last.5
  409.4 2.2 collective-permute-done.33.refs_3_
  413.0 10.3 %all_gather.7.refs_1_ = bf16[256,1152]{1,0:T(8,128)(2,1)S(1)} all-gather(bf16[32,1152]{1,0:T(8,128)(2,1)S(1)} %slice_bitcast_fusion.8), channel_id=1, replica_groups=mesh['bucket'=8,'seq'=4] {'bucket'}, dimensions={0}, use_global_device_ids=true | all-gather | bytes 663552 | tf_op jit(solution)/shard_map/all_gather | solution.py:1444
  423.3 2.2 notes_part.1
  428.8 1.5 cross.7
  431.1 2.0 collective-permute-start.44
  435.6 17.4 %collective-permute-done.47 = bf16[6,36,1152]{2,1,0:T(8,128)(2,1)} collective-permute-done((bf16[6,36,1152]{2,1,0:T(8,128)(2,1)}, bf16[6,36,1152]{2,1,0:T(8,128)(2,1)}, u32[]{:S(2)}, u32[]{:S(2)}) %collective-permute-start.47) | collective-permute-done | bytes 497696 | tf_op jit(solution)/shard_map/ppermute | solution.py:30
  454.2 2.3 pick_blocks.3
  456.5 5.4 %collective-permute-done.42.refs_2_ = bf16[2,2,36,1152]{3,2,1,0:T(8,128)(2,1)} collective-permute-done((bf16[2,2,36,1152]{3,2,1,0:T(8,128)(2,1)S(1)}, bf16[2,2,36,1152]{3,2,1,0:T(8,128)(2,1)}, u32[]{:S(2)}, u32[]{:S(2)}) %collective-permute-start.42) | collective-permute-done | bytes 331808 | tf_op jit(solution)/shard_map/ppermute | solution.py:30
  463.0 1.7 last.7
  466.9 2.6 collective-permute-start.43
  469.5 9.9 %collective-permute-done.45 = bf16[2,36,1152]{2,1,0:T(8,128)(2,1)S(1)} collective-permute-done((bf16[2,36,1152]{2,1,0:T(8,128)(2,1)S(1)}, bf16[2,36,1152]{2,1,0:T(8,128)(2,1)S(1)}, u32[]{:S(2)}, u32[]{:S(2)}) %collective-permute-start.45) | collective-permute-done | bytes 165920 | tf_op jit(solution)/shard_map/ppermute | solution.py:30
  479.5 3.8 collective-permute-done.43
  (294 shorter events, 59.3 us)
Async XLA Ops:
  7.2 16.4 %copy-start.8 = (bf16[8,1152]{1,0:T(8,128)(2,1)S(1)}, bf16[8,1152]{1,0:T(8,128)(2,1)}, u32[]{:S(2)}) copy-start(bf16[8,1152]{1,0:T(8,128)(2,1)} %own_ref.1) | copy-start | bytes 55300
  7.2 16.4 %copy-start.70 = (f32[6912]{0:T(1024)S(1)}, f32[6912]{0:T(1024)}, u32[]{:S(2)}) copy-start(f32[6912]{0:T(1024)} %param.27) | copy-start | bytes 82948
  7.2 16.4 %copy-start.75 = (f32[1152]{0:T(1024)S(1)}, f32[1152]{0:T(1024)}, u32[]{:S(2)}) copy-start(f32[1152]{0:T(1024)} %param.30) | copy-start | bytes 13828
  7.2 364.4 %all-gather.2.cloned.1.call-start = ((), (), s32[]{:S(2)}) async-start(), calls=%async_computation | async-start | bytes 1327104 | tf_op jit(solution)/shard_map/all_gather | solution.py:1430
  7.3 6.8 %collective-permute-start.3 = (bf16[8,64,1152]{2,1,0:T(8,128)(2,1)}, bf16[8,64,1152]{2,1,0:T(8,128)(2,1)S(1)}, u32[]{:S(2)}, u32[]{:S(2)}) collective-permute-start(bf16[8,64,1152]{2,1,0:T(8,128)(2,1)} %bitcast.59), channel_id=1, source_target_pairs={{0,4},{4,0},{8,12},{12,8},{16,20},{20,16},{24,28},{28,24},{1,5},{5... | collective-permute-start | bytes 3538952 | tf_op jit(solution)/shard_map/ppermute | solution.py:30
  7.8 2.7 collective-permute-start
  7.9 2.5 collective-permute-start.1
  18.0 16.8 %collective-permute-start.4 = (bf16[2,64,1152]{2,1,0:T(8,128)(2,1)S(1)}, bf16[2,64,1152]{2,1,0:T(8,128)(2,1)S(1)}, u32[]{:S(2)}, u32[]{:S(2)}) collective-permute-start(bf16[2,64,1152]{2,1,0:T(8,128)(2,1)S(1)} %get-tuple-element.168), channel_id=1, source_target_pairs={{0,3},{1,2},{2,1},{3,0},{4,7},{5,6},{6,5},{7,4},{8,11},{9,10},{10,... | collective-permute-start | bytes 884744 | tf_op jit(solution)/shard_map/ppermute | solution.py:30
  23.0 14.8 %collective-permute-start.8 = (bf16[2,64,1152]{2,1,0:T(8,128)(2,1)S(1)}, bf16[2,64,1152]{2,1,0:T(8,128)(2,1)S(1)}, u32[]{:S(2)}, u32[]{:S(2)}) collective-permute-start(bf16[2,64,1152]{2,1,0:T(8,128)(2,1)S(1)} %get-tuple-element.177), channel_id=1, source_target_pairs={{0,1},{1,0},{2,3},{3,2},{4,5},{5,4},{6,7},{7,6},{8,9},{9,8},{10,11... | collective-permute-start | bytes 884744 | tf_op jit(solution)/shard_map/ppermute | solution.py:30
  23.0 25.4 %collective-permute-start.9 = (bf16[2,64,1152]{2,1,0:T(8,128)(2,1)S(1)}, bf16[2,64,1152]{2,1,0:T(8,128)(2,1)S(1)}, u32[]{:S(2)}, u32[]{:S(2)}) collective-permute-start(bf16[2,64,1152]{2,1,0:T(8,128)(2,1)S(1)} %get-tuple-element.178), channel_id=1, source_target_pairs={{0,2},{1,3},{2,0},{3,1},{4,6},{5,7},{6,4},{7,5},{8,10},{9,11},{10,... | collective-permute-start | bytes 884744 | tf_op jit(solution)/shard_map/ppermute | solution.py:30
  23.6 1.2 collective-permute-start.10
  30.3 38.3 %slice-start = ((s8[7962624]{0:T(1024)(128)(4,1)}), s8[4194304]{0:T(1024)(128)(4,1)S(1)}, s32[]{:S(2)}) async-start(s8[7962624]{0:T(1024)(128)(4,1)} %bitcast.53), calls=%async_computation.1 | async-start | bytes 8388608
  34.8 138.6 %copy-start.23 = (f32[8,6912]{1,0:T(8,128)}, f32[8,6912]{1,0:T(8,128)S(1)}, u32[]{:S(2)}) copy-start(f32[8,6912]{1,0:T(8,128)S(1)} %get-tuple-element.181.refs_4_.refs_8_.refs_10_.refs_9_) | copy-start | bytes 663556
  48.4 20.1 %slice-start.1 = ((s8[7962624]{0:T(1024)(128)(4,1)}), s8[3768320]{0:T(1024)(128)(4,1)S(1)}, s32[]{:S(2)}) async-start(s8[7962624]{0:T(1024)(128)(4,1)} %bitcast.53), calls=%async_computation.2 | async-start | bytes 7536640
  56.3 16.1 %collective-permute-start.11 = (bf16[512,2304]{1,0:T(8,128)(2,1)}, bf16[512,2304]{1,0:T(8,128)(2,1)}, u32[]{:S(2)}, u32[]{:S(2)}) collective-permute-start(bf16[512,2304]{1,0:T(8,128)(2,1)} %get-tuple-element.183.own_ref.refs_3_), channel_id=1, source_target_pairs={{0,4},{4,0},{8,12},{12,8},{16,20},{20,16},{24,28},{28,24},{1,5},{5... | collective-permute-start | bytes 7077896 | tf_op jit(solution)/shard_map/ppermute | solution.py:30
  56.7 6.1 %collective-permute-start.2 = (bf16[8,64,1280]{2,1,0:T(8,128)(2,1)S(1)}, bf16[8,64,1280]{2,1,0:T(8,128)(2,1)S(1)}, u32[]{:S(2)}, u32[]{:S(2)}) collective-permute-start(bf16[8,64,1280]{2,1,0:T(8,128)(2,1)S(1)} %bitcast.55), channel_id=1, source_target_pairs={{0,4},{4,0},{8,12},{12,8},{16,20},{20,16},{24,28},{28,24},{1,5},{5... | collective-permute-start | bytes 3932168 | tf_op jit(solution)/shard_map/ppermute | solution.py:30
  64.2 29.9 %collective-permute-start.5 = (bf16[2,64,1280]{2,1,0:T(8,128)(2,1)S(1)}, bf16[2,64,1280]{2,1,0:T(8,128)(2,1)S(1)}, u32[]{:S(2)}, u32[]{:S(2)}) collective-permute-start(bf16[2,64,1280]{2,1,0:T(8,128)(2,1)S(1)} %get-tuple-element.170), channel_id=1, source_target_pairs={{0,1},{1,0},{2,3},{3,2},{4,5},{5,4},{6,7},{7,6},{8,9},{9,8},{10,11... | collective-permute-start | bytes 983048 | tf_op jit(solution)/shard_map/ppermute | solution.py:30
  64.2 29.9 %collective-permute-start.6 = (bf16[2,64,1280]{2,1,0:T(8,128)(2,1)S(1)}, bf16[2,64,1280]{2,1,0:T(8,128)(2,1)S(1)}, u32[]{:S(2)}, u32[]{:S(2)}) collective-permute-start(bf16[2,64,1280]{2,1,0:T(8,128)(2,1)S(1)} %get-tuple-element.171), channel_id=1, source_target_pairs={{0,2},{1,3},{2,0},{3,1},{4,6},{5,7},{6,4},{7,5},{8,10},{9,11},{10,... | collective-permute-start | bytes 983048 | tf_op jit(solution)/shard_map/ppermute | solution.py:30
  67.2 26.8 %collective-permute-start.7 = (bf16[2,64,1280]{2,1,0:T(8,128)(2,1)S(1)}, bf16[2,64,1280]{2,1,0:T(8,128)(2,1)S(1)}, u32[]{:S(2)}, u32[]{:S(2)}) collective-permute-start(bf16[2,64,1280]{2,1,0:T(8,128)(2,1)S(1)} %get-tuple-element.172), channel_id=1, source_target_pairs={{0,3},{1,2},{2,1},{3,0},{4,7},{5,6},{6,5},{7,4},{8,11},{9,10},{10,... | collective-permute-start | bytes 983048 | tf_op jit(solution)/shard_map/ppermute | solution.py:30
  127.9 24.9 %collective-permute-start.12 = (bf16[4,144,2304]{2,1,0:T(8,128)(2,1)}, bf16[4,144,2304]{2,1,0:T(8,128)(2,1)}, u32[]{:S(2)}, u32[]{:S(2)}) collective-permute-start(bf16[4,144,2304]{2,1,0:T(8,128)(2,1)} %bitcast.98), channel_id=1, source_target_pairs={{0,4},{4,0},{8,12},{12,8},{16,20},{20,16},{24,28},{28,24},{1,5},{5... | collective-permute-start | bytes 7962632 | tf_op jit(solution)/shard_map/ppermute | solution.py:30
  157.5 15.9 %copy-start.30 = (s32[32]{0:T(128)S(1)}, s32[32]{0:T(128)}, u32[]{:S(2)}) copy-start(s32[32]{0:T(128)} %get-tuple-element.173.keep_ref.refs_4_.refs_1_) | copy-start | bytes 388
  157.5 15.9 %copy-start.61 = (f32[1,2304]{1,0:T(1,128)S(1)}, f32[1,2304]{1,0:T(1,128)}, u32[]{:S(2)}) copy-start(f32[1,2304]{1,0:T(1,128)} %get-tuple-element.197.refs_15_) | copy-start | bytes 27652
  169.8 26.1 %collective-permute-start.15 = (bf16[4,4,144,1152]{3,2,1,0:T(8,128)(2,1)}, bf16[4,4,144,1152]{3,2,1,0:T(8,128)(2,1)}, u32[]{:S(2)}, u32[]{:S(2)}) collective-permute-start(bf16[4,4,144,1152]{3,2,1,0:T(8,128)(2,1)} %bitcast.94), channel_id=1, source_target_pairs={{0,4},{4,0},{8,12},{12,8},{16,20},{20,16},{24,28},{28,24},{1,5},{5... | collective-permute-start | bytes 15925256 | tf_op jit(solution)/shard_map/ppermute | solution.py:30
  170.2 25.6 %collective-permute-start.14 = (bf16[4,144,2304]{2,1,0:T(8,128)(2,1)}, bf16[4,144,2304]{2,1,0:T(8,128)(2,1)S(1)}, u32[]{:S(2)}, u32[]{:S(2)}) collective-permute-start(bf16[4,144,2304]{2,1,0:T(8,128)(2,1)} %bitcast.96), channel_id=1, source_target_pairs={{0,4},{4,0},{8,12},{12,8},{16,20},{20,16},{24,28},{28,24},{1,5},{5... | collective-permute-start | bytes 7962632 | tf_op jit(solution)/shard_map/ppermute | solution.py:30
  170.3 21.0 %collective-permute-start.16 = (bf16[2,1,144,1152]{3,2,1,0:T(8,128)(2,1)S(1)}, bf16[2,1,144,1152]{3,2,1,0:T(8,128)(2,1)S(1)}, u32[]{:S(2)}, u32[]{:S(2)}) collective-permute-start(bf16[2,1,144,1152]{3,2,1,0:T(8,128)(2,1)S(1)} %copy-done.80), channel_id=1, source_target_pairs={{0,8},{4,12},{8,0},{12,4},{16,24},{20,28},{24,16},{28,20},{1,9},{5... | collective-permute-start | bytes 1990664 | tf_op jit(solution)/shard_map/ppermute | solution.py:30
  170.4 20.9 %collective-permute-start.17 = (bf16[2,1,144,1152]{3,2,1,0:T(8,128)(2,1)S(1)}, bf16[2,1,144,1152]{3,2,1,0:T(8,128)(2,1)S(1)}, u32[]{:S(2)}, u32[]{:S(2)}) collective-permute-start(bf16[2,1,144,1152]{3,2,1,0:T(8,128)(2,1)S(1)} %copy-done.79), channel_id=1, source_target_pairs={{0,16},{4,20},{8,24},{12,28},{16,0},{20,4},{24,8},{28,12},{1,17},{... | collective-permute-start | bytes 1990664 | tf_op jit(solution)/shard_map/ppermute | solution.py:30
  188.8 53.0 %collective-permute-start.13 = (bf16[272,1152]{1,0:T(8,128)(2,1)S(1)}, bf16[272,1152]{1,0:T(8,128)(2,1)S(1)}, u32[]{:S(2)}, u32[]{:S(2)}) collective-permute-start(bf16[272,1152]{1,0:T(8,128)(2,1)S(1)} %get-tuple-element.207.refs_1_), channel_id=1, source_target_pairs={{0,1},{1,0},{2,3},{3,2},{4,5},{5,4},{6,7},{7,6},{8,9},{9,8},{10,11... | collective-permute-start | bytes 1880072 | tf_op jit(solution)/shard_map/ppermute | solution.py:30
  207.8 65.1 %collective-permute-start.24 = (bf16[2,3,144,1152]{3,2,1,0:T(8,128)(2,1)}, bf16[2,3,144,1152]{3,2,1,0:T(8,128)(2,1)}, u32[]{:S(2)}, u32[]{:S(2)}) collective-permute-start(bf16[2,3,144,1152]{3,2,1,0:T(8,128)(2,1)} %get-tuple-element.245), channel_id=1, source_target_pairs={{0,8},{4,12},{8,0},{12,4},{16,24},{20,28},{24,16},{28,20},{1,9},{5... | collective-permute-start | bytes 5971976 | tf_op jit(solution)/shard_map/ppermute | solution.py:30
  208.4 64.5 %collective-permute-start.25 = (bf16[2,3,144,1152]{3,2,1,0:T(8,128)(2,1)}, bf16[2,3,144,1152]{3,2,1,0:T(8,128)(2,1)}, u32[]{:S(2)}, u32[]{:S(2)}) collective-permute-start(bf16[2,3,144,1152]{3,2,1,0:T(8,128)(2,1)} %get-tuple-element.247), channel_id=1, source_target_pairs={{0,16},{4,20},{8,24},{12,28},{16,0},{20,4},{24,8},{28,12},{1,17},{... | collective-permute-start | bytes 5971976 | tf_op jit(solution)/shard_map/ppermute | solution.py:30
  209.9 31.3 %copy-start.85 = (bf16[1,1,144,1152]{3,2,1,0:T(8,128)(2,1)S(1)}, bf16[1,1,144,1152]{3,2,1,0:T(8,128)(2,1)}, u32[]{:S(2)}) copy-start(bf16[1,1,144,1152]{3,2,1,0:T(8,128)(2,1)} %get-tuple-element.230) | copy-start | bytes 995332
  209.9 31.9 %copy-start.84 = (bf16[1,1,144,1152]{3,2,1,0:T(8,128)(2,1)S(1)}, bf16[1,1,144,1152]{3,2,1,0:T(8,128)(2,1)}, u32[]{:S(2)}) copy-start(bf16[1,1,144,1152]{3,2,1,0:T(8,128)(2,1)} %get-tuple-element.232) | copy-start | bytes 995332
  241.1 19.3 %copy-start.4 = (s32[3]{0:T(128)S(1)}, s32[3]{0:T(128)}, u32[]{:S(2)}) copy-start(s32[3]{0:T(128)} %pad_add_fusion.place_ref.refs_0_) | copy-start | bytes 40
  241.1 19.3 %copy-start.46 = (bf16[1,1,144,1152]{3,2,1,0:T(8,128)(2,1)S(1)}, bf16[1,1,144,1152]{3,2,1,0:T(8,128)(2,1)}, u32[]{:S(2)}) copy-start(bf16[1,1,144,1152]{3,2,1,0:T(8,128)(2,1)} %get-tuple-element.229.refs_1_) | copy-start | bytes 995332
  241.1 19.3 %copy-start.47 = (bf16[1,1,144,1152]{3,2,1,0:T(8,128)(2,1)S(1)}, bf16[1,1,144,1152]{3,2,1,0:T(8,128)(2,1)}, u32[]{:S(2)}) copy-start(bf16[1,1,144,1152]{3,2,1,0:T(8,128)(2,1)} %get-tuple-element.231.refs_3_) | copy-start | bytes 995332
  241.1 42.9 %collective-permute-start.22 = (bf16[512,2304]{1,0:T(8,128)(2,1)}, bf16[512,2304]{1,0:T(8,128)(2,1)}, u32[]{:S(2)}, u32[]{:S(2)}) collective-permute-start(bf16[512,2304]{1,0:T(8,128)(2,1)} %get-tuple-element.238), channel_id=1, source_target_pairs={{0,4},{4,0},{8,12},{12,8},{16,20},{20,16},{24,28},{28,24},{1,5},{5... | collective-permute-start | bytes 7077896 | tf_op jit(solution)/shard_map/ppermute | solution.py:30
  241.2 19.2 %collective-permute-start.19 = (bf16[1,1,144,1152]{3,2,1,0:T(8,128)(2,1)S(1)}, bf16[1,1,144,1152]{3,2,1,0:T(8,128)(2,1)S(1)}, u32[]{:S(2)}, u32[]{:S(2)}) collective-permute-start(bf16[1,1,144,1152]{3,2,1,0:T(8,128)(2,1)S(1)} %copy-done.85), channel_id=1, source_target_pairs={{0,16},{4,20},{8,24},{12,28},{16,0},{20,4},{24,8},{28,12},{1,17},{... | collective-permute-start | bytes 995336 | tf_op jit(solution)/shard_map/ppermute | solution.py:30
  241.8 19.4 %copy-start.19 = (bf16[272,1152]{1,0:T(8,128)(2,1)}, bf16[272,1152]{1,0:T(8,128)(2,1)S(1)}, u32[]{:S(2)}) copy-start(bf16[272,1152]{1,0:T(8,128)(2,1)S(1)} %collective-permute-done.13.refs_2_) | copy-start | bytes 1880068
  241.8 18.6 %collective-permute-start.20 = (bf16[1,1,144,1152]{3,2,1,0:T(8,128)(2,1)S(1)}, bf16[1,1,144,1152]{3,2,1,0:T(8,128)(2,1)S(1)}, u32[]{:S(2)}, u32[]{:S(2)}) collective-permute-start(bf16[1,1,144,1152]{3,2,1,0:T(8,128)(2,1)S(1)} %copy-done.84), channel_id=1, source_target_pairs={{0,8},{4,12},{8,0},{12,4},{16,24},{20,28},{24,16},{28,20},{1,9},{5... | collective-permute-start | bytes 995336 | tf_op jit(solution)/shard_map/ppermute | solution.py:30
  271.6 30.5 %collective-permute-start.21 = (bf16[4,144,2304]{2,1,0:T(8,128)(2,1)}, bf16[4,144,2304]{2,1,0:T(8,128)(2,1)S(1)}, u32[]{:S(2)}, u32[]{:S(2)}) collective-permute-start(bf16[4,144,2304]{2,1,0:T(8,128)(2,1)} %bitcast.97), channel_id=1, source_target_pairs={{0,4},{4,0},{8,12},{12,8},{16,20},{20,16},{24,28},{28,24},{1,5},{5... | collective-permute-start | bytes 7962632 | tf_op jit(solution)/shard_map/ppermute | solution.py:30
  271.6 11.0 %collective-permute-start.23 = (bf16[2,2,36,1152]{3,2,1,0:T(8,128)(2,1)S(1)}, bf16[2,2,36,1152]{3,2,1,0:T(8,128)(2,1)S(1)}, u32[]{:S(2)}, u32[]{:S(2)}) collective-permute-start(bf16[2,2,36,1152]{3,2,1,0:T(8,128)(2,1)S(1)} %get-tuple-element.243), channel_id=1, source_target_pairs={{0,1},{1,0},{2,3},{3,2},{4,5},{5,4},{6,7},{7,6},{8,9},{9,8},{10,11... | collective-permute-start | bytes 995336 | tf_op jit(solution)/shard_map/ppermute | solution.py:30
  299.8 57.9 %collective-permute-start.32 = (bf16[4,144,2304]{2,1,0:T(8,128)(2,1)}, bf16[4,144,2304]{2,1,0:T(8,128)(2,1)}, u32[]{:S(2)}, u32[]{:S(2)}) collective-permute-start(bf16[4,144,2304]{2,1,0:T(8,128)(2,1)} %bitcast.95), channel_id=1, source_target_pairs={{0,4},{4,0},{8,12},{12,8},{16,20},{20,16},{24,28},{28,24},{1,5},{5... | collective-permute-start | bytes 7962632 | tf_op jit(solution)/shard_map/ppermute | solution.py:30
  299.9 32.4 %collective-permute-start.18 = (bf16[288,1152]{1,0:T(8,128)(2,1)S(1)}, bf16[288,1152]{1,0:T(8,128)(2,1)S(1)}, u32[]{:S(2)}, u32[]{:S(2)}) collective-permute-start(bf16[288,1152]{1,0:T(8,128)(2,1)S(1)} %get-tuple-element.224), channel_id=1, source_target_pairs={{0,2},{1,3},{2,0},{3,1},{4,6},{5,7},{6,4},{7,5},{8,10},{9,11},{10,... | collective-permute-start | bytes 1990664 | tf_op jit(solution)/shard_map/ppermute | solution.py:30
  303.7 28.6 %copy-start.20 = (bf16[272,1152]{1,0:T(8,128)(2,1)S(1)}, bf16[272,1152]{1,0:T(8,128)(2,1)}, u32[]{:S(2)}) copy-start(bf16[272,1152]{1,0:T(8,128)(2,1)} %copy-done.19) | copy-start | bytes 1880068
  334.4 11.0 %collective-permute-start.46 = (bf16[2,36,1152]{2,1,0:T(8,128)(2,1)S(1)}, bf16[2,36,1152]{2,1,0:T(8,128)(2,1)S(1)}, u32[]{:S(2)}, u32[]{:S(2)}) collective-permute-start(bf16[2,36,1152]{2,1,0:T(8,128)(2,1)S(1)} %get-tuple-element.312), channel_id=1, source_target_pairs={{0,2},{1,3},{2,0},{3,1},{4,6},{5,7},{6,4},{7,5},{8,10},{9,11},{10,... | collective-permute-start | bytes 497672 | tf_op jit(solution)/shard_map/ppermute | solution.py:30
  334.4 20.6 %collective-permute-start.31 = (bf16[272,1152]{1,0:T(8,128)(2,1)S(1)}, bf16[272,1152]{1,0:T(8,128)(2,1)}, u32[]{:S(2)}, u32[]{:S(2)}) collective-permute-start(bf16[272,1152]{1,0:T(8,128)(2,1)S(1)} %copy-done.16), channel_id=1, source_target_pairs={{0,1},{1,0},{2,3},{3,2},{4,5},{5,4},{6,7},{7,6},{8,9},{9,8},{10,11... | collective-permute-start | bytes 1880072 | tf_op jit(solution)/shard_map/ppermute | solution.py:30
  337.4 29.9 %collective-permute-start.29 = (bf16[1,3,144,1152]{3,2,1,0:T(8,128)(2,1)}, bf16[1,3,144,1152]{3,2,1,0:T(8,128)(2,1)S(1)}, u32[]{:S(2)}, u32[]{:S(2)}) collective-permute-start(bf16[1,3,144,1152]{3,2,1,0:T(8,128)(2,1)} %get-tuple-element.259), channel_id=1, source_target_pairs={{0,16},{4,20},{8,24},{12,28},{16,0},{20,4},{24,8},{28,12},{1,17},{... | collective-permute-start | bytes 2985992 | tf_op jit(solution)/shard_map/ppermute | solution.py:30
  338.8 29.9 %collective-permute-start.30 = (bf16[1,3,144,1152]{3,2,1,0:T(8,128)(2,1)}, bf16[1,3,144,1152]{3,2,1,0:T(8,128)(2,1)S(1)}, u32[]{:S(2)}, u32[]{:S(2)}) collective-permute-start(bf16[1,3,144,1152]{3,2,1,0:T(8,128)(2,1)} %get-tuple-element.261), channel_id=1, source_target_pairs={{0,8},{4,12},{8,0},{12,4},{16,24},{20,28},{24,16},{28,20},{1,9},{5... | collective-permute-start | bytes 2985992 | tf_op jit(solution)/shard_map/ppermute | solution.py:30
  345.4 42.1 %collective-permute-start.26 = (bf16[8,64,1152]{2,1,0:T(8,128)(2,1)S(1)}, bf16[8,64,1152]{2,1,0:T(8,128)(2,1)S(1)}, u32[]{:S(2)}, u32[]{:S(2)}) collective-permute-start(bf16[8,64,1152]{2,1,0:T(8,128)(2,1)S(1)} %get-tuple-element.253.refs_2_), channel_id=1, source_target_pairs={{0,4},{4,0},{8,12},{12,8},{16,20},{20,16},{24,28},{28,24},{1,5},{5... | collective-permute-start | bytes 3538952 | tf_op jit(solution)/shard_map/ppermute | solution.py:30
  355.1 27.9 %collective-permute-start.27 = (bf16[2,1,144,1152]{3,2,1,0:T(8,128)(2,1)}, bf16[2,1,144,1152]{3,2,1,0:T(8,128)(2,1)}, u32[]{:S(2)}, u32[]{:S(2)}) collective-permute-start(bf16[2,1,144,1152]{3,2,1,0:T(8,128)(2,1)} %get-tuple-element.255), channel_id=1, source_target_pairs={{0,8},{4,12},{8,0},{12,4},{16,24},{20,28},{24,16},{28,20},{1,9},{5... | collective-permute-start | bytes 1990664 | tf_op jit(solution)/shard_map/ppermute | solution.py:30
  357.6 26.0 %collective-permute-start.28 = (bf16[2,1,144,1152]{3,2,1,0:T(8,128)(2,1)}, bf16[2,1,144,1152]{3,2,1,0:T(8,128)(2,1)}, u32[]{:S(2)}, u32[]{:S(2)}) collective-permute-start(bf16[2,1,144,1152]{3,2,1,0:T(8,128)(2,1)} %get-tuple-element.257), channel_id=1, source_target_pairs={{0,16},{4,20},{8,24},{12,28},{16,0},{20,4},{24,8},{28,12},{1,17},{... | collective-permute-start | bytes 1990664 | tf_op jit(solution)/shard_map/ppermute | solution.py:30
  371.6 33.2 %collective-permute-start.34 = (bf16[2,6,36,1152]{3,0,2,1:T(2,128)(2,1)}, bf16[2,6,36,1152]{3,0,2,1:T(2,128)(2,1)}, u32[]{:S(2)}, u32[]{:S(2)}) collective-permute-start(bf16[2,6,36,1152]{3,0,2,1:T(2,128)(2,1)} %copy.32), channel_id=1, source_target_pairs={{0,1},{1,0},{2,3},{3,2},{4,5},{5,4},{6,7},{7,6},{8,9},{9,8},{10,11... | collective-permute-start | bytes 2985992 | tf_op jit(solution)/shard_map/ppermute | solution.py:30
  372.8 22.5 %collective-permute-start.35 = (bf16[2,1,144,1152]{3,2,1,0:T(8,128)(2,1)}, bf16[2,1,144,1152]{3,2,1,0:T(8,128)(2,1)S(1)}, u32[]{:S(2)}, u32[]{:S(2)}) collective-permute-start(bf16[2,1,144,1152]{3,2,1,0:T(8,128)(2,1)} %get-tuple-element.277), channel_id=1, source_target_pairs={{0,8},{4,12},{8,0},{12,4},{16,24},{20,28},{24,16},{28,20},{1,9},{5... | collective-permute-start | bytes 1990664 | tf_op jit(solution)/shard_map/ppermute | solution.py:30
  383.0 17.1 %collective-permute-start.36 = (bf16[2,1,144,1152]{3,2,1,0:T(8,128)(2,1)}, bf16[2,1,144,1152]{3,2,1,0:T(8,128)(2,1)S(1)}, u32[]{:S(2)}, u32[]{:S(2)}) collective-permute-start(bf16[2,1,144,1152]{3,2,1,0:T(8,128)(2,1)} %get-tuple-element.279), channel_id=1, source_target_pairs={{0,16},{4,20},{8,24},{12,28},{16,0},{20,4},{24,8},{28,12},{1,17},{... | collective-permute-start | bytes 1990664 | tf_op jit(solution)/shard_map/ppermute | solution.py:30
  383.7 27.9 %collective-permute-start.33 = (bf16[288,1152]{1,0:T(8,128)(2,1)S(1)}, bf16[288,1152]{1,0:T(8,128)(2,1)S(1)}, u32[]{:S(2)}, u32[]{:S(2)}) collective-permute-start(bf16[288,1152]{1,0:T(8,128)(2,1)S(1)} %get-tuple-element.273), channel_id=1, source_target_pairs={{0,2},{1,3},{2,0},{3,1},{4,6},{5,7},{6,4},{7,5},{8,10},{9,11},{10,... | collective-permute-start | bytes 1990664 | tf_op jit(solution)/shard_map/ppermute | solution.py:30
  387.5 38.7 %collective-permute-start.40 = (bf16[1,1,144,1152]{3,2,1,0:T(8,128)(2,1)}, bf16[1,1,144,1152]{3,2,1,0:T(8,128)(2,1)S(1)}, u32[]{:S(2)}, u32[]{:S(2)}) collective-permute-start(bf16[1,1,144,1152]{3,2,1,0:T(8,128)(2,1)} %get-tuple-element.289), channel_id=1, source_target_pairs={{0,16},{4,20},{8,24},{12,28},{16,0},{20,4},{24,8},{28,12},{1,17},{... | collective-permute-start | bytes 995336 | tf_op jit(solution)/shard_map/ppermute | solution.py:30
  395.3 30.9 %collective-permute-start.41 = (bf16[1,1,144,1152]{3,2,1,0:T(8,128)(2,1)}, bf16[1,1,144,1152]{3,2,1,0:T(8,128)(2,1)S(1)}, u32[]{:S(2)}, u32[]{:S(2)}) collective-permute-start(bf16[1,1,144,1152]{3,2,1,0:T(8,128)(2,1)} %get-tuple-element.291), channel_id=1, source_target_pairs={{0,8},{4,12},{8,0},{12,4},{16,24},{20,28},{24,16},{28,20},{1,9},{5... | collective-permute-start | bytes 995336 | tf_op jit(solution)/shard_map/ppermute | solution.py:30
  404.5 24.3 %collective-permute-start.38 = (bf16[1,1,144,1152]{3,2,1,0:T(8,128)(2,1)}, bf16[1,1,144,1152]{3,2,1,0:T(8,128)(2,1)S(1)}, u32[]{:S(2)}, u32[]{:S(2)}) collective-permute-start(bf16[1,1,144,1152]{3,2,1,0:T(8,128)(2,1)} %get-tuple-element.285), channel_id=1, source_target_pairs={{0,16},{4,20},{8,24},{12,28},{16,0},{20,4},{24,8},{28,12},{1,17},{... | collective-permute-start | bytes 995336 | tf_op jit(solution)/shard_map/ppermute | solution.py:30
  404.9 23.9 %collective-permute-start.39 = (bf16[1,1,144,1152]{3,2,1,0:T(8,128)(2,1)}, bf16[1,1,144,1152]{3,2,1,0:T(8,128)(2,1)S(1)}, u32[]{:S(2)}, u32[]{:S(2)}) collective-permute-start(bf16[1,1,144,1152]{3,2,1,0:T(8,128)(2,1)} %get-tuple-element.287), channel_id=1, source_target_pairs={{0,8},{4,12},{8,0},{12,4},{16,24},{20,28},{24,16},{28,20},{1,9},{5... | collective-permute-start | bytes 995336 | tf_op jit(solution)/shard_map/ppermute | solution.py:30
  412.9 41.3 %collective-permute-start.37 = (bf16[8,64,1152]{2,1,0:T(8,128)(2,1)S(1)}, bf16[8,64,1152]{2,1,0:T(8,128)(2,1)S(1)}, u32[]{:S(2)}, u32[]{:S(2)}) collective-permute-start(bf16[8,64,1152]{2,1,0:T(8,128)(2,1)S(1)} %get-tuple-element.283.refs_2_), channel_id=1, source_target_pairs={{0,4},{4,0},{8,12},{12,8},{16,20},{20,16},{24,28},{28,24},{1,5},{5... | collective-permute-start | bytes 3538952 | tf_op jit(solution)/shard_map/ppermute | solution.py:30
  426.2 26.9 %collective-permute-start.47 = (bf16[6,36,1152]{2,1,0:T(8,128)(2,1)}, bf16[6,36,1152]{2,1,0:T(8,128)(2,1)}, u32[]{:S(2)}, u32[]{:S(2)}) collective-permute-start(bf16[6,36,1152]{2,1,0:T(8,128)(2,1)} %get-tuple-element.314), channel_id=1, source_target_pairs={{0,2},{1,3},{2,0},{3,1},{4,6},{5,7},{6,4},{7,5},{8,10},{9,11},{10,... | collective-permute-start | bytes 1493000 | tf_op jit(solution)/shard_map/ppermute | solution.py:30
  431.1 32.0 %collective-permute-start.44 = (bf16[2,2,36,1152]{3,2,1,0:T(8,128)(2,1)}, bf16[2,2,36,1152]{3,2,1,0:T(8,128)(2,1)}, u32[]{:S(2)}, u32[]{:S(2)}) collective-permute-start(bf16[2,2,36,1152]{3,2,1,0:T(8,128)(2,1)} %get-tuple-element.307), channel_id=1, source_target_pairs={{0,1},{1,0},{2,3},{3,2},{4,5},{5,4},{6,7},{7,6},{8,9},{9,8},{10,11... | collective-permute-start | bytes 995336 | tf_op jit(solution)/shard_map/ppermute | solution.py:30
  433.1 28.8 %collective-permute-start.42 = (bf16[2,2,36,1152]{3,2,1,0:T(8,128)(2,1)S(1)}, bf16[2,2,36,1152]{3,2,1,0:T(8,128)(2,1)}, u32[]{:S(2)}, u32[]{:S(2)}) collective-permute-start(bf16[2,2,36,1152]{3,2,1,0:T(8,128)(2,1)S(1)} %get-tuple-element.302), channel_id=1, source_target_pairs={{0,1},{1,0},{2,3},{3,2},{4,5},{5,4},{6,7},{7,6},{8,9},{9,8},{10,11... | collective-permute-start | bytes 995336 | tf_op jit(solution)/shard_map/ppermute | solution.py:30
  464.7 14.7 %collective-permute-start.45 = (bf16[2,36,1152]{2,1,0:T(8,128)(2,1)S(1)}, bf16[2,36,1152]{2,1,0:T(8,128)(2,1)S(1)}, u32[]{:S(2)}, u32[]{:S(2)}) collective-permute-start(bf16[2,36,1152]{2,1,0:T(8,128)(2,1)S(1)} %get-tuple-element.310), channel_id=1, source_target_pairs={{0,2},{1,3},{2,0},{3,1},{4,6},{5,7},{6,4},{7,5},{8,10},{9,11},{10,... | collective-permute-start | bytes 497672 | tf_op jit(solution)/shard_map/ppermute | solution.py:30
  466.9 16.3 %collective-permute-start.43 = (bf16[2,36,1152]{2,1,0:T(8,128)(2,1)S(1)}, bf16[2,36,1152]{2,1,0:T(8,128)(2,1)S(1)}, u32[]{:S(2)}, u32[]{:S(2)}) collective-permute-start(bf16[2,36,1152]{2,1,0:T(8,128)(2,1)S(1)} %get-tuple-element.305), channel_id=1, source_target_pairs={{0,2},{1,3},{2,0},{3,1},{4,6},{5,7},{6,4},{7,5},{8,10},{9,11},{10,... | collective-permute-start | bytes 497672 | tf_op jit(solution)/shard_map/ppermute | solution.py:30
  (73 other events, 287.1 us)
Sparse Core Ops, SparseCore 0:
  334.5 29.1 all-gather.1
